TPU v7x, 32 devices: a whole 2x2x4 slice. The times are simulated.
32 devices in a mesh: fsdp: 32 (over z, y, x, core).
Axes of the slice: x: 2, y: 2, z: 4, core: 2. Of those that a mesh axis runs over, the one named last changes fastest.
Arguments:
- tokens: bfloat16 [8192, 2048], P('fsdp'), may hold values from -6 to 6
- per_layer: bfloat16 [8192, 256], P('fsdp'), may hold values from -6 to 6
- cotangent: bfloat16 [8192, 2048], P('fsdp'), may hold values from -6 to 6
- seq_lengths: int32 [5], replicated, may hold values from 1024 to 2048, as said below
- seq_order: int32 [5], replicated, may hold values from 0 to 4, each once
- qkv_weight: bfloat16 [2048, 3072], P('fsdp'), may hold values from -0.125 to 0.125
- out_weight: bfloat16 [2048, 2048], P('fsdp'), may hold values from -2 to 2
- ffn_weights: bfloat16 [8192, 3, 2048], P('fsdp'), may hold values from -0.125 to 0.125
- side_weights: bfloat16 [2048, 640], P('fsdp'), may hold values from -0.125 to 0.125
- norm_gains: bfloat16 [4608], P('fsdp'), may hold values from 0.25 to 1.75
Outputs:
- output: bfloat16 [8192, 2048], P('fsdp')
- input_grad: bfloat16 [8192, 2048], P('fsdp')
- per_layer_grad: bfloat16 [8192, 256], P('fsdp')
- qkv_grad: float32 [2048, 3072], P('fsdp')
- out_grad: float32 [2048, 2048], P('fsdp')
- ffn_grad: float32 [8192, 3, 2048], P('fsdp')
- side_grad: float32 [2048, 640], P('fsdp')
- gains_grad: float32 [4608], P('fsdp')
Inputs may be any that keep to these rules, and one draw needn't show every extreme that they name: `seq_lengths`: each length is a multiple of 128, from 1024 to 2048, and they sum to 8192; the longest is exactly 2048 and the shortest exactly 1024. The i-th sequence in the stream is the one whose length is seq_lengths[seq_order[i]].
All inputs are finite; a program needn't handle non-finite values.
Results may differ from a plain program's by a relative error of at most 0.019.
Values may be sent and summed in bfloat16 or wider, within the bound.
A program may use at most 704 MiB of HBM per device.

v0:
```python
import jax
import jax.numpy as jnp
from jax import lax
from jax.sharding import PartitionSpec as P

D = 2048
HQ = 8
KVH = 2
HD = 256
PL = 256
RANK = 64
WINDOW = 512


EPSILON = 1e-06
NEGATIVE = -1e30
ROPE_BASE = 10000.0


def passed_along(block, axis, distance):
    devices = range(lax.axis_size(axis))
    route = [(i - distance, i) for i in devices if i - distance in devices]
    return lax.ppermute(block, axis, route)


def inv_rms(field):
    return lax.rsqrt(jnp.mean(field * field, axis=-1, keepdims=True) + EPSILON)


def gelu_tanh(field):
    return jax.nn.gelu(field, approximate=True)


def layout(seq_lengths, seq_order, token_index):
    slot_ids = jnp.arange(seq_lengths.shape[0], dtype=jnp.int32)
    packed = jnp.sum(
        jnp.where(seq_order[:, None] == slot_ids[None, :], seq_lengths[None, :], 0), axis=1
    )
    starts = jnp.cumsum(packed) - packed
    segment = jnp.sum((token_index[:, None] >= starts[None, :]).astype(jnp.int32), axis=1) - 1
    offset = jnp.max(jnp.where(starts[None, :] <= token_index[:, None], starts[None, :], 0), axis=1)
    return (segment, token_index - offset)


def angles(position):
    half_width = HD // 2
    freq = ROPE_BASE ** (-2.0 * jnp.arange(half_width, dtype=jnp.float32) / HD)
    phase = position.astype(jnp.float32)[:, None] * freq[None, :]
    phase = jnp.concatenate([phase, phase], axis=-1)
    return (jnp.cos(phase)[:, None, :], jnp.sin(phase)[:, None, :])


def rotate(field, cosine, sine):
    half_width = field.shape[-1] // 2
    turned = jnp.concatenate([-field[..., half_width:], field[..., :half_width]], axis=-1)
    return field * cosine + turned * sine


def rotate_back(grad_in, cosine, sine):
    half_width = grad_in.shape[-1] // 2
    shifted = grad_in * sine
    return grad_in * cosine + jnp.concatenate(
        [shifted[..., half_width:], -shifted[..., :half_width]], axis=-1
    )


def norm_back(grad_out, field, scale_inv, gain):
    weighted = grad_out * gain
    return scale_inv * weighted - field * scale_inv**3 * jnp.mean(
        weighted * field, axis=-1, keepdims=True
    )


def contract_rows(left_op, right_op):
    return lax.dot_general(
        left_op, right_op, (((0,), (0,)), ((), ())), preferred_element_type=jnp.float32
    )


def contract_cols(left_op, right_op):
    return lax.dot_general(
        left_op, right_op, (((1,), (1,)), ((), ())), preferred_element_type=jnp.float32
    )


def split_gains(gain_all):
    gain_f = gain_all.astype(jnp.float32)
    return (gain_f[:D], gain_f[D : 2 * D], gain_f[2 * D : 2 * D + HD], gain_f[2 * D + HD :])


def soft_weights(query_four, key_rows, allowed, score_scale):
    scores = (
        jnp.einsum("qkgd,nkd->kgqn", query_four, key_rows, preferred_element_type=jnp.float32)
        * score_scale
    )
    scores = jnp.where(allowed[None, None], scores, NEGATIVE)
    highest = jnp.max(scores, axis=-1, keepdims=True)
    exponent = jnp.exp(scores - highest)
    return exponent / jnp.sum(exponent, axis=-1, keepdims=True)


def local(
    tokens,
    per_layer,
    cotangent,
    seq_lengths,
    seq_order,
    qkv_weight,
    out_weight,
    ffn_weights,
    side_weights,
    norm_gains,
):
    tok_rows = tokens.shape[0]
    my_index = lax.axis_index("fsdp")
    token_index = my_index * tok_rows + jnp.arange(tok_rows, dtype=jnp.int32)
    segment, position = layout(seq_lengths, seq_order, token_index)
    cosine, sine = angles(position)
    reach = (WINDOW + tok_rows - 2) // tok_rows
    key_index = jnp.concatenate(
        [token_index - distance * tok_rows for distance in range(reach, 0, -1)] + [token_index]
    )
    key_segment, unused_pos = layout(seq_lengths, seq_order, key_index)
    key_gap = token_index[:, None] - key_index[None, :]
    allowed = (segment[:, None] == key_segment[None, :]) & (key_gap >= 0) & (key_gap < WINDOW)
    score_scale = HD ** (-0.5)
    split_at = PL + RANK
    group_size = HQ // KVH
    query_width = HQ * HD
    kv_width = KVH * HD
    qkv_all, out_all, side_all, gain_all = (
        lax.all_gather(qkv_weight, "fsdp", axis=0, tiled=True),
        lax.all_gather(out_weight, "fsdp", axis=0, tiled=True),
        lax.all_gather(side_weights, "fsdp", axis=0, tiled=True),
        lax.all_gather(norm_gains, "fsdp", axis=0, tiled=True),
    )
    attn_gain, ffn_gain, query_gain, key_gain = split_gains(gain_all)
    tokens_f = tokens.astype(jnp.float32)
    rms_one = inv_rms(tokens_f)
    normed_b = (tokens_f * rms_one * attn_gain).astype(jnp.bfloat16)
    projected = jnp.dot(normed_b, qkv_all, preferred_element_type=jnp.float32)
    query = projected[:, :query_width].reshape(tok_rows, HQ, HD)
    key_raw = projected[:, query_width : query_width + kv_width].reshape(tok_rows, KVH, HD)
    value_raw = projected[:, query_width + kv_width :].reshape(tok_rows, KVH, HD)
    rms_query = inv_rms(query)
    rms_key = inv_rms(key_raw)
    query_b = rotate(query * rms_query * query_gain, cosine, sine).astype(jnp.bfloat16)
    key_b = rotate(key_raw * rms_key * key_gain, cosine, sine).astype(jnp.bfloat16)
    value_b = value_raw.astype(jnp.bfloat16)
    key_parts = []
    value_parts = []
    for distance in range(reach, 0, -1):
        moved_keys, moved_values = passed_along((key_b, value_b), "fsdp", distance)
        key_parts.append(moved_keys)
        value_parts.append(moved_values)
    key_rows = jnp.concatenate(key_parts + [key_b], axis=0)
    value_rows = jnp.concatenate(value_parts + [value_b], axis=0)
    query_four = query_b.reshape(tok_rows, KVH, group_size, HD)
    probs = soft_weights(query_four, key_rows, allowed, score_scale)
    probs_b = probs.astype(jnp.bfloat16)
    mixed = jnp.einsum("kgqn,nkd->qkgd", probs_b, value_rows, preferred_element_type=jnp.float32)
    mixed_b = mixed.reshape(tok_rows, query_width).astype(jnp.bfloat16)
    first_sum = tokens_f + jnp.dot(mixed_b, out_all, preferred_element_type=jnp.float32)
    rms_two = inv_rms(first_sum)
    normed_two = (first_sum * rms_two * ffn_gain).astype(jnp.bfloat16)
    weight_rows = lax.all_gather(ffn_weights, "fsdp", axis=0, tiled=True)
    gate_out = contract_cols(normed_two, weight_rows[:, 0, :])
    up_out = contract_cols(normed_two, weight_rows[:, 1, :])
    act_out = (gelu_tanh(gate_out) * up_out).astype(jnp.bfloat16)
    ffn_out = jnp.dot(act_out, weight_rows[:, 2, :], preferred_element_type=jnp.float32)
    second_sum = first_sum + ffn_out
    second_b = second_sum.astype(jnp.bfloat16)
    side_in = jnp.dot(second_b, side_all[:, :split_at], preferred_element_type=jnp.float32)
    per_f = per_layer.astype(jnp.float32)
    gelu_per, pull_per = jax.vjp(gelu_tanh, side_in[:, :PL])
    combined = jnp.concatenate(
        [(gelu_per * per_f).astype(jnp.bfloat16), side_in[:, PL:].astype(jnp.bfloat16)], axis=1
    )
    output = (second_sum + contract_cols(combined, side_all[:, split_at:])).astype(jnp.bfloat16)
    back_qkv, back_out, back_side, back_gain = (
        lax.all_gather(qkv_weight, "fsdp", axis=0, tiled=True),
        lax.all_gather(out_weight, "fsdp", axis=0, tiled=True),
        lax.all_gather(side_weights, "fsdp", axis=0, tiled=True),
        lax.all_gather(norm_gains, "fsdp", axis=0, tiled=True),
    )
    attn_gain, ffn_gain, query_gain, key_gain = split_gains(back_gain)
    grad_y = cotangent.astype(jnp.float32)
    grad_comb = jnp.dot(cotangent, back_side[:, split_at:], preferred_element_type=jnp.float32)
    side_out_grad = contract_rows(cotangent, combined)
    per_layer_grad = (grad_comb[:, :PL] * gelu_per).astype(jnp.bfloat16)
    grad_per = pull_per(grad_comb[:, :PL] * per_f)[0]
    grad_side = jnp.concatenate([grad_per, grad_comb[:, PL:]], axis=1).astype(jnp.bfloat16)
    side_in_grad = contract_rows(second_b, grad_side)
    side_grad_full = jnp.concatenate([side_in_grad, side_out_grad], axis=1)
    grad_two = grad_y + contract_cols(grad_side, back_side[:, :split_at])
    grad_two_b = grad_two.astype(jnp.bfloat16)
    weight_rows = lax.all_gather(ffn_weights, "fsdp", axis=0, tiled=True)
    gate_out = contract_cols(normed_two, weight_rows[:, 0, :])
    up_out = contract_cols(normed_two, weight_rows[:, 1, :])
    gelu_gate, pull_gate = jax.vjp(gelu_tanh, gate_out)
    act_b = (gelu_gate * up_out).astype(jnp.bfloat16)
    grad_act_b = contract_cols(grad_two_b, weight_rows[:, 2, :]).astype(jnp.bfloat16)
    grad_gate_b = pull_gate(grad_act_b * up_out)[0].astype(jnp.bfloat16)
    grad_up_b = (grad_act_b * gelu_gate).astype(jnp.bfloat16)
    grad_h2 = jnp.dot(grad_gate_b, weight_rows[:, 0, :], preferred_element_type=jnp.float32)
    grad_h2 = grad_h2 + jnp.dot(grad_up_b, weight_rows[:, 1, :], preferred_element_type=jnp.float32)
    grad_h2, gate_buf, up_buf, act_buf = (grad_h2, grad_gate_b, grad_up_b, act_b)
    ffn_grad = lax.psum_scatter(
        jnp.stack(
            [
                contract_rows(gate_buf, normed_two),
                contract_rows(up_buf, normed_two),
                contract_rows(act_buf, grad_two_b),
            ],
            axis=1,
        ),
        "fsdp",
        scatter_dimension=0,
        tiled=True,
    )
    ffn_gain_grad = jnp.sum(grad_h2 * first_sum * rms_two, axis=0)
    grad_one = grad_two + norm_back(grad_h2, first_sum, rms_two, ffn_gain)
    grad_one_b = grad_one.astype(jnp.bfloat16)
    out_grad_full = contract_rows(mixed_b, grad_one_b)
    grad_mixed_b = contract_cols(grad_one_b, back_out).astype(jnp.bfloat16)
    grad_mixed_four = grad_mixed_b.reshape(tok_rows, KVH, group_size, HD)
    probs_again = soft_weights(query_four, key_rows, allowed, score_scale)
    probs_again_b = probs_again.astype(jnp.bfloat16)
    grad_probs = jnp.einsum(
        "qkgd,nkd->kgqn", grad_mixed_four, value_rows, preferred_element_type=jnp.float32
    )
    row_delta = jnp.sum(probs_again * grad_probs, axis=-1, keepdims=True)
    grad_scores_b = (probs_again * (grad_probs - row_delta)).astype(jnp.bfloat16)
    grad_query_rot = (
        jnp.einsum("kgqn,nkd->qkgd", grad_scores_b, key_rows, preferred_element_type=jnp.float32)
        * score_scale
    )
    grad_keys = (
        jnp.einsum("kgqn,qkgd->nkd", grad_scores_b, query_four, preferred_element_type=jnp.float32)
        * score_scale
    )
    grad_values = jnp.einsum(
        "kgqn,qkgd->nkd", probs_again_b, grad_mixed_four, preferred_element_type=jnp.float32
    )
    local_keys = grad_keys[reach * tok_rows :]
    local_values = grad_values[reach * tok_rows :]
    for distance in range(1, reach + 1):
        first_row = (reach - distance) * tok_rows
        back_keys, back_values = (
            passed_along(
                grad_keys[first_row : first_row + tok_rows].astype(jnp.bfloat16), "fsdp", -distance
            ).astype(jnp.float32),
            passed_along(
                grad_values[first_row : first_row + tok_rows].astype(jnp.bfloat16),
                "fsdp",
                -distance,
            ).astype(jnp.float32),
        )
        local_keys = local_keys + back_keys
        local_values = local_values + back_values
    grad_query_norm = rotate_back(grad_query_rot.reshape(tok_rows, HQ, HD), cosine, sine)
    query_gain_grad = jnp.sum(grad_query_norm * query * rms_query, axis=(0, 1))
    grad_query = norm_back(grad_query_norm, query, rms_query, query_gain)
    grad_key_norm = rotate_back(local_keys, cosine, sine)
    key_gain_grad = jnp.sum(grad_key_norm * key_raw * rms_key, axis=(0, 1))
    grad_key = norm_back(grad_key_norm, key_raw, rms_key, key_gain)
    grad_projected = jnp.concatenate(
        [
            grad_query.reshape(tok_rows, query_width),
            grad_key.reshape(tok_rows, kv_width),
            local_values.reshape(tok_rows, kv_width),
        ],
        axis=1,
    ).astype(jnp.bfloat16)
    qkv_grad_full = contract_rows(normed_b, grad_projected)
    grad_normed = contract_cols(grad_projected, back_qkv)
    attn_gain_grad = jnp.sum(grad_normed * tokens_f * rms_one, axis=0)
    input_grad = (grad_one + norm_back(grad_normed, tokens_f, rms_one, attn_gain)).astype(
        jnp.bfloat16
    )
    gains_grad_full = jnp.concatenate(
        [attn_gain_grad, ffn_gain_grad, query_gain_grad, key_gain_grad]
    )
    qkv_grad, out_grad, side_grad, gains_grad = (
        lax.psum_scatter(qkv_grad_full, "fsdp", scatter_dimension=0, tiled=True),
        lax.psum_scatter(out_grad_full, "fsdp", scatter_dimension=0, tiled=True),
        lax.psum_scatter(side_grad_full, "fsdp", scatter_dimension=0, tiled=True),
        lax.psum_scatter(gains_grad_full, "fsdp", scatter_dimension=0, tiled=True),
    )
    return (output, input_grad, per_layer_grad, qkv_grad, out_grad, ffn_grad, side_grad, gains_grad)


def solution(mesh):
    return jax.shard_map(
        local,
        mesh=mesh,
        in_specs=(
            P("fsdp", None),
            P("fsdp", None),
            P("fsdp", None),
            P(),
            P(),
            P("fsdp", None),
            P("fsdp", None),
            P("fsdp", None, None),
            P("fsdp", None),
            P("fsdp"),
        ),
        out_specs=(
            P("fsdp", None),
            P("fsdp", None),
            P("fsdp", None),
            P("fsdp", None),
            P("fsdp", None),
            P("fsdp", None, None),
            P("fsdp", None),
            P("fsdp"),
        ),
        check_vma=False,
    )
```

profile of v0, /device:TPU:0, one launch (start us, length us, event | category | flops | bytes accessed | tf_op | source)
XLA Modules:
  0.0 3531.5 jit_solution(984430290758359062)
XLA Ops:
  13.7 42.2 %all-reduce = bf16[4608]{0:T(1024)(128)(2,1)S(1)} all-reduce(bf16[4608]{0:T(1024)(128)(2,1)S(1)} %dynamic-update-slice), channel_id=1, replica_groups=mesh['fsdp'=32] {'fsdp'}, use_global_device_ids=true, to_apply=%add | all-reduce | flops 4608 | bytes 18432
  58.4 13.3 all-gather.11.cloned.1.call-done
  71.7 2.9 fusion.49
  75.9 93.5 %all-gather.5.cloned.1.call-done = bf16[2048,3072]{1,0:T(8,128)(2,1)} async-done(((bf16[64,3072]{1,0:T(8,128)(2,1)}), bf16[2048,3072]{1,0:T(8,128)(2,1)}) %all-gather.5.cloned.1.call-update) | async-done | bytes 12582928 | tf_op jit(solution)/shard_map/all_gather | solution.py:132
  169.4 6.5 fusion.83
  175.9 1.6 copy-done.23
  178.4 3.0 collective-permute-start.1
  181.5 3.3 collective-permute-start
  188.3 3.7 collective-permute-start.3
  192.0 2.1 collective-permute-start.2
  194.4 1.3 copy-done.10
  197.9 1.3 multiply_multiply_fusion.7
  200.0 3.0 copy.232
  203.3 1.5 slice_negate_fusion.1
  204.8 2.7 copy.194
  207.5 2.5 copy.195
  210.0 3.1 fusion.37
  213.1 6.3 fusion.122
  219.4 4.0 fusion.43
  223.5 29.5 all-gather.7.cloned.1.call-done
  253.0 5.8 multiply_reduce_fusion.4
  260.4 510.8 %all-gather.9.cloned.1.call-done = bf16[8192,3,2048]{2,0,1:T(8,128)(2,1)} async-done(((bf16[256,3,2048]{2,0,1:T(8,128)(2,1)}), bf16[8192,3,2048]{2,0,1:T(8,128)(2,1)}) %all-gather.9.cloned.1.call-update) | async-done | bytes 100663312 | tf_op jit(solution)/shard_map/all_gather | solution.py:166
  771.2 18.2 fusion.2
  789.5 22.5 multiply_convert_fusion
  811.9 16.8 fusion.23
  828.8 2.9 fusion.53
  834.4 2.9 pad_maximum_fusion.1
  837.4 5.9 copy.240
  843.3 1.7 copy-done.20
  845.0 2.0 convolution_add_fusion
  847.0 23.9 fusion.15
  870.9 17.7 fusion.1
  888.6 21.7 multiply_reduce_fusion.1
  910.3 3.5 subtract_add_fusion
  913.8 8.1 fusion.71
  923.0 2.2 copy.248
  925.7 2.2 copy.251
  928.3 2.2 copy.247
  930.5 5.8 convolution_convert_fusion
  936.9 5.2 fusion.123
  944.2 1.6 collective-permute-start.7
  945.8 4.2 fusion.16
  951.3 2.1 fusion.124
  956.8 3.5 convolution_multiply_fusion
  960.3 2.3 copy.205
  963.0 1.4 copy-done.1
  965.0 2.2 copy.249
  967.8 2.2 copy.252
  970.0 3.0 copy.237
  973.1 7.8 multiply_reduce_fusion
  980.9 1.3 fusion.67
  983.8 2.0 fusion.65
  986.2 10.7 fusion.57
  998.1 26.2 convolution_bitcast_fusion.2
  1024.3 26.2 convolution_bitcast_fusion
  1050.5 30.9 convolution_bitcast_fusion.1
  1081.4 135.4 %pad_maximum_fusion = f32[8192,3,2048]{2,0,1:T(8,128)} fusion(f32[8192,1,2048]{2,0,1:T(8,128)} %convolution_bitcast_fusion, f32[8192,1,2048]{2,0,1:T(8,128)} %convolution_bitcast_fusion.1, f32[8192,1,2048]{2,0,1:T(8,128)} %convolution_bitcast_fusion.2), kind=kLoop, calls=%fused_computation.1 | loop fusion | flops 100663296 | bytes 402653184 | tf_op jit(solution)/shard_map/stack | solution.py:209
  1216.8 1.8 copy.219
  1220.0 3.8 fusion.25
  1223.9 11.1 fusion.35
  1235.1 50.3 %all-reduce.1 = f32[4608]{0:T(1024)S(1)} all-reduce(f32[4608]{0:T(1024)S(1)} %pad_maximum_fusion.13), channel_id=6, replica_groups=mesh['fsdp'=32] {'fsdp'}, use_global_device_ids=true, to_apply=%region_25.26.clone | all-reduce | flops 4608 | bytes 36864
  1286.0 3.2 fusion.32
  1289.2 137.1 %reduce-scatter.7.cloned.1.call-done = f32[64,3072]{1,0:T(8,128)} async-done(((f32[2048,3072]{1,0:T(8,128)}), f32[64,3072]{1,0:T(8,128)}) %reduce-scatter.7.cloned.1.call-update) | async-done | bytes 786448 | tf_op jit(solution)/shard_map/reduce_scatter | solution.py:285
  1426.3 2098.2 %reduce-scatter.11.cloned.1.call-done = f32[256,3,2048]{2,0,1:T(8,128)} async-done(((f32[8192,3,2048]{2,0,1:T(8,128)}), f32[256,3,2048]{2,0,1:T(8,128)}) %reduce-scatter.11.cloned.1.call-update) | async-done | bytes 6291472 | tf_op jit(solution)/shard_map/reduce_scatter | solution.py:208
  (257 shorter events, 38.0 us)
Async XLA Ops:
  7.2 3.7 copy-start.73
  7.2 3.7 copy-start.72
  7.2 64.5 %all-gather.11.cloned.1.call-start = ((), (), s32[]{:S(2)}) async-start(), calls=%async_computation.7 | async-start | bytes 2703360 | tf_op jit(solution)/shard_map/all_gather | solution.py:134
  7.9 161.5 %all-gather.5.cloned.1.call-start = ((), (), s32[]{:S(2)}) async-start(), calls=%async_computation.4 | async-start | bytes 12976128 | tf_op jit(solution)/shard_map/all_gather | solution.py:132
  8.7 244.3 %all-gather.7.cloned.1.call-start = ((), (), s32[]{:S(2)}) async-start(), calls=%async_computation.5 | async-start | bytes 8650752 | tf_op jit(solution)/shard_map/all_gather | solution.py:133
  9.4 4.0 copy-start.74
  9.4 46.5 %copy-start.13 = (bf16[256,2048]{1,0:T(8,128)(2,1)S(1)}, bf16[256,2048]{1,0:T(8,128)(2,1)}, u32[]{:S(2)}) copy-start(bf16[256,2048]{1,0:T(8,128)(2,1)} %param.10) | copy-start | bytes 3145732
  9.4 62.2 %copy-start.32 = (bf16[256,2048]{1,0:T(8,128)(2,1)S(1)}, bf16[256,2048]{1,0:T(8,128)(2,1)}, u32[]{:S(2)}) copy-start(bf16[256,2048]{1,0:T(8,128)(2,1)} %param.12) | copy-start | bytes 3145732
  9.5 761.8 %all-gather.9.cloned.1.call-start = ((), (), s32[]{:S(2)}) async-start(), calls=%async_computation.6 | async-start | bytes 103809024 | tf_op jit(solution)/shard_map/all_gather | solution.py:166
  10.0 1279.1 %reduce-scatter.13.cloned.1.call-start = ((), (), s32[]{:S(2)}) async-start(), calls=%async_computation.11 | async-start | bytes 5406720
  12.4 175.0 %copy-start.18 = (f32[256,256]{1,0:T(8,128)}, f32[256,256]{1,0:T(8,128)S(1)}, u32[]{:S(2)}) copy-start(f32[256,256]{1,0:T(8,128)S(1)} %get-tuple-element.84) | copy-start | bytes 786436
  12.4 175.0 %copy-start.25 = (f32[256,256]{1,0:T(8,128)}, f32[256,256]{1,0:T(8,128)S(1)}, u32[]{:S(2)}) copy-start(f32[256,256]{1,0:T(8,128)S(1)} %get-tuple-element.85) | copy-start | bytes 786436
  56.8 119.1 %copy-start.56 = (f32[256]{0:T(256)}, f32[256]{0:T(256)S(1)}, u32[]{:S(2)}) copy-start(f32[256]{0:T(256)S(1)} %get-tuple-element.95) | copy-start | bytes 3076
  57.4 118.5 %copy-start.47 = (f32[2048]{0:T(1024)}, f32[2048]{0:T(1024)S(1)}, u32[]{:S(2)}) copy-start(f32[2048]{0:T(1024)S(1)} %get-tuple-element.87) | copy-start | bytes 24580
  177.6 9.7 copy-start.59
  178.4 9.0 copy-start.60
  178.4 41.0 %collective-permute-start.1 = (bf16[256,2,256]{0,2,1:T(8,128)(2,1)}, bf16[256,2,256]{0,2,1:T(8,128)(2,1)}, u32[]{:S(2)}, u32[]{:S(2)}) collective-permute-start(bf16[256,2,256]{0,2,1:T(8,128)(2,1)} %bitcast.35), channel_id=1, source_target_pairs={{0,1},{1,2},{2,3},{3,4},{4,5},{5,6},{6,7},{7,8},{8,9},{9,10},{10,1... | collective-permute-start | bytes 786440 | tf_op jit(solution)/shard_map/ppermute | solution.py:23
  181.5 38.0 %collective-permute-start = (bf16[256,2,256]{0,2,1:T(8,128)(2,1)}, bf16[256,2,256]{0,2,1:T(8,128)(2,1)}, u32[]{:S(2)}, u32[]{:S(2)}) collective-permute-start(bf16[256,2,256]{0,2,1:T(8,128)(2,1)} %bitcast.35), channel_id=1, source_target_pairs={{0,2},{1,3},{2,4},{3,5},{4,6},{5,7},{6,8},{7,9},{8,10},{9,11},{10,... | collective-permute-start | bytes 786440 | tf_op jit(solution)/shard_map/ppermute | solution.py:23
  186.6 7.5 copy-start.24
  187.2 7.2 copy-start.51
  188.3 24.8 collective-permute-start.3
  192.0 21.1 collective-permute-start.2
  196.6 6.4 copy-start
  200.0 3.4 copy-start.34
  204.8 5.2 copy-start.22
  204.8 5.2 copy-start.54
  204.8 5.2 copy-start.63
  219.4 4.1 copy-start.65
  223.5 35.3 copy-start.27
  260.4 529.0 %copy-start.16 = (bf16[256,2048]{1,0:T(8,128)(2,1)}, bf16[256,2048]{1,0:T(8,128)(2,1)S(1)}, u32[]{:S(2)}) copy-start(bf16[256,2048]{1,0:T(8,128)(2,1)S(1)} %multiply_convert_fusion.1) | copy-start | bytes 3145732
  828.7 4.4 copy-start.2
  828.8 3.9 copy-start.44
  843.3 445.9 %reduce-scatter.9.cloned.1.call-start = ((), (), s32[]{:S(2)}) async-start(), calls=%async_computation.9 | async-start | bytes 17301504 | tf_op jit(solution)/shard_map/reduce_scatter | solution.py:286
  847.0 24.0 copy-start.6
  870.9 17.7 copy-start.9
  888.6 21.7 copy-start.71
  910.3 3.5 copy-start.28
  913.8 16.7 copy-start.4
  921.9 504.4 %reduce-scatter.7.cloned.1.call-start = ((), (), s32[]{:S(2)}) async-start(), calls=%async_computation.8 | async-start | bytes 25952256 | tf_op jit(solution)/shard_map/reduce_scatter | solution.py:285
  930.5 6.4 copy-start.66
  936.9 13.1 slice-start
  942.9 38.0 %collective-permute-start.6 = (bf16[256,2,256]{0,2,1:T(8,128)(2,1)}, bf16[256,2,256]{0,2,1:T(8,128)(2,1)}, u32[]{:S(2)}, u32[]{:S(2)}) collective-permute-start(bf16[256,2,256]{0,2,1:T(8,128)(2,1)} %get-tuple-element.75), channel_id=1, source_target_pairs={{1,0},{2,1},{3,2},{4,3},{5,4},{6,5},{7,6},{8,7},{9,8},{10,9},{11,1... | collective-permute-start | bytes 786440 | tf_op jit(solution)/shard_map/ppermute | solution.py:23
  944.2 5.8 slice-start.1
  944.2 36.7 %collective-permute-start.7 = (bf16[256,2,256]{0,2,1:T(8,128)(2,1)}, bf16[256,2,256]{0,2,1:T(8,128)(2,1)}, u32[]{:S(2)}, u32[]{:S(2)}) collective-permute-start(bf16[256,2,256]{0,2,1:T(8,128)(2,1)} %get-tuple-element.76), channel_id=1, source_target_pairs={{2,0},{3,1},{4,2},{5,3},{6,4},{7,5},{8,6},{9,7},{10,8},{11,9},{12,... | collective-permute-start | bytes 786440 | tf_op jit(solution)/shard_map/ppermute | solution.py:23
  954.2 28.2 collective-permute-start.4
  955.5 26.9 collective-permute-start.5
  970.0 3.1 copy-start.21
  982.4 3.7 copy-start.38
  982.4 3.4 copy-start.67
  986.1 10.8 copy-start.40
  996.9 27.4 copy-start.7
  996.9 2527.5 %reduce-scatter.11.cloned.1.call-start = ((), (), s32[]{:S(2)}) async-start(), calls=%async_computation.10 | async-start | bytes 207618048 | tf_op jit(solution)/shard_map/reduce_scatter | solution.py:208
  1216.7 3.2 copy-start.3
  1216.8 3.2 copy-start.37
  1216.8 7.0 copy-start.15
  1216.8 7.0 copy-start.39
  1216.8 7.0 copy-start.49
  1219.3 4.6 copy-start.58
  1220.0 3.9 copy-start.31
  1220.0 3.9 copy-start.41
  1223.9 11.2 copy-start.68
  1223.9 11.2 copy-start.69
  1223.9 62.1 %copy-start.5 = (f32[256,2048]{1,0:T(8,128)S(1)}, f32[256,2048]{1,0:T(8,128)}, u32[]{:S(2)}) copy-start(f32[256,2048]{1,0:T(8,128)} %copy-done.4) | copy-start | bytes 6291460
  1223.9 62.1 %copy-start.70 = (f32[256]{0:T(256)S(1)}, f32[256]{0:T(256)}, u32[]{:S(2)}) copy-start(f32[256]{0:T(256)} %get-tuple-element.94) | copy-start | bytes 3076
  (29 other events, 58.3 us)
Sparse Core Ops, SparseCore 0:
  10.9 60.7 all-gather.10
  74.5 94.8 all-gather.4
  172.3 80.6 all-gather.6
  255.7 515.4 all-gather.8
  843.4 144.0 reduce-scatter.12
  990.2 180.8 reduce-scatter.8
  1178.1 248.1 reduce-scatter.6
  1429.4 2095.0 reduce-scatter.10
where the time goes:
time: 3550 us; the launch traced here: 3530 us
  waiting for transfers between devices  2890 us (81%)
  matrix products  290 us (8%)
  other arithmetic  174 us (5%)
  blocking collectives  92.5 us (3%)
  local copies, waits for them, and re-layouts  55.8 us (2%)
    reduce_scatter x1, waiting for transfers between devices, local(): lax.psum_scatter(jnp.stack([contract_rows(gate_buf, normed_two), contract...  2100 us
    all_gather x1, waiting for transfers between devices, local(): weight_rows = lax.all_gather(ffn_weights, 'fsdp', axis=0, tiled=True)  511 us
    reduce_scatter x1, waiting for transfers between devices, local(): lax.psum_scatter(qkv_grad_full, 'fsdp', scatter_dimension=0, tiled=True)  137 us
    another operation x1, other arithmetic, local(): jnp.stack([contract_rows(gate_buf, normed_two), contract_rows(up_buf, nor...  135 us
    dot_general x7, matrix products, contract_rows(): lax.dot_general(left_op, right_op, (((0,), (0,)), ((), ())), preferred_el...  103 us
    all_gather x1, waiting for transfers between devices, local(): lax.all_gather(qkv_weight, 'fsdp', axis=0, tiled=True)  93.5 us
    unnamed x2, blocking collectives  92.5 us
    dot_general x7, matrix products, contract_cols(): lax.dot_general(left_op, right_op, (((1,), (1,)), ((), ())), preferred_el...  87.4 us
  transfers between devices with their start and end apart: 16, of which 6 were waited for; matrix products, arithmetic and copies ran while one was open for 12% of the time, Pallas kernels for 0%

commit v1 on v0

--- a/solution.py
+++ b/solution.py
@@ -17,6 +17,17 @@
 ROPE_BASE = 10000.0
 
 
+GROUP = 8
+
+
+def token_groups(count):
+    return [[g * GROUP + i for i in range(GROUP)] for g in range(count // GROUP)]
+
+
+def weight_groups(count):
+    return [[g * GROUP + i for g in range(count // GROUP)] for i in range(GROUP)]
+
+
 def passed_along(block, axis, distance):
     devices = range(lax.axis_size(axis))
     route = [(i - distance, i) for i in devices if i - distance in devices]
@@ -36,7 +47,7 @@
     packed = jnp.sum(
         jnp.where(seq_order[:, None] == slot_ids[None, :], seq_lengths[None, :], 0), axis=1
     )
-    starts = jnp.cumsum(packed) - packed
+    starts = jnp.sum(jnp.where(slot_ids[None, :] < slot_ids[:, None], packed[None, :], 0), axis=1)
     segment = jnp.sum((token_index[:, None] >= starts[None, :]).astype(jnp.int32), axis=1) - 1
     offset = jnp.max(jnp.where(starts[None, :] <= token_index[:, None], starts[None, :], 0), axis=1)
     return (segment, token_index - offset)
@@ -163,11 +174,25 @@
     first_sum = tokens_f + jnp.dot(mixed_b, out_all, preferred_element_type=jnp.float32)
     rms_two = inv_rms(first_sum)
     normed_two = (first_sum * rms_two * ffn_gain).astype(jnp.bfloat16)
-    weight_rows = lax.all_gather(ffn_weights, "fsdp", axis=0, tiled=True)
-    gate_out = contract_cols(normed_two, weight_rows[:, 0, :])
-    up_out = contract_cols(normed_two, weight_rows[:, 1, :])
-    act_out = (gelu_tanh(gate_out) * up_out).astype(jnp.bfloat16)
-    ffn_out = jnp.dot(act_out, weight_rows[:, 2, :], preferred_element_type=jnp.float32)
+    count = lax.axis_size("fsdp")
+    by_token, by_weight = token_groups(count), weight_groups(count)
+    gate_w, up_w, down_w = (
+        lax.all_gather(
+            ffn_weights[:, i, :], "fsdp", axis=0, tiled=True, axis_index_groups=by_weight
+        )
+        for i in range(3)
+    )
+    normed_all = lax.all_gather(
+        normed_two, "fsdp", axis=0, tiled=True, axis_index_groups=by_token
+    )
+    gate_out = contract_cols(normed_all, gate_w)
+    up_out = contract_cols(normed_all, up_w)
+    gelu_gate, pull_gate = jax.vjp(gelu_tanh, gate_out)
+    act_b = (gelu_gate * up_out).astype(jnp.bfloat16)
+    ffn_part = jnp.dot(act_b, down_w, preferred_element_type=jnp.float32).astype(jnp.bfloat16)
+    ffn_out = lax.psum_scatter(
+        ffn_part, "fsdp", scatter_dimension=0, tiled=True, axis_index_groups=by_token
+    ).astype(jnp.float32)
     second_sum = first_sum + ffn_out
     second_b = second_sum.astype(jnp.bfloat16)
     side_in = jnp.dot(second_b, side_all[:, :split_at], preferred_element_type=jnp.float32)
@@ -177,13 +202,7 @@
         [(gelu_per * per_f).astype(jnp.bfloat16), side_in[:, PL:].astype(jnp.bfloat16)], axis=1
     )
     output = (second_sum + contract_cols(combined, side_all[:, split_at:])).astype(jnp.bfloat16)
-    back_qkv, back_out, back_side, back_gain = (
-        lax.all_gather(qkv_weight, "fsdp", axis=0, tiled=True),
-        lax.all_gather(out_weight, "fsdp", axis=0, tiled=True),
-        lax.all_gather(side_weights, "fsdp", axis=0, tiled=True),
-        lax.all_gather(norm_gains, "fsdp", axis=0, tiled=True),
-    )
-    attn_gain, ffn_gain, query_gain, key_gain = split_gains(back_gain)
+    back_qkv, back_out, back_side = qkv_all, out_all, side_all
     grad_y = cotangent.astype(jnp.float32)
     grad_comb = jnp.dot(cotangent, back_side[:, split_at:], preferred_element_type=jnp.float32)
     side_out_grad = contract_rows(cotangent, combined)
@@ -194,29 +213,37 @@
     side_grad_full = jnp.concatenate([side_in_grad, side_out_grad], axis=1)
     grad_two = grad_y + contract_cols(grad_side, back_side[:, :split_at])
     grad_two_b = grad_two.astype(jnp.bfloat16)
-    weight_rows = lax.all_gather(ffn_weights, "fsdp", axis=0, tiled=True)
-    gate_out = contract_cols(normed_two, weight_rows[:, 0, :])
-    up_out = contract_cols(normed_two, weight_rows[:, 1, :])
-    gelu_gate, pull_gate = jax.vjp(gelu_tanh, gate_out)
-    act_b = (gelu_gate * up_out).astype(jnp.bfloat16)
-    grad_act_b = contract_cols(grad_two_b, weight_rows[:, 2, :]).astype(jnp.bfloat16)
+    grad_two_all = lax.all_gather(
+        grad_two_b, "fsdp", axis=0, tiled=True, axis_index_groups=by_token
+    )
+    grad_act_b = contract_cols(grad_two_all, down_w).astype(jnp.bfloat16)
     grad_gate_b = pull_gate(grad_act_b * up_out)[0].astype(jnp.bfloat16)
     grad_up_b = (grad_act_b * gelu_gate).astype(jnp.bfloat16)
-    grad_h2 = jnp.dot(grad_gate_b, weight_rows[:, 0, :], preferred_element_type=jnp.float32)
-    grad_h2 = grad_h2 + jnp.dot(grad_up_b, weight_rows[:, 1, :], preferred_element_type=jnp.float32)
-    grad_h2, gate_buf, up_buf, act_buf = (grad_h2, grad_gate_b, grad_up_b, act_b)
-    ffn_grad = lax.psum_scatter(
-        jnp.stack(
-            [
-                contract_rows(gate_buf, normed_two),
-                contract_rows(up_buf, normed_two),
-                contract_rows(act_buf, grad_two_b),
-            ],
-            axis=1,
-        ),
+    grad_h2 = jnp.dot(grad_gate_b, gate_w, preferred_element_type=jnp.float32)
+    grad_h2 = grad_h2 + jnp.dot(grad_up_b, up_w, preferred_element_type=jnp.float32)
+    grad_h2 = lax.psum_scatter(
+        grad_h2.astype(jnp.bfloat16),
         "fsdp",
         scatter_dimension=0,
         tiled=True,
+        axis_index_groups=by_token,
+    ).astype(jnp.float32)
+    ffn_grad = jnp.stack(
+        [
+            lax.psum_scatter(
+                contract_rows(left, right).astype(jnp.bfloat16),
+                "fsdp",
+                scatter_dimension=0,
+                tiled=True,
+                axis_index_groups=by_weight,
+            ).astype(jnp.float32)
+            for left, right in (
+                (grad_gate_b, normed_all),
+                (grad_up_b, normed_all),
+                (act_b, grad_two_all),
+            )
+        ],
+        axis=1,
     )
     ffn_gain_grad = jnp.sum(grad_h2 * first_sum * rms_two, axis=0)
     grad_one = grad_two + norm_back(grad_h2, first_sum, rms_two, ffn_gain)
@@ -281,12 +308,13 @@
     gains_grad_full = jnp.concatenate(
         [attn_gain_grad, ffn_gain_grad, query_gain_grad, key_gain_grad]
     )
-    qkv_grad, out_grad, side_grad, gains_grad = (
-        lax.psum_scatter(qkv_grad_full, "fsdp", scatter_dimension=0, tiled=True),
-        lax.psum_scatter(out_grad_full, "fsdp", scatter_dimension=0, tiled=True),
-        lax.psum_scatter(side_grad_full, "fsdp", scatter_dimension=0, tiled=True),
-        lax.psum_scatter(gains_grad_full, "fsdp", scatter_dimension=0, tiled=True),
-    )
+    qkv_grad, out_grad, side_grad = (
+        lax.psum_scatter(
+            full.astype(jnp.bfloat16), "fsdp", scatter_dimension=0, tiled=True
+        ).astype(jnp.float32)
+        for full in (qkv_grad_full, out_grad_full, side_grad_full)
+    )
+    gains_grad = lax.psum_scatter(gains_grad_full, "fsdp", scatter_dimension=0, tiled=True)
     return (output, input_grad, per_layer_grad, qkv_grad, out_grad, ffn_grad, side_grad, gains_grad)
 
 

time: 3550 us -> 1520 us (0.43)
  waiting for transfers between devices: 2890 us -> 1040 us
  other arithmetic: 174 us -> 50.8 us
  matrix products: 290 us -> 241 us
    reduce_scatter x3 -> x7, waiting for transfers between devices: 2240 us -> 561 us  [the longest x2 246 us: local(): lax.psum_scatter(full.astype(jnp.bfloat16), 'fsdp', scatter_dimension=0,...]
    all_gather x1 -> x5, waiting for transfers between devices: 511 us -> 309 us  [the longest x3 199 us: local(): lax.all_gather(ffn_weights[:, i, :], 'fsdp', axis=0, tiled=True, axis_ind...]
    another operation x3 -> x2, other arithmetic: 137 us -> 7.09 us  [the longest x1 5.13 us: local(): jnp.stack([lax.psum_scatter(contract_rows(left, right).astype(jnp.bfloat1...]
    unnamed x9 -> x17, waiting for transfers between devices: 2.65 us -> 49.9 us
    all_gather x1, waiting for transfers between devices: 93.5 us -> 49.5 us  [local(): lax.all_gather(qkv_weight, 'fsdp', axis=0, tiled=True)]
    dot_general x7, matrix products: 103 us -> 63.8 us  [contract_rows(): lax.dot_general(left_op, right_op, (((0,), (0,)), ((), ())), preferred_el...]
  transfers between devices with their start and end apart: 16 -> 24, of which waited for: 6 -> 16; matrix products, arithmetic and copies ran while one was open for 12% -> 18% of each run, Pallas kernels for 0% -> 0%
where the time goes in v1:
time: 1520 us
  waiting for transfers between devices  1040 us (68%)
  matrix products  241 us (16%)
  blocking collectives  86.4 us (6%)
  local copies, waits for them, and re-layouts  63.1 us (4%)
  other arithmetic  50.8 us (3%)
  starting transfers between devices  18.6 us (1%)
  between operations  15.3 us (1%)
    reduce_scatter x2, waiting for transfers between devices, local(): lax.psum_scatter(full.astype(jnp.bfloat16), 'fsdp', scatter_dimension=0,...  246 us
    reduce_scatter x3, waiting for transfers between devices, local(): lax.psum_scatter(contract_rows(left, right).astype(jnp.bfloat16), 'fsdp',...  232 us
    all_gather x3, waiting for transfers between devices, local(): lax.all_gather(ffn_weights[:, i, :], 'fsdp', axis=0, tiled=True, axis_ind...  199 us
    unnamed x2, blocking collectives  86.4 us
    dot_general x7, matrix products, contract_cols(): lax.dot_general(left_op, right_op, (((1,), (1,)), ((), ())), preferred_el...  81.1 us
    reduce_scatter x1, waiting for transfers between devices, local(): lax.psum_scatter(ffn_part, 'fsdp', scatter_dimension=0, tiled=True, axis_...  70.1 us
    dot_general x7, matrix products, contract_rows(): lax.dot_general(left_op, right_op, (((0,), (0,)), ((), ())), preferred_el...  63.8 us
    all_gather x1, waiting for transfers between devices, local(): lax.all_gather(normed_two, 'fsdp', axis=0, tiled=True, axis_index_groups=...  54.7 us
  transfers between devices with their start and end apart: 24, of which 16 were waited for; matrix products, arithmetic and copies ran while one was open for 18% of the time, Pallas kernels for 0%

profile of v1, /device:TPU:0, one launch (start us, length us, event | category | flops | bytes accessed | tf_op | source)
XLA Modules:
  0.0 1516.0 jit_solution(16277975072961098665)
XLA Ops:
  8.7 3.7 fusion.124
  12.8 43.0 %all-reduce = bf16[4608]{0:T(1024)(128)(2,1)S(1)} all-reduce(bf16[4608]{0:T(1024)(128)(2,1)S(1)} %dynamic-update-slice), channel_id=1, replica_groups=mesh['fsdp'=32] {'fsdp'}, use_global_device_ids=true, to_apply=%add | all-reduce | flops 4608 | bytes 18432
  60.9 49.5 %all-gather.12.cloned.1.call-done = bf16[2048,3072]{1,0:T(8,128)(2,1)} async-done(((bf16[64,3072]{1,0:T(8,128)(2,1)}), bf16[2048,3072]{1,0:T(8,128)(2,1)}) %all-gather.12.cloned.1.call-update) | async-done | bytes 12582928 | tf_op jit(solution)/shard_map/all_gather | solution.py:143
  110.4 6.5 fusion.89
  119.4 2.9 collective-permute-start.1
  122.3 3.3 collective-permute-start
  129.1 3.7 collective-permute-start.3
  140.8 3.0 copy.232
  145.6 2.7 copy.194
  148.3 2.5 copy.195
  150.8 3.1 fusion.49
  153.9 6.3 fusion.131
  160.3 5.0 fusion.55
  165.3 28.5 %all-gather.14.cloned.1.call-done = bf16[2048,2048]{1,0:T(8,128)(2,1)} async-done(((bf16[64,2048]{1,0:T(8,128)(2,1)}), bf16[2048,2048]{1,0:T(8,128)(2,1)}) %all-gather.14.cloned.1.call-update) | async-done | bytes 8388624 | tf_op jit(solution)/shard_map/all_gather | solution.py:144
  193.8 6.2 multiply_reduce_fusion.2
  204.5 70.2 %all-gather.22.cloned.1.call-done = bf16[1024,1,2048]{2,0,1:T(8,128)(2,1)} async-done(((bf16[256,1,2048]{2,0,1:T(8,128)(2,1)}), bf16[1024,1,2048]{2,0,1:T(8,128)(2,1)}) %all-gather.22.cloned.1.call-update) | async-done | bytes 4194320 | tf_op jit(solution)/shard_map/all_gather | solution.py:180
  274.8 54.7 %all-gather.16.cloned.1.call-done = bf16[2048,2048]{1,0:T(8,128)(2,1)} async-done(((bf16[256,2048]{1,0:T(8,128)(2,1)}), bf16[2048,2048]{1,0:T(8,128)(2,1)}) %all-gather.16.cloned.1.call-update) | async-done | bytes 8388624 | tf_op jit(solution)/shard_map/all_gather | solution.py:185
  329.5 14.6 fusion.21
  344.1 67.6 %all-gather.24.cloned.1.call-done = bf16[1024,1,2048]{2,0,1:T(8,128)(2,1)} async-done(((bf16[256,1,2048]{2,0,1:T(8,128)(2,1)}), bf16[1024,1,2048]{2,0,1:T(8,128)(2,1)}) %all-gather.24.cloned.1.call-update) | async-done | bytes 4194320 | tf_op jit(solution)/shard_map/all_gather | solution.py:180
  411.7 19.1 %multiply_convert_fusion = (bf16[2048,1024]{1,0:T(8,128)(2,1)}, f32[2048,1024]{1,0:T(8,128)}) fusion(f32[2048,1024]{1,0:T(8,128)} %fusion.21, bf16[2048,2048]{1,0:T(8,128)(2,1)} %all-gather.16.cloned.1.call-done, bf16[1024,1,2048]{2,0,1:T(8,128)(2,1)} %all-gather.24.cloned.1.call-done), kind=kOutput, calls=%fused_computation.15 | convolution fusion | flops 8610906112 | bytes 33554432 | tf_op jit(solution)/shard_map/dot_general | solution.py:92
  430.8 61.6 %all-gather.26.cloned.1.call-done = bf16[1024,1,2048]{2,0,1:T(8,128)(2,1)} async-done(((bf16[256,1,2048]{2,0,1:T(8,128)(2,1)}), bf16[1024,1,2048]{2,0,1:T(8,128)(2,1)}) %all-gather.26.cloned.1.call-update) | async-done | bytes 4194320 | tf_op jit(solution)/shard_map/all_gather | solution.py:180
  492.4 14.4 convolution_convert_fusion.2
  508.5 43.2 %all-gather.18.cloned.1.call-done = bf16[2048,640]{1,0:T(8,128)(2,1)} async-done(((bf16[64,640]{1,0:T(8,128)(2,1)}), bf16[2048,640]{1,0:T(8,128)(2,1)}) %all-gather.18.cloned.1.call-update) | async-done | bytes 2621456 | tf_op jit(solution)/shard_map/all_gather | solution.py:145
  551.8 2.9 fusion.62
  555.3 70.1 %reduce-scatter.11.cloned.1.call-done = bf16[256,2048]{1,0:T(8,128)(2,1)} async-done(((bf16[2048,2048]{1,0:T(8,128)(2,1)}), bf16[256,2048]{1,0:T(8,128)(2,1)}) %reduce-scatter.11.cloned.1.call-update) | async-done | bytes 1048592 | tf_op jit(solution)/shard_map/reduce_scatter | solution.py:193
  625.4 2.6 fusion.66
  629.9 2.5 fusion.132
  632.4 54.5 %all-gather.20.cloned.1.call-done = bf16[2048,2048]{1,0:T(8,128)(2,1)} async-done(((bf16[256,2048]{1,0:T(8,128)(2,1)}), bf16[2048,2048]{1,0:T(8,128)(2,1)}) %all-gather.20.cloned.1.call-update) | async-done | bytes 8388624 | tf_op jit(solution)/shard_map/all_gather | solution.py:216
  686.9 24.2 %fusion.8 = (bf16[2048,1024]{1,0:T(8,128)(2,1)}, bf16[2048,1024]{1,0:T(8,128)(2,1)}) fusion(f32[2048,1024]{1,0:T(8,128)} %fusion.21, f32[2048,1024]{1,0:T(8,128)} %get-tuple-element.106, bf16[2048,2048]{1,0:T(8,128)(2,1)} %all-gather.20.cloned.1.call-done, bf16[1024,1,2048]{2,0,1:T(8,128)(2,1)} %all-gather.26.cloned.1.call-done), kind=kOutput, calls=%fused_computation.14 | convolution fusion | flops 8638169088 | bytes 37748736 | tf_op jit(solution)/shard_map/dot_general | solution.py:92
  711.1 15.2 %fusion.19 = f32[2048,2048]{1,0:T(8,128)} fusion(bf16[2048,1024]{1,0:T(8,128)(2,1)} %get-tuple-element.109, bf16[1024,1,2048]{2,0,1:T(8,128)(2,1)} %all-gather.22.cloned.1.call-done), kind=kOutput, calls=%fused_computation.39 | convolution fusion | flops 8589934592 | bytes 25165824 | tf_op jit(solution)/shard_map/dot_general | solution.py:222
  726.3 20.3 %add_convert_fusion = bf16[2048,2048]{1,0:T(8,128)(2,1)} fusion(f32[2048,2048]{1,0:T(8,128)} %fusion.19, bf16[1024,1,2048]{2,0,1:T(8,128)(2,1)} %all-gather.24.cloned.1.call-done, bf16[2048,1024]{1,0:T(8,128)(2,1)} %get-tuple-element.110, f32[2048,1024]{1,0:T(8,128)} %fusion.21), kind=kOutput, calls=%fused_computation.1 | convolution fusion | flops 8621391872 | bytes 41943040 | tf_op jit(solution)/shard_map/dot_general | solution.py:223
  752.5 4.6 copy.240
  757.1 15.6 %convolution_convert_fusion.3 = bf16[1024,2048]{1,0:T(8,128)(2,1)} fusion(bf16[2048,1024]{1,0:T(8,128)(2,1)} %get-tuple-element.105, bf16[2048,2048]{1,0:T(8,128)(2,1)} %all-gather.20.cloned.1.call-done), kind=kOutput, calls=%fused_computation.44 | convolution fusion | flops 8592031744 | bytes 16777216 | tf_op jit(solution)/shard_map/dot_general | solution.py:86
  772.8 18.0 %convolution_convert_fusion.4 = bf16[1024,2048]{1,0:T(8,128)(2,1)} fusion(bf16[2048,2048]{1,0:T(8,128)(2,1)} %all-gather.16.cloned.1.call-done, bf16[2048,1024]{1,0:T(8,128)(2,1)} %get-tuple-element.110, f32[2048,1024]{1,0:T(8,128)} %fusion.21), kind=kOutput, calls=%fused_computation.45 | convolution fusion | flops 8615100416 | bytes 25165824 | tf_op jit(solution)/shard_map/dot_general | solution.py:86
  790.9 14.2 convolution_convert_fusion.5
  805.3 12.9 reduce-scatter.13.cloned.1.call-done
  818.2 2.6 fusion.37
  822.8 5.6 convolution_convert_fusion.1
  829.5 2.3 copy.248
  832.3 2.2 copy.251
  834.9 2.3 copy.247
  837.1 6.7 convolution_convert_fusion.8
  843.9 2.3 copy.243
  846.1 5.5 fusion.133
  855.4 4.2 fusion.9
  860.8 3.4 fusion.134
  867.6 3.5 convolution_multiply_fusion
  871.1 3.1 copy.205
  878.9 2.2 copy.249
  883.9 3.0 copy.237
  886.9 8.7 multiply_reduce_fusion
  900.1 2.2 fusion.77
  903.3 7.2 convolution_convert_fusion
  912.3 3.6 fusion.29
  915.9 46.6 %reduce-scatter.25.cloned.1.call-done = bf16[64,640]{1,0:T(8,128)(2,1)} async-done(((bf16[2048,640]{1,0:T(8,128)(2,1)}), bf16[64,640]{1,0:T(8,128)(2,1)}) %reduce-scatter.25.cloned.1.call-update) | async-done | bytes 81936
  964.3 73.2 %reduce-scatter.23.cloned.1.call-done = bf16[256,2048]{1,0:T(8,128)(2,1)} async-done(((bf16[1024,2048]{1,0:T(8,128)(2,1)}), bf16[256,2048]{1,0:T(8,128)(2,1)}) %reduce-scatter.23.cloned.1.call-update) | async-done | bytes 1048592 | tf_op jit(solution)/shard_map/reduce_scatter | solution.py:233
  1037.4 79.7 %reduce-scatter.21.cloned.1.call-done = bf16[256,2048]{1,0:T(8,128)(2,1)} async-done(((bf16[1024,2048]{1,0:T(8,128)(2,1)}), bf16[256,2048]{1,0:T(8,128)(2,1)}) %reduce-scatter.21.cloned.1.call-update) | async-done | bytes 1048592 | tf_op jit(solution)/shard_map/reduce_scatter | solution.py:233
  1117.1 79.4 %reduce-scatter.19.cloned.1.call-done = bf16[256,2048]{1,0:T(8,128)(2,1)} async-done(((bf16[1024,2048]{1,0:T(8,128)(2,1)}), bf16[256,2048]{1,0:T(8,128)(2,1)}) %reduce-scatter.19.cloned.1.call-update) | async-done | bytes 1048592 | tf_op jit(solution)/shard_map/reduce_scatter | solution.py:233
  1196.5 5.1 maximum_convert_fusion
  1201.8 10.4 fusion.47
  1212.2 43.4 %all-reduce.1 = f32[4608]{0:T(1024)S(1)} all-reduce(f32[4608]{0:T(1024)S(1)} %pad_maximum_fusion.12), channel_id=13, replica_groups=mesh['fsdp'=32] {'fsdp'}, use_global_device_ids=true, to_apply=%region_29.30.clone | all-reduce | flops 4608 | bytes 36864
  1256.2 3.2 fusion.44
  1259.3 88.8 %reduce-scatter.17.cloned.1.call-done = bf16[64,2048]{1,0:T(8,128)(2,1)} async-done(((bf16[2048,2048]{1,0:T(8,128)(2,1)}), bf16[64,2048]{1,0:T(8,128)(2,1)}) %reduce-scatter.17.cloned.1.call-update) | async-done | bytes 262160 | tf_op jit(solution)/shard_map/reduce_scatter | solution.py:312
  1349.9 157.2 %reduce-scatter.15.cloned.1.call-done = bf16[64,3072]{1,0:T(8,128)(2,1)} async-done(((bf16[2048,3072]{1,0:T(8,128)(2,1)}), bf16[64,3072]{1,0:T(8,128)(2,1)}) %reduce-scatter.15.cloned.1.call-update) | async-done | bytes 393232 | tf_op jit(solution)/shard_map/reduce_scatter | solution.py:312
  (266 shorter events, 70.4 us)
Async XLA Ops:
  7.2 103.2 %all-gather.12.cloned.1.call-start = ((), (), s32[]{:S(2)}) async-start(), calls=%async_computation.8 | async-start | bytes 12976128 | tf_op jit(solution)/shard_map/all_gather | solution.py:143
  7.9 185.9 %all-gather.14.cloned.1.call-start = ((), (), s32[]{:S(2)}) async-start(), calls=%async_computation.9 | async-start | bytes 8650752 | tf_op jit(solution)/shard_map/all_gather | solution.py:144
  8.7 3.9 copy-start.62
  8.7 47.8 %copy-start.63 = (s32[5]{0:T(128)S(1)}, s32[5]{0:T(128)}, u32[]{:S(2)}) copy-start(s32[5]{0:T(128)} %param.13) | copy-start | bytes 64
  8.7 47.7 %copy-start.64 = (s32[5]{0:T(128)S(1)}, s32[5]{0:T(128)}, u32[]{:S(2)}) copy-start(s32[5]{0:T(128)} %param.14) | copy-start | bytes 64
  8.7 48.1 %copy-start.9 = (bf16[256,2048]{1,0:T(8,128)(2,1)S(1)}, bf16[256,2048]{1,0:T(8,128)(2,1)}, u32[]{:S(2)}) copy-start(bf16[256,2048]{1,0:T(8,128)(2,1)} %param.10) | copy-start | bytes 3145732
  8.7 266.1 %all-gather.22.cloned.1.call-start = ((), (), s32[]{:S(2)}) async-start(), calls=%async_computation.20 | async-start | bytes 5242880 | tf_op jit(solution)/shard_map/all_gather | solution.py:180
  12.4 317.0 %all-gather.16.cloned.1.call-start = ((), (), s32[]{:S(2)}) async-start(), calls=%async_computation.10 | async-start | bytes 9437184 | tf_op jit(solution)/shard_map/all_gather | solution.py:185
  56.4 71.8 %copy-start.47 = (f32[256]{0:T(256)}, f32[256]{0:T(256)S(1)}, u32[]{:S(2)}) copy-start(f32[256]{0:T(256)S(1)} %get-tuple-element.91) | copy-start | bytes 3076
  56.4 60.5 %copy-start.36 = (f32[2048]{0:T(1024)}, f32[2048]{0:T(1024)S(1)}, u32[]{:S(2)}) copy-start(f32[2048]{0:T(1024)S(1)} %get-tuple-element.90) | copy-start | bytes 24580
  56.4 144.1 %copy-start.38 = (f32[2048]{0:T(1024)}, f32[2048]{0:T(1024)S(1)}, u32[]{:S(2)}) copy-start(f32[2048]{0:T(1024)S(1)} %get-tuple-element.89) | copy-start | bytes 24580
  57.6 59.3 %copy-start.51 = (f32[256]{0:T(256)}, f32[256]{0:T(256)S(1)}, u32[]{:S(2)}) copy-start(f32[256]{0:T(256)S(1)} %get-tuple-element.98) | copy-start | bytes 3076
  58.9 69.4 %copy-start.12 = (f32[256,256]{1,0:T(8,128)}, f32[256,256]{1,0:T(8,128)S(1)}, u32[]{:S(2)}) copy-start(f32[256,256]{1,0:T(8,128)S(1)} %get-tuple-element.87) | copy-start | bytes 786436
  58.9 69.4 %copy-start.22 = (f32[256,256]{1,0:T(8,128)}, f32[256,256]{1,0:T(8,128)S(1)}, u32[]{:S(2)}) copy-start(f32[256,256]{1,0:T(8,128)S(1)} %get-tuple-element.88) | copy-start | bytes 786436
  119.4 40.8 %collective-permute-start.1 = (bf16[256,2,256]{0,2,1:T(8,128)(2,1)}, bf16[256,2,256]{0,2,1:T(8,128)(2,1)}, u32[]{:S(2)}, u32[]{:S(2)}) collective-permute-start(bf16[256,2,256]{0,2,1:T(8,128)(2,1)} %bitcast.33), channel_id=1, source_target_pairs={{0,1},{1,2},{2,3},{3,4},{4,5},{5,6},{6,7},{7,8},{8,9},{9,10},{10,1... | collective-permute-start | bytes 786440 | tf_op jit(solution)/shard_map/ppermute | solution.py:34
  122.3 38.0 %collective-permute-start = (bf16[256,2,256]{0,2,1:T(8,128)(2,1)}, bf16[256,2,256]{0,2,1:T(8,128)(2,1)}, u32[]{:S(2)}, u32[]{:S(2)}) collective-permute-start(bf16[256,2,256]{0,2,1:T(8,128)(2,1)} %bitcast.33), channel_id=1, source_target_pairs={{0,2},{1,3},{2,4},{3,5},{4,6},{5,7},{6,8},{7,9},{8,10},{9,11},{10,... | collective-permute-start | bytes 786440 | tf_op jit(solution)/shard_map/ppermute | solution.py:34
  126.7 8.5 copy-start.7
  127.5 7.5 copy-start.21
  128.1 7.2 copy-start.41
  129.1 24.8 %collective-permute-start.3 = (bf16[256,2,256]{2,0,1:T(8,128)(2,1)}, bf16[256,2,256]{2,0,1:T(8,128)(2,1)}, u32[]{:S(2)}, u32[]{:S(2)}) collective-permute-start(bf16[256,2,256]{2,0,1:T(8,128)(2,1)} %fusion.82), channel_id=1, source_target_pairs={{0,1},{1,2},{2,3},{3,4},{4,5},{5,6},{6,7},{7,8},{8,9},{9,10},{10,1... | collective-permute-start | bytes 786440 | tf_op jit(solution)/shard_map/ppermute | solution.py:34
  132.8 21.1 %collective-permute-start.2 = (bf16[256,2,256]{2,0,1:T(8,128)(2,1)}, bf16[256,2,256]{2,0,1:T(8,128)(2,1)}, u32[]{:S(2)}, u32[]{:S(2)}) collective-permute-start(bf16[256,2,256]{2,0,1:T(8,128)(2,1)} %fusion.82), channel_id=1, source_target_pairs={{0,2},{1,3},{2,4},{3,5},{4,6},{5,7},{6,8},{7,9},{8,10},{9,11},{10,... | collective-permute-start | bytes 786440 | tf_op jit(solution)/shard_map/ppermute | solution.py:34
  137.4 6.4 copy-start
  140.8 3.4 copy-start.27
  145.6 5.2 copy-start.18
  145.6 5.2 copy-start.45
  160.2 5.0 copy-start.56
  202.3 209.4 %all-gather.24.cloned.1.call-start = ((), (), s32[]{:S(2)}) async-start(), calls=%async_computation.21 | async-start | bytes 5242880 | tf_op jit(solution)/shard_map/all_gather | solution.py:180
  202.9 289.5 %all-gather.26.cloned.1.call-start = ((), (), s32[]{:S(2)}) async-start(), calls=%async_computation.22 | async-start | bytes 5242880 | tf_op jit(solution)/shard_map/all_gather | solution.py:180
  203.5 348.3 %all-gather.18.cloned.1.call-start = ((), (), s32[]{:S(2)}) async-start(), calls=%async_computation.12 | async-start | bytes 2703360 | tf_op jit(solution)/shard_map/all_gather | solution.py:145
  204.2 421.2 %reduce-scatter.11.cloned.1.call-start = ((), (), s32[]{:S(2)}) async-start(), calls=%async_computation.11 | async-start | bytes 9437184 | tf_op jit(solution)/shard_map/reduce_scatter | solution.py:193
  506.9 44.9 %copy-start.26 = (bf16[256,2048]{1,0:T(8,128)(2,1)S(1)}, bf16[256,2048]{1,0:T(8,128)(2,1)}, u32[]{:S(2)}) copy-start(bf16[256,2048]{1,0:T(8,128)(2,1)} %param.12) | copy-start | bytes 3145732
  506.9 180.0 %all-gather.20.cloned.1.call-start = ((), (), s32[]{:S(2)}) async-start(), calls=%async_computation.13 | async-start | bytes 9437184 | tf_op jit(solution)/shard_map/all_gather | solution.py:216
  625.4 4.4 copy-start.16
  632.4 185.8 %reduce-scatter.13.cloned.1.call-start = ((), (), s32[]{:S(2)}) async-start(), calls=%async_computation.14 | async-start | bytes 9437184 | tf_op jit(solution)/shard_map/reduce_scatter | solution.py:224
  746.7 215.7 %reduce-scatter.25.cloned.1.call-start = ((), (), s32[]{:S(2)}) async-start(), calls=%async_computation.23 | async-start | bytes 2703360
  757.1 280.3 %reduce-scatter.23.cloned.1.call-start = ((), (), s32[]{:S(2)}) async-start(), calls=%async_computation.19 | async-start | bytes 5242880 | tf_op jit(solution)/shard_map/reduce_scatter | solution.py:233
  772.8 344.3 %reduce-scatter.21.cloned.1.call-start = ((), (), s32[]{:S(2)}) async-start(), calls=%async_computation.18 | async-start | bytes 5242880 | tf_op jit(solution)/shard_map/reduce_scatter | solution.py:233
  790.8 405.7 %reduce-scatter.19.cloned.1.call-start = ((), (), s32[]{:S(2)}) async-start(), calls=%async_computation.17 | async-start | bytes 5242880 | tf_op jit(solution)/shard_map/reduce_scatter | solution.py:233
  805.1 13.1 copy-start.39
  805.1 13.1 copy-start.55
  805.1 15.7 %copy-start.61 = (f32[256]{0:T(256)S(1)}, f32[256]{0:T(256)}, u32[]{:S(2)}) copy-start(f32[256]{0:T(256)} %get-tuple-element.99) | copy-start | bytes 3076
  805.1 543.0 %reduce-scatter.17.cloned.1.call-start = ((), (), s32[]{:S(2)}) async-start(), calls=%async_computation.16 | async-start | bytes 8650752 | tf_op jit(solution)/shard_map/reduce_scatter | solution.py:312
  828.4 678.7 %reduce-scatter.15.cloned.1.call-start = ((), (), s32[]{:S(2)}) async-start(), calls=%async_computation.15 | async-start | bytes 12976128 | tf_op jit(solution)/shard_map/reduce_scatter | solution.py:312
  837.1 9.0 copy-start.57
  846.1 9.3 copy-start.32
  846.1 13.4 slice-start
  852.4 43.1 %collective-permute-start.6 = (bf16[256,2,256]{0,2,1:T(8,128)(2,1)}, bf16[256,2,256]{0,2,1:T(8,128)(2,1)S(1)}, u32[]{:S(2)}, u32[]{:S(2)}) collective-permute-start(bf16[256,2,256]{0,2,1:T(8,128)(2,1)} %get-tuple-element.78), channel_id=1, source_target_pairs={{1,0},{2,1},{3,2},{4,3},{5,4},{6,5},{7,6},{8,7},{9,8},{10,9},{11,1... | collective-permute-start | bytes 786440 | tf_op jit(solution)/shard_map/ppermute | solution.py:34
  853.7 5.9 slice-start.1
  853.8 41.8 %collective-permute-start.7 = (bf16[256,2,256]{0,2,1:T(8,128)(2,1)}, bf16[256,2,256]{0,2,1:T(8,128)(2,1)}, u32[]{:S(2)}, u32[]{:S(2)}) collective-permute-start(bf16[256,2,256]{0,2,1:T(8,128)(2,1)} %get-tuple-element.79), channel_id=1, source_target_pairs={{2,0},{3,1},{4,2},{5,3},{6,4},{7,5},{8,6},{9,7},{10,8},{11,9},{12,... | collective-permute-start | bytes 786440 | tf_op jit(solution)/shard_map/ppermute | solution.py:34
  865.0 33.6 %collective-permute-start.4 = (bf16[256,2,256]{2,0,1:T(8,128)(2,1)}, bf16[256,2,256]{2,0,1:T(8,128)(2,1)}, u32[]{:S(2)}, u32[]{:S(2)}) collective-permute-start(bf16[256,2,256]{2,0,1:T(8,128)(2,1)} %get-tuple-element.76), channel_id=1, source_target_pairs={{1,0},{2,1},{3,2},{4,3},{5,4},{6,5},{7,6},{8,7},{9,8},{10,9},{11,1... | collective-permute-start | bytes 786440 | tf_op jit(solution)/shard_map/ppermute | solution.py:34
  866.3 32.3 %collective-permute-start.5 = (bf16[256,2,256]{2,0,1:T(8,128)(2,1)}, bf16[256,2,256]{2,0,1:T(8,128)(2,1)}, u32[]{:S(2)}, u32[]{:S(2)}) collective-permute-start(bf16[256,2,256]{2,0,1:T(8,128)(2,1)} %get-tuple-element.77), channel_id=1, source_target_pairs={{2,0},{3,1},{4,2},{5,3},{6,4},{7,5},{8,6},{9,7},{10,8},{11,9},{12,... | collective-permute-start | bytes 786440 | tf_op jit(solution)/shard_map/ppermute | solution.py:34
  895.5 4.5 copy-start.8
  895.5 4.5 copy-start.42
  895.5 4.5 copy-start.48
  897.5 4.8 copy-start.58
  899.9 3.4 copy-start.10
  900.0 3.3 copy-start.24
  1196.5 5.1 copy-start.44
  1196.5 5.2 copy-start.11
  1196.5 5.2 copy-start.53
  1201.7 10.4 copy-start.43
  1201.7 10.4 copy-start.59
  1201.7 54.4 %copy-start.4 = (f32[256,2048]{1,0:T(8,128)S(1)}, f32[256,2048]{1,0:T(8,128)}, u32[]{:S(2)}) copy-start(f32[256,2048]{1,0:T(8,128)} %copy-done.2) | copy-start | bytes 6291460
  1201.8 54.4 %copy-start.60 = (f32[256]{0:T(256)S(1)}, f32[256]{0:T(256)}, u32[]{:S(2)}) copy-start(f32[256]{0:T(256)} %get-tuple-element.97) | copy-start | bytes 3076
  (27 other events, 52.1 us)
Sparse Core Ops, SparseCore 0:
  10.9 99.4 all-gather.11
  113.3 80.5 all-gather.13
  195.4 79.3 all-gather.21
  276.5 52.9 all-gather.15
  330.9 80.7 all-gather.23
  413.1 79.2 all-gather.25
  495.3 56.4 all-gather.17
  555.2 70.1 reduce-scatter.10
  632.5 54.3 all-gather.19
  746.8 71.3 reduce-scatter.12
  820.4 141.9 reduce-scatter.24
  964.6 72.8 reduce-scatter.22
  1039.8 77.2 reduce-scatter.20
  1119.3 77.2 reduce-scatter.18
  1198.8 149.2 reduce-scatter.16
  1355.0 152.0 reduce-scatter.14

commit v2 on v1

--- a/solution.py
+++ b/solution.py
@@ -1,6 +1,10 @@
+import functools
+
 import jax
 import jax.numpy as jnp
 from jax import lax
+from jax.experimental import pallas as pl
+from jax.experimental.pallas import tpu as pltpu
 from jax.sharding import PartitionSpec as P
 
 D = 2048
@@ -17,15 +21,448 @@
 ROPE_BASE = 10000.0
 
 
-GROUP = 8
-
-
-def token_groups(count):
-    return [[g * GROUP + i for i in range(GROUP)] for g in range(count // GROUP)]
-
-
-def weight_groups(count):
-    return [[g * GROUP + i for g in range(count // GROUP)] for i in range(GROUP)]
+PLANE = 8
+LANES = 128
+MESH = pl.DeviceIdType.MESH
+BF16 = jnp.bfloat16
+F32 = jnp.float32
+
+
+def flipped(index, bit):
+    return index + bit - 2 * bit * lax.rem(lax.div(index, bit), 2)
+
+
+def swapped(block, bit):
+    route = [(i, i ^ bit) for i in range(lax.axis_size("fsdp"))]
+    return lax.ppermute(block, "fsdp", route)
+
+
+def weight_bits(count):
+    return [8] + [1 << i for i in range(5, count.bit_length() - 1)] + [1]
+
+
+def greet(partners):
+    barrier = pltpu.get_barrier_semaphore()
+    for partner in partners:
+        pl.semaphore_signal(barrier, inc=1, device_id=(partner,), device_id_type=MESH)
+    pl.semaphore_wait(barrier, len(partners))
+
+
+def remote(src, dst, send, recv, device):
+    return pltpu.make_async_remote_copy(
+        src_ref=src,
+        dst_ref=dst,
+        send_sem=send,
+        recv_sem=recv,
+        device_id=(device,),
+        device_id_type=MESH,
+    )
+
+
+def half_split(width):
+    return (width // LANES + 1) // 2 * LANES
+
+
+def gather_kernel(chain, own_a, own_b, out_a, out_b, *sems):
+    me = lax.axis_index("fsdp")
+    core, x_at, y_at = lax.rem(me, 2), lax.rem(lax.div(me, 2), 2), lax.rem(lax.div(me, 4), 2)
+    z_at = lax.div(me, PLANE)
+    next_x, next_y, next_c = flipped(me, 2), flipped(me, 4), flipped(me, 1)
+    z_peers = [me + (lax.rem(z_at + s, chain) - z_at) * PLANE for s in range(1, chain)]
+    greet([next_x, next_y, next_c] + z_peers)
+    waves = []
+    for own, out, (local, zs, zr, xs, xr, ys, yr, a_s, ar, bs, br, cs, cr) in (
+        (own_a, out_a, sems[:13]),
+        (own_b, out_b, sems[13:]),
+    ):
+        cut = half_split(own.shape[-1])
+        ops = {"own": pltpu.make_async_copy(own, out.at[z_at, y_at, x_at, core], local)}
+        ops["z"] = [
+            remote(own, out.at[z_at, y_at, x_at, core], zs.at[s], zr.at[s], z_peers[s - 1])
+            for s in range(1, chain)
+        ]
+        steps = []
+        for s in range(chain):
+            k = lax.rem(z_at + chain - s, chain)
+            here = out.at[k, y_at, x_at, core]
+            src = own if s == 0 else here
+            from_x = out.at[k, y_at, 1 - x_at, core]
+            from_y = out.at[k, 1 - y_at, x_at, core]
+            left, right = pl.ds(0, cut), pl.ds(cut, own.shape[-1] - cut)
+            steps.append(
+                {
+                    "x": remote(src, here, xs.at[s], xr.at[s], next_x),
+                    "y": remote(src, here, ys.at[s], yr.at[s], next_y),
+                    "a": remote(
+                        from_x.at[:, left], from_x.at[:, left], a_s.at[s], ar.at[s], next_y
+                    ),
+                    "b": remote(
+                        from_y.at[:, right], from_y.at[:, right], bs.at[s], br.at[s], next_x
+                    ),
+                    "c": remote(
+                        out.at[k, :, :, core], out.at[k, :, :, core], cs.at[s], cr.at[s], next_c
+                    ),
+                }
+            )
+        ops["steps"] = steps
+        waves.append(ops)
+    flat = [(w, s) for w in range(2) for s in range(chain)]
+
+    def spread(w, s):
+        ops = waves[w]
+        if s == 0:
+            for copy in [ops["own"]] + ops["z"]:
+                copy.start()
+        else:
+            ops["z"][s - 1].wait_recv()
+        ops["steps"][s]["x"].start()
+        ops["steps"][s]["y"].start()
+
+    def pass_on(w, s):
+        step = waves[w]["steps"][s]
+        step["x"].wait_recv()
+        step["a"].start()
+        step["y"].wait_recv()
+        step["b"].start()
+
+    def across(w, s):
+        step = waves[w]["steps"][s]
+        step["a"].wait_recv()
+        step["b"].wait_recv()
+        if s == 0:
+            waves[w]["own"].wait()
+        step["c"].start()
+
+    for i in range(len(flat) + 2):
+        if i < len(flat):
+            spread(*flat[i])
+        if 1 <= i <= len(flat):
+            pass_on(*flat[i - 1])
+        if i >= 2:
+            across(*flat[i - 2])
+    for ops in waves:
+        for copy in ops["z"]:
+            copy.wait_send()
+        for step in ops["steps"]:
+            for name in "xyab":
+                step[name].wait_send()
+            step["c"].wait()
+
+
+def gather_weights(own_a, own_b):
+    count = lax.axis_size("fsdp")
+    chain = count // PLANE
+    dma = pltpu.SemaphoreType.DMA
+    sems = [dma] + [dma((chain,))] * 12
+    outs = [
+        jax.ShapeDtypeStruct((chain, 2, 2, 2) + own.shape, own.dtype) for own in (own_a, own_b)
+    ]
+    moved = sum(o.size * 2 for o in outs)
+    full_a, full_b = pl.pallas_call(
+        functools.partial(gather_kernel, chain),
+        out_shape=outs,
+        in_specs=[pl.BlockSpec(memory_space=pl.ANY)] * 2,
+        out_specs=[pl.BlockSpec(memory_space=pl.ANY)] * 2,
+        scratch_shapes=sems * 2,
+        compiler_params=pltpu.CompilerParams(collective_id=0, has_side_effects=True),
+        cost_estimate=pl.CostEstimate(flops=0, bytes_accessed=moved * 16, transcendentals=0),
+        name="gather_weights",
+    )(own_a, own_b)
+    return (full_a.reshape(-1, own_a.shape[1]), full_b.reshape(-1, own_b.shape[1]))
+
+
+def add_into(target, *terms):
+    rows = target.shape[0]
+    tile = 16
+
+    @pl.loop(0, rows // tile)
+    def _(i):
+        at = pl.ds(pl.multiple_of(i * tile, tile), tile)
+        total = target[at].astype(F32)
+        for term in terms:
+            total = total + term[at].astype(F32)
+        target[at] = total.astype(target.dtype)
+
+
+def scatter_kernel(chain, part_a, part_b, out_a, out_b, *scratch):
+    me = lax.axis_index("fsdp")
+    core, x_at, y_at = lax.rem(me, 2), lax.rem(lax.div(me, 2), 2), lax.rem(lax.div(me, 4), 2)
+    z_at = lax.div(me, PLANE)
+    next_x, next_y, next_c = flipped(me, 2), flipped(me, 4), flipped(me, 1)
+    z_peers = [me + (lax.rem(z_at + s, chain) - z_at) * PLANE for s in range(1, chain)]
+    greet([next_x, next_y, next_c] + z_peers)
+    waves = []
+    half = len(scratch) // 2
+    for part, out, held in ((part_a, out_a, scratch[:half]), (part_b, out_b, scratch[half:])):
+        mine, sibling, in_a, in_b, in_x, in_y, in_z = held[:7]
+        local, cs, cr, a_s, ar, bs, br, xs, xr, ys, yr, zs, zr = held[7:]
+        width = out.shape[-1]
+        cut = half_split(width)
+        left, right = pl.ds(0, cut), pl.ds(cut, width - cut)
+        steps = []
+        for s in range(chain):
+            k = lax.rem(z_at + s, chain)
+            step = {
+                "left": left,
+                "right": right,
+                "mine": mine.at[s],
+                "sibling": sibling.at[s],
+                "in_a": in_a.at[s],
+                "in_b": in_b.at[s],
+                "in_x": in_x.at[s],
+                "in_y": in_y.at[s],
+                "here": mine.at[s, y_at, x_at],
+                "to_x": mine.at[s, y_at, 1 - x_at],
+                "to_y": mine.at[s, 1 - y_at, x_at],
+                "local": pltpu.make_async_copy(part.at[k, :, :, core], mine.at[s], local.at[s]),
+                "c": remote(
+                    part.at[k, :, :, 1 - core], sibling.at[s], cs.at[s], cr.at[s], next_c
+                ),
+                "a": remote(
+                    mine.at[s, 1 - y_at, 1 - x_at, :, left],
+                    in_a.at[s],
+                    a_s.at[s],
+                    ar.at[s],
+                    next_x,
+                ),
+                "b": remote(
+                    mine.at[s, 1 - y_at, 1 - x_at, :, right],
+                    in_b.at[s],
+                    bs.at[s],
+                    br.at[s],
+                    next_y,
+                ),
+            }
+            step["x"] = remote(step["to_x"], step["in_x"], xs.at[s], xr.at[s], next_x)
+            step["y"] = remote(step["to_y"], step["in_y"], ys.at[s], yr.at[s], next_y)
+            if s > 0:
+                step["z"] = remote(
+                    step["here"], in_z.at[s - 1], zs.at[s - 1], zr.at[s - 1], z_peers[s - 1]
+                )
+            steps.append(step)
+        waves.append((steps, in_z, out))
+    order = [s for s in range(1, chain)] + [0]
+    flat = [waves[w][0][s] for w in range(2) for s in order]
+
+    def halve(step):
+        step["local"].wait()
+        step["c"].wait_recv()
+        for j in range(4):
+            add_into(step["mine"].at[j // 2, j % 2], step["sibling"].at[j // 2, j % 2])
+        step["a"].start()
+        step["b"].start()
+
+    def sideways(step):
+        step["a"].wait_recv()
+        add_into(step["to_y"].at[:, step["left"]], step["in_a"])
+        step["y"].start()
+        step["b"].wait_recv()
+        add_into(step["to_x"].at[:, step["right"]], step["in_b"])
+        step["x"].start()
+
+    def finish(step):
+        step["x"].wait_recv()
+        step["y"].wait_recv()
+        add_into(step["here"], step["in_x"], step["in_y"])
+        if "z" in step:
+            step["z"].start()
+
+    for step in flat:
+        step["local"].start()
+        step["c"].start()
+    for i in range(len(flat) + 2):
+        if i < len(flat):
+            halve(flat[i])
+        if 1 <= i <= len(flat):
+            sideways(flat[i - 1])
+        if i >= 2:
+            finish(flat[i - 2])
+    for steps, in_z, out in waves:
+        for step in steps[1:]:
+            step["z"].wait_recv()
+        rows = out.shape[0]
+
+        @pl.loop(0, rows // 16)
+        def _(i):
+            at = pl.ds(pl.multiple_of(i * 16, 16), 16)
+            total = steps[0]["here"][at].astype(F32)
+            for s in range(chain - 1):
+                total = total + in_z[s, at].astype(F32)
+            out[at] = total
+
+    for step in flat:
+        for name in "cabxyz":
+            if name in step:
+                step[name].wait_send()
+
+
+def scatter_weights(part_a, part_b):
+    count = lax.axis_size("fsdp")
+    chain = count // PLANE
+    dma = pltpu.SemaphoreType.DMA
+    scratch, outs, parts = [], [], []
+    for part in (part_a, part_b):
+        rows, width = part.shape[0] // count, part.shape[1]
+        cut = half_split(width)
+        shapes = [
+            (chain, 2, 2, rows, width),
+            (chain, 2, 2, rows, width),
+            (chain, rows, cut),
+            (chain, rows, width - cut),
+            (chain, rows, width),
+            (chain, rows, width),
+            (chain - 1, rows, width),
+        ]
+        scratch += [pltpu.VMEM(shape, BF16) for shape in shapes] + [dma((chain,))] * 13
+        outs.append(jax.ShapeDtypeStruct((rows, width), F32))
+        parts.append(part.reshape(chain, 2, 2, 2, rows, width))
+    return pl.pallas_call(
+        functools.partial(scatter_kernel, chain),
+        out_shape=outs,
+        in_specs=[pl.BlockSpec(memory_space=pl.ANY)] * 2,
+        out_specs=[pl.BlockSpec(memory_space=pltpu.VMEM)] * 2,
+        scratch_shapes=scratch,
+        compiler_params=pltpu.CompilerParams(
+            collective_id=1, has_side_effects=True, vmem_limit_bytes=56 * 2**20
+        ),
+        name="scatter_weights",
+    )(*parts)
+
+
+TOKEN_BITS = (2, 4, 16)
+
+
+def token_gather_kernel(own, out, local, ss, rs):
+    me = lax.axis_index("fsdp")
+    next_x, next_y, next_z = (flipped(me, bit) for bit in TOKEN_BITS)
+    greet([next_x, next_y, next_z])
+    half = own.shape[0] // 2
+    top, low = pl.ds(0, half), pl.ds(half, half)
+    keep = pltpu.make_async_copy(own, out.at[0], local)
+    copies = [
+        remote(own, out.at[4], ss.at[0], rs.at[0], next_z),
+        remote(own, out.at[1], ss.at[1], rs.at[1], next_x),
+        remote(own, out.at[2], ss.at[2], rs.at[2], next_y),
+        remote(out.at[1, top], out.at[3, top], ss.at[3], rs.at[3], next_y),
+        remote(out.at[2, low], out.at[3, low], ss.at[4], rs.at[4], next_x),
+        remote(out.at[4], out.at[5], ss.at[5], rs.at[5], next_x),
+        remote(out.at[4], out.at[6], ss.at[6], rs.at[6], next_y),
+        remote(out.at[5, top], out.at[7, top], ss.at[7], rs.at[7], next_y),
+        remote(out.at[6, low], out.at[7, low], ss.at[8], rs.at[8], next_x),
+    ]
+    keep.start()
+    for i, after in enumerate((None, None, None, 1, 2, 0, None, 5, 6)):
+        if after is not None:
+            copies[after].wait_recv()
+        copies[i].start()
+    for i in (3, 4, 7, 8):
+        copies[i].wait_recv()
+    for copy in copies:
+        copy.wait_send()
+    keep.wait()
+
+
+def gather_tokens(own, collective_id):
+    dma = pltpu.SemaphoreType.DMA
+    return pl.pallas_call(
+        token_gather_kernel,
+        out_shape=jax.ShapeDtypeStruct((8,) + own.shape, own.dtype),
+        in_specs=[pl.BlockSpec(memory_space=pl.ANY)],
+        out_specs=pl.BlockSpec(memory_space=pl.ANY),
+        scratch_shapes=[dma, dma((9,)), dma((9,))],
+        compiler_params=pltpu.CompilerParams(collective_id=collective_id, has_side_effects=True),
+        name="gather_tokens",
+    )(own).reshape(8 * own.shape[0], own.shape[1])
+
+
+def token_scatter_kernel(part, out, mine, in_half, in_x, in_y, in_z, local, ss, rs):
+    me = lax.axis_index("fsdp")
+    next_x, next_y, next_z = (flipped(me, bit) for bit in TOKEN_BITS)
+    greet([next_x, next_y, next_z])
+    half = out.shape[0] // 2
+    top, low = pl.ds(0, half), pl.ds(half, half)
+    loads = [pltpu.make_async_copy(part.at[j], mine.at[j], local.at[j]) for j in range(8)]
+    order = (7, 5, 6, 4, 3, 1, 2, 0)
+    for j in order:
+        loads[j].start()
+    waves = []
+    for w, base in enumerate((4, 0)):
+        waves.append(
+            {
+                "a": remote(
+                    mine.at[base + 3, top], in_half.at[w, 0], ss.at[w, 0], rs.at[w, 0], next_x
+                ),
+                "b": remote(
+                    mine.at[base + 3, low], in_half.at[w, 1], ss.at[w, 1], rs.at[w, 1], next_y
+                ),
+                "x": remote(mine.at[base + 1], in_x.at[w], ss.at[w, 2], rs.at[w, 2], next_x),
+                "y": remote(mine.at[base + 2], in_y.at[w], ss.at[w, 3], rs.at[w, 3], next_y),
+            }
+        )
+    across = remote(mine.at[4], in_z, ss.at[0, 4], rs.at[0, 4], next_z)
+    for w, base in enumerate((4, 0)):
+        loads[base + 3].wait()
+        waves[w]["a"].start()
+        waves[w]["b"].start()
+    for w, base in enumerate((4, 0)):
+        loads[base + 2].wait()
+        waves[w]["a"].wait_recv()
+        add_into(mine.at[base + 2, top], in_half.at[w, 0])
+        waves[w]["y"].start()
+        loads[base + 1].wait()
+        waves[w]["b"].wait_recv()
+        add_into(mine.at[base + 1, low], in_half.at[w, 1])
+        waves[w]["x"].start()
+        loads[base].wait()
+        if w == 0:
+            continue
+        waves[0]["x"].wait_recv()
+        waves[0]["y"].wait_recv()
+        add_into(mine.at[4], in_x.at[0], in_y.at[0])
+        across.start()
+    waves[1]["x"].wait_recv()
+    waves[1]["y"].wait_recv()
+    across.wait_recv()
+
+    @pl.loop(0, out.shape[0] // 16)
+    def _(i):
+        at = pl.ds(pl.multiple_of(i * 16, 16), 16)
+        out[at] = (
+            mine[0, at].astype(F32)
+            + in_x[1, at].astype(F32)
+            + in_y[1, at].astype(F32)
+            + in_z[at].astype(F32)
+        )
+
+    for wave in waves:
+        for copy in wave.values():
+            copy.wait_send()
+    across.wait_send()
+
+
+def scatter_tokens(part, collective_id):
+    rows, width = part.shape[0] // 8, part.shape[1]
+    dma = pltpu.SemaphoreType.DMA
+    return pl.pallas_call(
+        token_scatter_kernel,
+        out_shape=jax.ShapeDtypeStruct((rows, width), F32),
+        in_specs=[pl.BlockSpec(memory_space=pl.ANY)],
+        out_specs=pl.BlockSpec(memory_space=pltpu.VMEM),
+        scratch_shapes=[
+            pltpu.VMEM((8, rows, width), BF16),
+            pltpu.VMEM((2, 2, rows // 2, width), BF16),
+            pltpu.VMEM((2, rows, width), BF16),
+            pltpu.VMEM((2, rows, width), BF16),
+            pltpu.VMEM((rows, width), BF16),
+            dma((8,)),
+            dma((2, 5)),
+            dma((2, 5)),
+        ],
+        compiler_params=pltpu.CompilerParams(
+            collective_id=collective_id, has_side_effects=True, vmem_limit_bytes=40 * 2**20
+        ),
+        name="scatter_tokens",
+    )(part.reshape(8, rows, width))
 
 
 def passed_along(block, axis, distance):
@@ -139,11 +576,24 @@
     group_size = HQ // KVH
     query_width = HQ * HD
     kv_width = KVH * HD
-    qkv_all, out_all, side_all, gain_all = (
-        lax.all_gather(qkv_weight, "fsdp", axis=0, tiled=True),
-        lax.all_gather(out_weight, "fsdp", axis=0, tiled=True),
-        lax.all_gather(side_weights, "fsdp", axis=0, tiled=True),
-        lax.all_gather(norm_gains, "fsdp", axis=0, tiled=True),
+    count = lax.axis_size("fsdp")
+    bits = weight_bits(count)
+    held = ffn_weights.transpose(1, 0, 2)
+    for bit in bits:
+        held = jnp.concatenate([held, swapped(held, bit)], axis=1)
+    gate_w, up_w, down_w = held[0], held[1], held[2]
+    weight_rows = qkv_weight.shape[0]
+    gain_block = jnp.pad(norm_gains, (0, weight_rows * LANES - norm_gains.shape[0]))
+    qkv_gathered, out_gathered = gather_weights(
+        jnp.concatenate([qkv_weight, gain_block.reshape(weight_rows, LANES)], axis=1),
+        jnp.concatenate([out_weight, side_weights], axis=1),
+    )
+    qkv_all = qkv_gathered[:, : qkv_weight.shape[1]]
+    out_all, side_all = out_gathered[:, :D], out_gathered[:, D:]
+    gain_all = (
+        qkv_gathered[:, qkv_weight.shape[1] :]
+        .reshape(count, weight_rows * LANES)[:, : norm_gains.shape[0]]
+        .reshape(-1)
     )
     attn_gain, ffn_gain, query_gain, key_gain = split_gains(gain_all)
     tokens_f = tokens.astype(jnp.float32)
@@ -174,25 +624,13 @@
     first_sum = tokens_f + jnp.dot(mixed_b, out_all, preferred_element_type=jnp.float32)
     rms_two = inv_rms(first_sum)
     normed_two = (first_sum * rms_two * ffn_gain).astype(jnp.bfloat16)
-    count = lax.axis_size("fsdp")
-    by_token, by_weight = token_groups(count), weight_groups(count)
-    gate_w, up_w, down_w = (
-        lax.all_gather(
-            ffn_weights[:, i, :], "fsdp", axis=0, tiled=True, axis_index_groups=by_weight
-        )
-        for i in range(3)
-    )
-    normed_all = lax.all_gather(
-        normed_two, "fsdp", axis=0, tiled=True, axis_index_groups=by_token
-    )
+    normed_all = gather_tokens(normed_two, 2)
     gate_out = contract_cols(normed_all, gate_w)
     up_out = contract_cols(normed_all, up_w)
     gelu_gate, pull_gate = jax.vjp(gelu_tanh, gate_out)
     act_b = (gelu_gate * up_out).astype(jnp.bfloat16)
     ffn_part = jnp.dot(act_b, down_w, preferred_element_type=jnp.float32).astype(jnp.bfloat16)
-    ffn_out = lax.psum_scatter(
-        ffn_part, "fsdp", scatter_dimension=0, tiled=True, axis_index_groups=by_token
-    ).astype(jnp.float32)
+    ffn_out = scatter_tokens(ffn_part, 3)
     second_sum = first_sum + ffn_out
     second_b = second_sum.astype(jnp.bfloat16)
     side_in = jnp.dot(second_b, side_all[:, :split_at], preferred_element_type=jnp.float32)
@@ -213,38 +651,27 @@
     side_grad_full = jnp.concatenate([side_in_grad, side_out_grad], axis=1)
     grad_two = grad_y + contract_cols(grad_side, back_side[:, :split_at])
     grad_two_b = grad_two.astype(jnp.bfloat16)
-    grad_two_all = lax.all_gather(
-        grad_two_b, "fsdp", axis=0, tiled=True, axis_index_groups=by_token
-    )
+    grad_two_all = gather_tokens(grad_two_b, 4)
     grad_act_b = contract_cols(grad_two_all, down_w).astype(jnp.bfloat16)
     grad_gate_b = pull_gate(grad_act_b * up_out)[0].astype(jnp.bfloat16)
     grad_up_b = (grad_act_b * gelu_gate).astype(jnp.bfloat16)
     grad_h2 = jnp.dot(grad_gate_b, gate_w, preferred_element_type=jnp.float32)
     grad_h2 = grad_h2 + jnp.dot(grad_up_b, up_w, preferred_element_type=jnp.float32)
-    grad_h2 = lax.psum_scatter(
-        grad_h2.astype(jnp.bfloat16),
-        "fsdp",
-        scatter_dimension=0,
-        tiled=True,
-        axis_index_groups=by_token,
-    ).astype(jnp.float32)
-    ffn_grad = jnp.stack(
-        [
-            lax.psum_scatter(
-                contract_rows(left, right).astype(jnp.bfloat16),
-                "fsdp",
-                scatter_dimension=0,
-                tiled=True,
-                axis_index_groups=by_weight,
-            ).astype(jnp.float32)
-            for left, right in (
-                (grad_gate_b, normed_all),
-                (grad_up_b, normed_all),
-                (act_b, grad_two_all),
+    grad_h2 = scatter_tokens(grad_h2.astype(BF16), 5)
+    ffn_parts = []
+    for left, right in (
+        (grad_gate_b, normed_all),
+        (grad_up_b, normed_all),
+        (act_b, grad_two_all),
+    ):
+        part = contract_rows(left, right).astype(BF16)
+        for bit in reversed(bits):
+            half = part.shape[0] // 2
+            part = (part[:half].astype(F32) + swapped(part[half:], bit).astype(F32)).astype(
+                F32 if bit == bits[0] else BF16
             )
-        ],
-        axis=1,
-    )
+        ffn_parts.append(part)
+    ffn_grad = jnp.stack(ffn_parts, axis=1)
     ffn_gain_grad = jnp.sum(grad_h2 * first_sum * rms_two, axis=0)
     grad_one = grad_two + norm_back(grad_h2, first_sum, rms_two, ffn_gain)
     grad_one_b = grad_one.astype(jnp.bfloat16)
@@ -308,13 +735,17 @@
     gains_grad_full = jnp.concatenate(
         [attn_gain_grad, ffn_gain_grad, query_gain_grad, key_gain_grad]
     )
-    qkv_grad, out_grad, side_grad = (
-        lax.psum_scatter(
-            full.astype(jnp.bfloat16), "fsdp", scatter_dimension=0, tiled=True
-        ).astype(jnp.float32)
-        for full in (qkv_grad_full, out_grad_full, side_grad_full)
-    )
-    gains_grad = lax.psum_scatter(gains_grad_full, "fsdp", scatter_dimension=0, tiled=True)
+    gain_rows = jnp.pad(
+        gains_grad_full.astype(BF16).reshape(count, -1),
+        ((0, 0), (0, weight_rows * LANES - norm_gains.shape[0])),
+    ).reshape(count * weight_rows, LANES)
+    qkv_sum, out_sum = scatter_weights(
+        jnp.concatenate([qkv_grad_full.astype(BF16), gain_rows], axis=1),
+        jnp.concatenate([out_grad_full.astype(BF16), side_grad_full.astype(BF16)], axis=1),
+    )
+    qkv_grad = qkv_sum[:, : qkv_weight.shape[1]]
+    gains_grad = qkv_sum[:, qkv_weight.shape[1] :].reshape(-1)[: norm_gains.shape[0]]
+    out_grad, side_grad = out_sum[:, :D], out_sum[:, D:]
     return (output, input_grad, per_layer_grad, qkv_grad, out_grad, ffn_grad, side_grad, gains_grad)
 
 

time: 1520 us -> 1120 us (0.74)
  waiting for transfers between devices: 1040 us -> 71.6 us
  Pallas kernels: 0 us -> 635 us
  blocking collectives: 86.4 us -> 0 us
  other arithmetic: 50.8 us -> 82.6 us
  matrix products: 241 us -> 218 us
  local copies, waits for them, and re-layouts: 63.1 us -> 79.8 us
    pallas_call x0 -> x6, Pallas kernels: none -> 635 us  [the longest x2 176 us: gather_tokens(): pl.pallas_call(token_gather_kernel, out_shape=jax.ShapeDtypeStruct((8,) +...]
    reduce_scatter x7 -> x0, waiting for transfers between devices: 561 us -> none  [the longest x2 246 us: local(): lax.psum_scatter(full.astype(jnp.bfloat16), 'fsdp', scatter_dimension=0,...]
    all_gather x8 -> x0, waiting for transfers between devices: 430 us -> none  [the longest x3 199 us: local(): lax.all_gather(ffn_weights[:, i, :], 'fsdp', axis=0, tiled=True, axis_ind...]
    unnamed x2 -> x0, blocking collectives: 86.4 us -> none
    ppermute x0 -> x8, waiting for transfers between devices: none -> 62.1 us  [swapped(): return lax.ppermute(block, 'fsdp', route)]
    unnamed x17 -> x0, waiting for transfers between devices: 49.9 us -> none
    concatenate x1 -> x6, other arithmetic: 1.82 us -> 41 us  [the longest x1 15.2 us: local(): jnp.concatenate([out_grad_full.astype(BF16), side_grad_full.astype(BF16)]...]
    unnamed x150 -> x196, local copies, waits for them, and re-layouts: 32.8 us -> 22.6 us
  transfers between devices with their start and end apart: 24 -> 16, of which waited for: 16 -> 4; matrix products, arithmetic and copies ran while one was open for 18% -> 17% of each run, Pallas kernels for 0% -> 34%
where the time goes in v2:
time: 1120 us; the launch traced here: 1110 us
  Pallas kernels  635 us (57%)
  matrix products  218 us (19%)
  other arithmetic  82.6 us (7%)
  local copies, waits for them, and re-layouts  79.8 us (7%)
  waiting for transfers between devices  71.6 us (6%)
  starting transfers between devices  23.2 us (2%)
    pallas_call x2, Pallas kernels, gather_tokens(): pl.pallas_call(token_gather_kernel, out_shape=jax.ShapeDtypeStruct((8,) +...  176 us
    pallas_call x2, Pallas kernels, scatter_tokens(): pl.pallas_call(token_scatter_kernel, out_shape=jax.ShapeDtypeStruct((rows...  173 us
    pallas_call x1, Pallas kernels, gather_weights(): pl.pallas_call(functools.partial(gather_kernel, chain), out_shape=outs, i...  171 us
    pallas_call x1, Pallas kernels, scatter_weights(): pl.pallas_call(functools.partial(scatter_kernel, chain), out_shape=outs,...  115 us
    dot_general x7, matrix products, contract_cols(): lax.dot_general(left_op, right_op, (((1,), (1,)), ((), ())), preferred_el...  71.3 us
    ppermute x8, waiting for transfers between devices, swapped(): return lax.ppermute(block, 'fsdp', route)  62.1 us
    dot_general x7, matrix products, contract_rows(): lax.dot_general(left_op, right_op, (((0,), (0,)), ((), ())), preferred_el...  61.8 us
    unnamed x196, local copies, waits for them, and re-layouts  22.6 us
  transfers between devices with their start and end apart: 16, of which 4 were waited for; matrix products, arithmetic and copies ran while one was open for 17% of the time, Pallas kernels for 34%

profile of v2, /device:TPU:0, one launch (start us, length us, event | category | flops | bytes accessed | tf_op | source)
XLA Modules:
  0.0 1112.8 jit_solution(15648408916758050507)
XLA Ops:
  0.6 3.1 collective-permute-start.4
  7.9 171.4 %gather_weights.1 = (bf16[4,2,2,2,64,3200]{5,4,3,2,1,0:T(8,128)(2,1)}, bf16[4,2,2,2,64,2688]{5,4,3,2,1,0:T(8,128)(2,1)}) custom-call(bf16[64,3200]{1,0:T(8,128)(2,1)} %pad_maximum_fusion.9.own_a, bf16[64,2688]{1,0:T(8,128)(2,1)} %pad_maximum_fusion.10.own_b), custom_call_target="tpu_custom_call" | custom-call | bytes 385875968 | tf_op jit(solution)/shard_map/gather_weights/pallas_call | solution.py:161
  181.7 6.5 fusion.3
  193.7 6.6 pad_maximum_fusion.3
  202.6 3.4 collective-permute-start.2
  205.9 2.5 collective-permute-start.3
  210.3 2.8 collective-permute-start
  213.1 3.0 collective-permute-start.1
  216.1 3.1 slice.226
  219.2 2.5 copy.244
  225.0 3.1 copy.232
  232.6 2.7 copy.194
  235.3 2.5 copy.195
  240.6 3.5 fusion.63
  244.2 2.2 fusion.45
  249.9 2.3 copy.245
  252.6 2.4 copy.249
  255.1 2.2 copy.246
  258.2 5.9 fusion.126
  264.2 4.0 fusion.51
  268.2 6.2 multiply_reduce_fusion.4
  277.0 93.8 %gather_tokens.2 = bf16[8,256,2048]{2,1,0:T(8,128)(2,1)} custom-call(bf16[256,2048]{1,0:T(8,128)(2,1)} %multiply_convert_fusion.1.own), custom_call_target="tpu_custom_call" | custom-call | tf_op jit(solution)/shard_map/gather_tokens/pallas_call | solution.py:367
  370.9 5.8 pad_maximum_fusion.1
  377.1 11.2 %fusion.21 = f32[2048,1024]{1,0:T(8,128)} fusion(bf16[2048,2048]{1,0:T(8,128)(2,1)S(1)} %bitcast.204, bf16[3,1024,2048]{2,1,0:T(8,128)(2,1)S(1)} %pad_maximum_fusion.1), kind=kOutput, calls=%fused_computation.56 | convolution fusion | flops 8589934592 | bytes 20971520 | tf_op jit(solution)/shard_map/dot_general | solution.py:529
  388.3 17.3 %multiply_convert_fusion = (bf16[2048,1024]{1,0:T(8,128)(2,1)}, f32[2048,1024]{1,0:T(8,128)}) fusion(f32[2048,1024]{1,0:T(8,128)} %fusion.21, bf16[2048,2048]{1,0:T(8,128)(2,1)} %bitcast.202, bf16[3,1024,2048]{2,1,0:T(8,128)(2,1)S(1)} %pad_maximum_fusion.1), kind=kOutput, calls=%fused_computation.22 | convolution fusion | flops 8610906112 | bytes 33554432 | tf_op jit(solution)/shard_map/dot_general | solution.py:529
  405.6 10.7 convolution_convert_fusion.2
  416.3 90.6 %scatter_tokens.2 = f32[256,2048]{1,0:T(8,128)S(1)} custom-call(bf16[8,256,2048]{2,1,0:T(8,128)(2,1)S(1)} %bitcast.184), custom_call_target="tpu_custom_call" | custom-call | tf_op jit(solution)/shard_map/scatter_tokens/pallas_call | solution.py:446
  507.2 2.3 fusion.61
  510.5 3.8 fusion.127
  515.9 82.1 %gather_tokens.3 = bf16[8,256,2048]{2,1,0:T(8,128)(2,1)} custom-call(bf16[256,2048]{1,0:T(8,128)(2,1)} %get-tuple-element.112.own), custom_call_target="tpu_custom_call" | custom-call | tf_op jit(solution)/shard_map/gather_tokens/pallas_call | solution.py:367
  598.0 14.0 %convolution_convert_fusion.3 = bf16[1024,2048]{1,0:T(8,128)(2,1)} fusion(bf16[2048,1024]{1,0:T(8,128)(2,1)} %get-tuple-element.110, bf16[2048,2048]{1,0:T(8,128)(2,1)} %bitcast.208), kind=kOutput, calls=%fused_computation.52 | convolution fusion | flops 8592031744 | bytes 16777216 | tf_op jit(solution)/shard_map/dot_general | solution.py:523
  612.1 23.7 %fusion.12 = (bf16[2048,1024]{1,0:T(8,128)(2,1)S(1)}, bf16[2048,1024]{1,0:T(8,128)(2,1)}) fusion(f32[2048,1024]{1,0:T(8,128)} %fusion.21, f32[2048,1024]{1,0:T(8,128)} %get-tuple-element.111, bf16[2048,2048]{1,0:T(8,128)(2,1)} %bitcast.209, bf16[3,1024,2048]{2,1,0:T(8,128)(2,1)} %copy-done.9), kind=kOutput, calls=%fused_computation.21 | convolution fusion | flops 8638169088 | bytes 37748736 | tf_op jit(solution)/shard_map/dot_general | solution.py:529
  635.8 19.6 %convolution_convert_fusion.4 = bf16[1024,2048]{1,0:T(8,128)(2,1)} fusion(bf16[2048,2048]{1,0:T(8,128)(2,1)} %bitcast.203, bf16[2048,1024]{1,0:T(8,128)(2,1)} %get-tuple-element.115, f32[2048,1024]{1,0:T(8,128)} %fusion.21), kind=kOutput, calls=%fused_computation.53 | convolution fusion | flops 8615100416 | bytes 25165824 | tf_op jit(solution)/shard_map/dot_general | solution.py:523
  655.4 17.6 %fusion.22 = f32[2048,2048]{1,0:T(8,128)} fusion(bf16[3,1024,2048]{2,1,0:T(8,128)(2,1)} %copy-done.9, bf16[2048,1024]{1,0:T(8,128)(2,1)} %get-tuple-element.115, f32[2048,1024]{1,0:T(8,128)} %fusion.21), kind=kOutput, calls=%fused_computation.57 | convolution fusion | flops 8613003264 | bytes 33554432 | tf_op jit(solution)/shard_map/dot_general | solution.py:659
  673.0 11.5 %convolution_convert_fusion.5 = bf16[1024,2048]{1,0:T(8,128)(2,1)} fusion(bf16[2048,1024]{1,0:T(8,128)(2,1)S(1)} %get-tuple-element.114, bf16[2048,2048]{1,0:T(8,128)(2,1)S(1)} %bitcast.207), kind=kOutput, calls=%fused_computation.54 | convolution fusion | flops 8592031744 | bytes 16777216 | tf_op jit(solution)/shard_map/dot_general | solution.py:523
  684.6 14.3 %add_convert_fusion = bf16[2048,2048]{1,0:T(8,128)(2,1)S(1)} fusion(f32[2048,2048]{1,0:T(8,128)} %fusion.22, bf16[2048,1024]{1,0:T(8,128)(2,1)} %copy-done.84, bf16[3,1024,2048]{2,1,0:T(8,128)(2,1)} %copy-done.9), kind=kOutput, calls=%fused_computation.1 | convolution fusion | flops 8598323200 | bytes 33554432 | tf_op jit(solution)/shard_map/dot_general | solution.py:658
  698.9 82.2 %scatter_tokens.3 = f32[256,2048]{1,0:T(8,128)S(1)} custom-call(bf16[8,256,2048]{2,1,0:T(8,128)(2,1)S(1)} %bitcast.183), custom_call_target="tpu_custom_call" | custom-call | tf_op jit(solution)/shard_map/scatter_tokens/pallas_call | solution.py:446
  783.3 6.3 convolution_convert_fusion.1
  790.0 3.3 fusion.30
  795.0 2.1 fusion.29
  804.0 5.7 fusion.128
  809.7 2.3 fusion.17
  813.4 2.2 fusion.129
  815.6 3.5 convolution_multiply_fusion
  819.1 2.2 copy.205
  826.6 2.2 copy.247
  828.8 3.0 copy.237
  835.5 15.2 %pad_maximum_fusion.2 = bf16[2048,2688]{0,1:T(8,128)(2,1)} fusion(bf16[2048,320]{0,1:T(8,128)(2,1)} %fusion.33, bf16[2048,320]{0,1:T(8,128)(2,1)} %convolution_convert_fusion.7, bf16[2048,2048]{0,1:T(8,128)(2,1)} %convolution_convert_fusion.1), kind=kLoop, calls=%fused_computation.11 | loop fusion | flops 33030144 | bytes 22020096 | tf_op jit(solution)/shard_map/concatenate | solution.py:744
  850.7 2.8 multiply_reduce_fusion
  853.5 13.9 %copy.219 = bf16[2048,2688]{1,0:T(8,128)(2,1)} copy(bf16[2048,2688]{0,1:T(8,128)(2,1)} %pad_maximum_fusion.2) | data formatting | bytes 22020096 | tf_op jit(solution)/shard_map/concatenate | solution.py:744
  874.2 9.5 collective-permute-done.9
  885.0 7.1 convolution_convert_fusion
  892.2 9.7 fusion.43
  902.1 9.9 pad_maximum_fusion.part_a
  912.0 115.1 %scatter_weights.1 = (f32[64,3200]{1,0:T(8,128)}, f32[64,2688]{1,0:T(8,128)}) custom-call(bf16[4,2,2,2,64,3200]{5,4,3,2,1,0:T(8,128)(2,1)} %pad_maximum_fusion.part_a, bf16[4,2,2,2,64,2688]{5,4,3,2,1,0:T(8,128)(2,1)} %bitcast.186), custom_call_target="tpu_custom_call" | custom-call | tf_op jit(solution)/shard_map/scatter_weights/pallas_call | solution.py:319
  1028.0 2.1 slice.200
  1030.1 2.0 slice.201
  1035.9 2.5 add_convert_fusion.3
  1038.7 2.5 add_convert_fusion.2
  1043.2 2.4 add_convert_fusion.1
  1046.0 18.6 %collective-permute-done.11 = bf16[256,2048]{1,0:T(8,128)(2,1)S(1)} collective-permute-done((bf16[256,2048]{1,0:T(8,128)(2,1)S(1)}, bf16[256,2048]{1,0:T(8,128)(2,1)S(1)}, u32[]{:S(2)}, u32[]{:S(2)}) %collective-permute-start.11) | collective-permute-done | bytes 1048608 | tf_op jit(solution)/shard_map/ppermute | solution.py:37
  1065.0 22.1 %collective-permute-done.13 = bf16[256,2048]{1,0:T(8,128)(2,1)S(1)} collective-permute-done((bf16[256,2048]{1,0:T(8,128)(2,1)S(1)}, bf16[256,2048]{1,0:T(8,128)(2,1)S(1)}, u32[]{:S(2)}, u32[]{:S(2)}) %collective-permute-start.13) | collective-permute-done | bytes 1048608 | tf_op jit(solution)/shard_map/ppermute | solution.py:37
  1087.5 21.3 %collective-permute-done.15 = bf16[256,2048]{1,0:T(8,128)(2,1)S(1)} collective-permute-done((bf16[256,2048]{1,0:T(8,128)(2,1)S(1)}, bf16[256,2048]{1,0:T(8,128)(2,1)S(1)}, u32[]{:S(2)}, u32[]{:S(2)}) %collective-permute-start.15) | collective-permute-done | bytes 1048608 | tf_op jit(solution)/shard_map/ppermute | solution.py:37
  1109.1 3.1 pad_maximum_fusion.4
  (313 shorter events, 74.9 us)
Async XLA Ops:
  0.6 180.1 %copy-start.11 = (bf16[256,2048]{1,0:T(8,128)(2,1)S(1)}, bf16[256,2048]{1,0:T(8,128)(2,1)}, u32[]{:S(2)}) copy-start(bf16[256,2048]{1,0:T(8,128)(2,1)} %param.10) | copy-start | bytes 3145732
  0.6 193.1 %collective-permute-start.4 = (bf16[3,256,2048]{2,1,0:T(8,128)(2,1)}, bf16[3,256,2048]{2,1,0:T(8,128)(2,1)}, u32[]{:S(2)}, u32[]{:S(2)}) collective-permute-start(bf16[3,256,2048]{2,1,0:T(8,128)(2,1)} %bitcast.193), channel_id=1, source_target_pairs={{0,8},{1,9},{2,10},{3,11},{4,12},{5,13},{6,14},{7,15},{8,0},{9,1},... | collective-permute-start | bytes 9437192 | tf_op jit(solution)/shard_map/ppermute | solution.py:37
  180.8 7.4 copy-start.55
  180.8 94.3 %copy-start.57 = (f32[2048]{0:T(1024)}, f32[2048]{0:T(1024)S(1)}, u32[]{:S(2)}) copy-start(f32[2048]{0:T(1024)S(1)} %get-tuple-element.94) | copy-start | bytes 24580
  181.7 6.5 copy-start.68
  181.7 9.0 copy-start.82
  181.7 9.0 copy-start.83
  189.9 11.8 %copy-start.7 = (f32[256,512]{1,0:T(8,128)}, f32[256,512]{1,0:T(8,128)S(1)}, u32[]{:S(2)}) copy-start(f32[256,512]{1,0:T(8,128)S(1)} %slice.222) | copy-start | bytes 1572868
  190.7 9.6 copy-start.73
  192.9 8.8 copy-start.66
  193.4 8.3 copy-start.59
  200.3 170.5 %collective-permute-start.5 = (bf16[3,512,2048]{2,1,0:T(8,128)(2,1)}, bf16[3,512,2048]{2,1,0:T(8,128)(2,1)}, u32[]{:S(2)}, u32[]{:S(2)}) collective-permute-start(bf16[3,512,2048]{2,1,0:T(8,128)(2,1)} %pad_maximum_fusion.3), channel_id=1, source_target_pairs={{0,1},{1,0},{2,3},{3,2},{4,5},{5,4},{6,7},{7,6},{8,9},{9,8},{10,11... | collective-permute-start | bytes 18874376 | tf_op jit(solution)/shard_map/ppermute | solution.py:37
  201.7 17.6 %copy-start.26 = (f32[256,256]{1,0:T(8,128)}, f32[256,256]{1,0:T(8,128)S(1)}, u32[]{:S(2)}) copy-start(f32[256,256]{1,0:T(8,128)S(1)} %get-tuple-element.93) | copy-start | bytes 786436
  201.7 53.3 %copy-start.13 = (f32[256,256]{1,0:T(8,128)}, f32[256,256]{1,0:T(8,128)S(1)}, u32[]{:S(2)}) copy-start(f32[256,256]{1,0:T(8,128)S(1)} %get-tuple-element.92) | copy-start | bytes 786436
  202.6 55.6 %collective-permute-start.2 = (bf16[256,2,256]{2,0,1:T(8,128)(2,1)}, bf16[256,2,256]{2,0,1:T(8,128)(2,1)}, u32[]{:S(2)}, u32[]{:S(2)}) collective-permute-start(bf16[256,2,256]{2,0,1:T(8,128)(2,1)} %fusion.79), channel_id=1, source_target_pairs={{0,2},{1,3},{2,4},{3,5},{4,6},{5,7},{6,8},{7,9},{8,10},{9,11},{10,... | collective-permute-start | bytes 786440 | tf_op jit(solution)/shard_map/ppermute | solution.py:471
  205.9 52.3 %collective-permute-start.3 = (bf16[256,2,256]{2,0,1:T(8,128)(2,1)}, bf16[256,2,256]{2,0,1:T(8,128)(2,1)}, u32[]{:S(2)}, u32[]{:S(2)}) collective-permute-start(bf16[256,2,256]{2,0,1:T(8,128)(2,1)} %fusion.79), channel_id=1, source_target_pairs={{0,1},{1,2},{2,3},{3,4},{4,5},{5,6},{6,7},{7,8},{8,9},{9,10},{10,1... | collective-permute-start | bytes 786440 | tf_op jit(solution)/shard_map/ppermute | solution.py:471
  210.3 53.8 %collective-permute-start = (bf16[256,2,256]{0,2,1:T(8,128)(2,1)}, bf16[256,2,256]{0,2,1:T(8,128)(2,1)}, u32[]{:S(2)}, u32[]{:S(2)}) collective-permute-start(bf16[256,2,256]{0,2,1:T(8,128)(2,1)} %bitcast.44), channel_id=1, source_target_pairs={{0,2},{1,3},{2,4},{3,5},{4,6},{5,7},{6,8},{7,9},{8,10},{9,11},{10,... | collective-permute-start | bytes 786440 | tf_op jit(solution)/shard_map/ppermute | solution.py:471
  213.1 51.0 %collective-permute-start.1 = (bf16[256,2,256]{0,2,1:T(8,128)(2,1)}, bf16[256,2,256]{0,2,1:T(8,128)(2,1)}, u32[]{:S(2)}, u32[]{:S(2)}) collective-permute-start(bf16[256,2,256]{0,2,1:T(8,128)(2,1)} %bitcast.44), channel_id=1, source_target_pairs={{0,1},{1,2},{2,3},{3,4},{4,5},{5,6},{6,7},{7,8},{8,9},{9,10},{10,1... | collective-permute-start | bytes 786440 | tf_op jit(solution)/shard_map/ppermute | solution.py:471
  221.7 9.4 copy-start
  232.6 11.6 %copy-start.23 = (f32[256,2048]{0,1:T(8,128)S(1)}, f32[256,2048]{0,1:T(8,128)}, u32[]{:S(2)}) copy-start(f32[256,2048]{0,1:T(8,128)} %copy.232) | copy-start | bytes 6291460
  237.8 6.4 copy-start.37
  237.8 6.4 copy-start.38
  237.8 6.4 copy-start.46
  237.8 6.4 copy-start.47
  277.0 93.9 %copy-start.10 = (bf16[256,3,2048]{2,0,1:T(8,128)(2,1)S(1)}, bf16[256,3,2048]{2,0,1:T(8,128)(2,1)}, u32[]{:S(2)}) copy-start(bf16[256,3,2048]{2,0,1:T(8,128)(2,1)} %param.17) | copy-start | bytes 9437188
  376.7 28.9 %copy-start.9 = (bf16[3,1024,2048]{2,1,0:T(8,128)(2,1)}, bf16[3,1024,2048]{2,1,0:T(8,128)(2,1)S(1)}, u32[]{:S(2)}) copy-start(bf16[3,1024,2048]{2,1,0:T(8,128)(2,1)S(1)} %pad_maximum_fusion.1) | copy-start | bytes 37748740
  416.3 90.6 %copy-start.3 = (f32[256,2048]{1,0:T(8,128)S(1)}, f32[256,2048]{1,0:T(8,128)}, u32[]{:S(2)}) copy-start(f32[256,2048]{1,0:T(8,128)} %copy-done.2) | copy-start | bytes 6291460
  635.8 37.2 %copy-start.84 = (bf16[2048,1024]{1,0:T(8,128)(2,1)}, bf16[2048,1024]{1,0:T(8,128)(2,1)S(1)}, u32[]{:S(2)}) copy-start(bf16[2048,1024]{1,0:T(8,128)(2,1)S(1)} %get-tuple-element.114) | copy-start | bytes 12582916
  635.8 37.2 %slice-start = ((s8[8388608]{0:T(1024)(128)(4,1)}), s8[4194304]{0:T(1024)(128)(4,1)S(1)}, s32[]{:S(2)}) async-start(s8[8388608]{0:T(1024)(128)(4,1)} %bitcast.205), calls=%async_computation | async-start | bytes 8388608
  655.4 17.6 %slice-start.1 = ((s8[8388608]{0:T(1024)(128)(4,1)}), s8[4194304]{0:T(1024)(128)(4,1)S(1)}, s32[]{:S(2)}) async-start(s8[8388608]{0:T(1024)(128)(4,1)} %bitcast.205), calls=%async_computation.1 | async-start | bytes 8388608
  698.9 82.2 %copy-start.4 = (f32[256,2048]{1,0:T(8,128)S(1)}, f32[256,2048]{1,0:T(8,128)}, u32[]{:S(2)}) copy-start(f32[256,2048]{1,0:T(8,128)} %copy-done.2) | copy-start | bytes 6291460
  698.9 82.2 %copy-start.58 = (f32[2048]{0:T(1024)S(1)}, f32[2048]{0:T(1024)}, u32[]{:S(2)}) copy-start(f32[2048]{0:T(1024)} %copy-done.57) | copy-start | bytes 24580
  698.9 82.2 %copy-start.71 = (f32[256]{0:T(256)S(1)}, f32[256]{0:T(256)}, u32[]{:S(2)}) copy-start(f32[256]{0:T(256)} %copy-done.70) | copy-start | bytes 3076
  782.7 6.9 slice-start.4
  782.7 6.9 slice-start.5
  783.3 6.7 slice-start.6
  798.6 237.3 %collective-permute-start.10 = (bf16[512,2048]{1,0:T(8,128)(2,1)}, bf16[512,2048]{1,0:T(8,128)(2,1)}, u32[]{:S(2)}, u32[]{:S(2)}) collective-permute-start(bf16[512,2048]{1,0:T(8,128)(2,1)} %slice.252), channel_id=1, source_target_pairs={{0,1},{1,0},{2,3},{3,2},{4,5},{5,4},{6,7},{7,6},{8,9},{9,8},{10,11... | collective-permute-start | bytes 6291464 | tf_op jit(solution)/shard_map/ppermute | solution.py:37
  800.1 238.6 %collective-permute-start.12 = (bf16[512,2048]{1,0:T(8,128)(2,1)}, bf16[512,2048]{1,0:T(8,128)(2,1)}, u32[]{:S(2)}, u32[]{:S(2)}) collective-permute-start(bf16[512,2048]{1,0:T(8,128)(2,1)} %slice.256), channel_id=1, source_target_pairs={{0,1},{1,0},{2,3},{3,2},{4,5},{5,4},{6,7},{7,6},{8,9},{9,8},{10,11... | collective-permute-start | bytes 6291464 | tf_op jit(solution)/shard_map/ppermute | solution.py:37
  801.0 8.7 slice-start.2
  802.5 240.8 %collective-permute-start.14 = (bf16[512,2048]{1,0:T(8,128)(2,1)}, bf16[512,2048]{1,0:T(8,128)(2,1)}, u32[]{:S(2)}, u32[]{:S(2)}) collective-permute-start(bf16[512,2048]{1,0:T(8,128)(2,1)} %slice.260), channel_id=1, source_target_pairs={{0,1},{1,0},{2,3},{3,2},{4,5},{5,4},{6,7},{7,6},{8,9},{9,8},{10,11... | collective-permute-start | bytes 6291464 | tf_op jit(solution)/shard_map/ppermute | solution.py:37
  832.6 35.7 %collective-permute-start.6 = (bf16[256,2,256]{2,0,1:T(8,128)(2,1)}, bf16[256,2,256]{2,0,1:T(8,128)(2,1)S(1)}, u32[]{:S(2)}, u32[]{:S(2)}) collective-permute-start(bf16[256,2,256]{2,0,1:T(8,128)(2,1)} %get-tuple-element.81), channel_id=1, source_target_pairs={{1,0},{2,1},{3,2},{4,3},{5,4},{6,5},{7,6},{8,7},{9,8},{10,9},{11,1... | collective-permute-start | bytes 786440 | tf_op jit(solution)/shard_map/ppermute | solution.py:471
  833.9 16.8 %copy-start.15 = (f32[32,8,8,256]{3,1,2,0:T(8,128)S(1)}, f32[32,8,8,256]{3,1,2,0:T(8,128)}, u32[]{:S(2)}) copy-start(f32[32,8,8,256]{3,1,2,0:T(8,128)} %copy.245) | copy-start | bytes 6291460
  833.9 16.8 %copy-start.16 = (f32[32,8,8,256]{3,1,2,0:T(8,128)S(1)}, f32[32,8,8,256]{3,1,2,0:T(8,128)}, u32[]{:S(2)}) copy-start(f32[32,8,8,256]{3,1,2,0:T(8,128)} %copy.249) | copy-start | bytes 6291460
  833.9 16.8 %copy-start.17 = (f32[32,8,8,256]{3,1,2,0:T(8,128)S(1)}, f32[32,8,8,256]{3,1,2,0:T(8,128)}, u32[]{:S(2)}) copy-start(f32[32,8,8,256]{3,1,2,0:T(8,128)} %copy.246) | copy-start | bytes 6291460
  833.9 16.8 %copy-start.18 = (f32[32,8,8,256]{3,1,2,0:T(8,128)S(1)}, f32[32,8,8,256]{3,1,2,0:T(8,128)}, u32[]{:S(2)}) copy-start(f32[32,8,8,256]{3,1,2,0:T(8,128)} %copy.247) | copy-start | bytes 6291460
  833.9 16.8 %copy-start.19 = (f32[256,2048]{1,0:T(8,128)S(1)}, f32[256,2048]{1,0:T(8,128)}, u32[]{:S(2)}) copy-start(f32[256,2048]{1,0:T(8,128)} %copy.237) | copy-start | bytes 6291460
  833.9 16.8 %copy-start.25 = (f32[256,3072]{1,0:T(8,128)S(1)}, f32[256,3072]{1,0:T(8,128)}, u32[]{:S(2)}) copy-start(f32[256,3072]{1,0:T(8,128)} %copy-done.24) | copy-start | bytes 9437188
  833.9 16.8 %copy-start.61 = (f32[1,2,8,128]{3,1,2,0:T(2,128)S(1)}, f32[1,2,8,128]{3,1,2,0:T(2,128)}, u32[]{:S(2)}) copy-start(f32[1,2,8,128]{3,1,2,0:T(2,128)} %copy.248) | copy-start | bytes 24580
  833.9 35.7 %collective-permute-start.7 = (bf16[256,2,256]{2,0,1:T(8,128)(2,1)}, bf16[256,2,256]{2,0,1:T(8,128)(2,1)S(1)}, u32[]{:S(2)}, u32[]{:S(2)}) collective-permute-start(bf16[256,2,256]{2,0,1:T(8,128)(2,1)} %get-tuple-element.82), channel_id=1, source_target_pairs={{2,0},{3,1},{4,2},{5,3},{6,4},{7,5},{8,6},{9,7},{10,8},{11,9},{12,... | collective-permute-start | bytes 786440 | tf_op jit(solution)/shard_map/ppermute | solution.py:471
  853.5 13.9 %copy-start.50 = (bf16[256,256]{0,1:T(8,128)(2,1)S(1)}, bf16[256,256]{0,1:T(8,128)(2,1)}, u32[]{:S(2)}) copy-start(bf16[256,256]{0,1:T(8,128)(2,1)} %get-tuple-element.85) | copy-start | bytes 393220
  853.5 14.7 %copy-start.52 = (bf16[768,2,256]{0,2,1:T(8,128)(2,1)S(1)}, bf16[768,2,256]{0,2,1:T(8,128)(2,1)}, u32[]{:S(2)}) copy-start(bf16[768,2,256]{0,2,1:T(8,128)(2,1)} %get-tuple-element.116) | copy-start | bytes 2359300
  867.4 6.4 copy-start.77
  868.3 5.9 collective-permute-start.8
  869.6 14.1 %collective-permute-start.9 = (bf16[256,2,256]{0,2,1:T(8,128)(2,1)S(1)}, bf16[256,2,256]{0,2,1:T(8,128)(2,1)S(1)}, u32[]{:S(2)}, u32[]{:S(2)}) collective-permute-start(bf16[256,2,256]{0,2,1:T(8,128)(2,1)S(1)} %get-tuple-element.84), channel_id=1, source_target_pairs={{2,0},{3,1},{4,2},{5,3},{6,4},{7,5},{8,6},{9,7},{10,8},{11,9},{12,... | collective-permute-start | bytes 786440 | tf_op jit(solution)/shard_map/ppermute | solution.py:471
  872.1 12.9 %copy-start.12 = (bf16[256,2048]{1,0:T(8,128)(2,1)S(1)}, bf16[256,2048]{1,0:T(8,128)(2,1)}, u32[]{:S(2)}) copy-start(bf16[256,2048]{1,0:T(8,128)(2,1)} %param.10) | copy-start | bytes 3145732
  872.1 12.9 %copy-start.30 = (bf16[256,2048]{1,0:T(8,128)(2,1)S(1)}, bf16[256,2048]{1,0:T(8,128)(2,1)}, u32[]{:S(2)}) copy-start(bf16[256,2048]{1,0:T(8,128)(2,1)} %get-tuple-element.74) | copy-start | bytes 3145732
  872.1 12.9 %copy-start.56 = (f32[2048]{0:T(1024)S(1)}, f32[2048]{0:T(1024)}, u32[]{:S(2)}) copy-start(f32[2048]{0:T(1024)} %copy-done.55) | copy-start | bytes 24580
  872.1 12.9 %copy-start.69 = (f32[256]{0:T(256)S(1)}, f32[256]{0:T(256)}, u32[]{:S(2)}) copy-start(f32[256]{0:T(256)} %copy-done.68) | copy-start | bytes 3076
  912.0 122.3 %copy-start.41 = (f32[256,2048]{1,0:T(8,128)S(1)}, f32[256,2048]{1,0:T(8,128)}, u32[]{:S(2)}) copy-start(f32[256,2048]{1,0:T(8,128)} %get-tuple-element.122) | copy-start | bytes 6291460
  912.0 122.3 %copy-start.78 = (f32[256]{0:T(256)S(1)}, f32[256]{0:T(256)}, u32[]{:S(2)}) copy-start(f32[256]{0:T(256)} %get-tuple-element.102) | copy-start | bytes 3076
  1027.1 7.2 copy-start.6
  1038.6 26.1 %collective-permute-start.11 = (bf16[256,2048]{1,0:T(8,128)(2,1)S(1)}, bf16[256,2048]{1,0:T(8,128)(2,1)S(1)}, u32[]{:S(2)}, u32[]{:S(2)}) collective-permute-start(bf16[256,2048]{1,0:T(8,128)(2,1)S(1)} %slice.254), channel_id=1, source_target_pairs={{0,8},{1,9},{2,10},{3,11},{4,12},{5,13},{6,14},{7,15},{8,0},{9,1},... | collective-permute-start | bytes 3145736 | tf_op jit(solution)/shard_map/ppermute | solution.py:37
  1041.4 45.8 %collective-permute-start.13 = (bf16[256,2048]{1,0:T(8,128)(2,1)S(1)}, bf16[256,2048]{1,0:T(8,128)(2,1)S(1)}, u32[]{:S(2)}, u32[]{:S(2)}) collective-permute-start(bf16[256,2048]{1,0:T(8,128)(2,1)S(1)} %slice.258), channel_id=1, source_target_pairs={{0,8},{1,9},{2,10},{3,11},{4,12},{5,13},{6,14},{7,15},{8,0},{9,1},... | collective-permute-start | bytes 3145736 | tf_op jit(solution)/shard_map/ppermute | solution.py:37
  1045.7 63.0 %collective-permute-start.15 = (bf16[256,2048]{1,0:T(8,128)(2,1)S(1)}, bf16[256,2048]{1,0:T(8,128)(2,1)S(1)}, u32[]{:S(2)}, u32[]{:S(2)}) collective-permute-start(bf16[256,2048]{1,0:T(8,128)(2,1)S(1)} %slice.262), channel_id=1, source_target_pairs={{0,8},{1,9},{2,10},{3,11},{4,12},{5,13},{6,14},{7,15},{8,0},{9,1},... | collective-permute-start | bytes 3145736 | tf_op jit(solution)/shard_map/ppermute | solution.py:37
  (44 other events, 152.4 us)

commit v3 on v2

--- a/solution.py
+++ b/solution.py
@@ -329,140 +329,439 @@
     )(*parts)
 
 
+class TokenCube:
+    def __init__(self, own, held, part, in_half, in_x, in_y, in_z, gs, gr, ss, sr):
+        me = lax.axis_index("fsdp")
+        next_x, next_y, next_z = (flipped(me, bit) for bit in TOKEN_BITS)
+        self.partners = [next_x, next_y, next_z]
+        half = own.shape[0] // 2
+        top, low = pl.ds(0, half), pl.ds(half, half)
+        self.top, self.low = top, low
+        plan = {
+            "zt": (own.at[top], held.at[4, top], next_z),
+            "zl": (own.at[low], held.at[4, low], next_z),
+            "x": (own, held.at[1], next_x),
+            "y": (own, held.at[2], next_y),
+            "dt": (held.at[1, top], held.at[3, top], next_y),
+            "dl": (held.at[2, low], held.at[3, low], next_x),
+            "xt": (held.at[4, top], held.at[5, top], next_x),
+            "yt": (held.at[4, top], held.at[6, top], next_y),
+            "xl": (held.at[4, low], held.at[5, low], next_x),
+            "yl": (held.at[4, low], held.at[6, low], next_y),
+            "et": (held.at[5, top], held.at[7, top], next_y),
+            "el": (held.at[6, low], held.at[7, low], next_x),
+        }
+        self.gather = {
+            name: remote(src, dst, gs.at[i], gr.at[i], device)
+            for i, (name, (src, dst, device)) in enumerate(plan.items())
+        }
+        self.part, self.in_half, self.in_x, self.in_y, self.in_z = part, in_half, in_x, in_y, in_z
+        self.waves = []
+        for w, base in enumerate((4, 0)):
+            self.waves.append(
+                {
+                    "a": remote(
+                        part.at[base + 3, top], in_half.at[w, 0], ss.at[w, 0], sr.at[w, 0], next_x
+                    ),
+                    "b": remote(
+                        part.at[base + 3, low], in_half.at[w, 1], ss.at[w, 1], sr.at[w, 1], next_y
+                    ),
+                    "x": remote(part.at[base + 1], in_x.at[w], ss.at[w, 2], sr.at[w, 2], next_x),
+                    "y": remote(part.at[base + 2], in_y.at[w], ss.at[w, 3], sr.at[w, 3], next_y),
+                }
+            )
+        self.waves[0]["z"] = remote(part.at[4], in_z, ss.at[0, 4], sr.at[0, 4], next_z)
+
+    def start(self, *names):
+        for name in names:
+            self.gather[name].start()
+
+    def arrive(self, *names):
+        for name in names:
+            self.gather[name].wait_recv()
+
+    def corners(self, w):
+        self.waves[w]["a"].start()
+        self.waves[w]["b"].start()
+
+    def sideways(self, w):
+        base, wave = 4 - 4 * w, self.waves[w]
+        wave["a"].wait_recv()
+        add_into(self.part.at[base + 2, self.top], self.in_half.at[w, 0])
+        wave["y"].start()
+        wave["b"].wait_recv()
+        add_into(self.part.at[base + 1, self.low], self.in_half.at[w, 1])
+        wave["x"].start()
+
+    def across(self):
+        self.waves[0]["x"].wait_recv()
+        self.waves[0]["y"].wait_recv()
+        add_into(self.part.at[4], self.in_x.at[0], self.in_y.at[0])
+        self.waves[0]["z"].start()
+
+    def finish(self, out):
+        self.waves[1]["x"].wait_recv()
+        self.waves[1]["y"].wait_recv()
+        self.waves[0]["z"].wait_recv()
+
+        @pl.loop(0, out.shape[0] // 16)
+        def _(i):
+            at = pl.ds(pl.multiple_of(i * 16, 16), 16)
+            out[at] = (
+                self.part[0, at].astype(F32)
+                + self.in_x[1, at].astype(F32)
+                + self.in_y[1, at].astype(F32)
+                + self.in_z[at].astype(F32)
+            )
+
+        for copy in self.gather.values():
+            copy.wait_send()
+        for wave in self.waves:
+            for copy in wave.values():
+                copy.wait_send()
+
+
 TOKEN_BITS = (2, 4, 16)
-
-
-def token_gather_kernel(own, out, local, ss, rs):
-    me = lax.axis_index("fsdp")
-    next_x, next_y, next_z = (flipped(me, bit) for bit in TOKEN_BITS)
-    greet([next_x, next_y, next_z])
-    half = own.shape[0] // 2
-    top, low = pl.ds(0, half), pl.ds(half, half)
-    keep = pltpu.make_async_copy(own, out.at[0], local)
-    copies = [
-        remote(own, out.at[4], ss.at[0], rs.at[0], next_z),
-        remote(own, out.at[1], ss.at[1], rs.at[1], next_x),
-        remote(own, out.at[2], ss.at[2], rs.at[2], next_y),
-        remote(out.at[1, top], out.at[3, top], ss.at[3], rs.at[3], next_y),
-        remote(out.at[2, low], out.at[3, low], ss.at[4], rs.at[4], next_x),
-        remote(out.at[4], out.at[5], ss.at[5], rs.at[5], next_x),
-        remote(out.at[4], out.at[6], ss.at[6], rs.at[6], next_y),
-        remote(out.at[5, top], out.at[7, top], ss.at[7], rs.at[7], next_y),
-        remote(out.at[6, low], out.at[7, low], ss.at[8], rs.at[8], next_x),
+ORDER = (0, 1, 2, 4, 5, 6, 7, 3)
+
+
+def cube_scratch(rows, width):
+    dma = pltpu.SemaphoreType.DMA
+    return [
+        pltpu.VMEM((8, rows, width), BF16),
+        pltpu.VMEM((8, rows, width), BF16),
+        pltpu.VMEM((2, 2, rows // 2, width), BF16),
+        pltpu.VMEM((2, rows, width), BF16),
+        pltpu.VMEM((2, rows, width), BF16),
+        pltpu.VMEM((rows, width), BF16),
+        dma((12,)),
+        dma((12,)),
+        dma((2, 5)),
+        dma((2, 5)),
+        dma,
     ]
+
+
+def load_weights(blocks, held, sems):
+    rows = blocks[0].shape[1]
+    loads = []
+    for m in (2, 0, 1):
+        loads.append(
+            [
+                pltpu.make_async_copy(
+                    block.at[m], held.at[m, pl.ds(i * rows, rows)], sems.at[m, i]
+                )
+                for i, block in enumerate(blocks)
+            ]
+        )
+        for load in loads[-1]:
+            load.start()
+    return loads[1:] + loads[:1]
+
+
+GELU_A = 0.7978845608028654
+GELU_B = 0.044715
+
+
+def tanh_inner(gate):
+    return jnp.tanh(GELU_A * (gate + GELU_B * gate * gate * gate))
+
+
+def dot_nt(left, right):
+    return lax.dot_general(left, right, (((1,), (1,)), ((), ())), preferred_element_type=F32)
+
+
+def dot_tn(left, right):
+    return lax.dot_general(left, right, (((0,), (0,)), ((), ())), preferred_element_type=F32)
+
+
+HIDDEN_TILE = 512
+WIDTH_TILE = 1024
+
+
+def ffn_forward_kernel(n_blocks, own, *refs):
+    blocks = refs[:n_blocks]
+    out, held_out, gate_out, up_out, weights, gate_st, up_st, act = refs[n_blocks : n_blocks + 8]
+    load_sem, save_sem, keep_sem = refs[n_blocks + 8 : n_blocks + 11]
+    held, part, in_half, in_x, in_y, in_z, gs, gr, ss, sr, own_sem = refs[n_blocks + 11 :]
+    cube = TokenCube(own, held, part, in_half, in_x, in_y, in_z, gs, gr, ss, sr)
+    greet(cube.partners)
+    cube.start("zt", "zl", "x", "y")
+    keep = pltpu.make_async_copy(own, held.at[0], own_sem)
     keep.start()
-    for i, after in enumerate((None, None, None, 1, 2, 0, None, 5, 6)):
-        if after is not None:
-            copies[after].wait_recv()
-        copies[i].start()
-    for i in (3, 4, 7, 8):
-        copies[i].wait_recv()
-    for copy in copies:
-        copy.wait_send()
+    loads = load_weights(blocks, weights, load_sem)
+    hidden, width = weights.shape[1], weights.shape[2]
+    saves = []
+
+    def compute(step):
+        j, slot = ORDER[step], step % 2
+        if step >= 2:
+            for save in saves[step - 2]:
+                save.wait()
+
+        @pl.loop(0, hidden // HIDDEN_TILE)
+        def _(n):
+            at = pl.ds(pl.multiple_of(n * HIDDEN_TILE, HIDDEN_TILE), HIDDEN_TILE)
+            gate = dot_nt(held[j], weights[0, at])
+            up = dot_nt(held[j], weights[1, at])
+            gate_st[slot, :, at] = gate
+            up_st[slot, :, at] = up
+            act[:, at] = (0.5 * gate * (1.0 + tanh_inner(gate)) * up).astype(BF16)
+
+        saves.append(
+            [
+                pltpu.make_async_copy(gate_st.at[slot], gate_out.at[j], save_sem.at[0, slot]),
+                pltpu.make_async_copy(up_st.at[slot], up_out.at[j], save_sem.at[1, slot]),
+            ]
+        )
+        for save in saves[step]:
+            save.start()
+        if step == 0:
+            for load in loads[2]:
+                load.wait()
+
+        @pl.loop(0, width // WIDTH_TILE)
+        def _(n):
+            at = pl.ds(pl.multiple_of(n * WIDTH_TILE, WIDTH_TILE), WIDTH_TILE)
+            part[j, :, at] = jnp.dot(
+                act[...], weights[2, :, at], preferred_element_type=F32
+            ).astype(BF16)
+
     keep.wait()
-
-
-def gather_tokens(own, collective_id):
+    for load in loads[0] + loads[1]:
+        load.wait()
+    compute(0)
+    cube.arrive("x", "y", "zt")
+    cube.start("xt", "yt")
+    compute(1)
+    compute(2)
+    cube.arrive("zl")
+    cube.start("xl", "yl")
+    cube.arrive("xt")
+    cube.start("et")
+    compute(3)
+    cube.arrive("xl", "yt", "yl")
+    cube.start("el", "dt", "dl")
+    compute(4)
+    compute(5)
+    cube.arrive("et", "el")
+    compute(6)
+    cube.corners(0)
+    cube.arrive("dt", "dl")
+    whole = pltpu.make_async_copy(held, held_out, keep_sem)
+    whole.start()
+    compute(7)
+    cube.sideways(0)
+    cube.corners(1)
+    cube.sideways(1)
+    cube.across()
+    cube.finish(out)
+    for save in saves[6] + saves[7]:
+        save.wait()
+    whole.wait()
+
+
+def ffn_forward(own, blocks):
+    rows, width = own.shape
+    hidden = blocks[0].shape[1] * len(blocks)
     dma = pltpu.SemaphoreType.DMA
+    anywhere = pl.BlockSpec(memory_space=pl.ANY)
     return pl.pallas_call(
-        token_gather_kernel,
-        out_shape=jax.ShapeDtypeStruct((8,) + own.shape, own.dtype),
-        in_specs=[pl.BlockSpec(memory_space=pl.ANY)],
-        out_specs=pl.BlockSpec(memory_space=pl.ANY),
-        scratch_shapes=[dma, dma((9,)), dma((9,))],
-        compiler_params=pltpu.CompilerParams(collective_id=collective_id, has_side_effects=True),
-        name="gather_tokens",
-    )(own).reshape(8 * own.shape[0], own.shape[1])
-
-
-def token_scatter_kernel(part, out, mine, in_half, in_x, in_y, in_z, local, ss, rs):
-    me = lax.axis_index("fsdp")
-    next_x, next_y, next_z = (flipped(me, bit) for bit in TOKEN_BITS)
-    greet([next_x, next_y, next_z])
-    half = out.shape[0] // 2
-    top, low = pl.ds(0, half), pl.ds(half, half)
-    loads = [pltpu.make_async_copy(part.at[j], mine.at[j], local.at[j]) for j in range(8)]
-    order = (7, 5, 6, 4, 3, 1, 2, 0)
-    for j in order:
-        loads[j].start()
-    waves = []
-    for w, base in enumerate((4, 0)):
-        waves.append(
-            {
-                "a": remote(
-                    mine.at[base + 3, top], in_half.at[w, 0], ss.at[w, 0], rs.at[w, 0], next_x
-                ),
-                "b": remote(
-                    mine.at[base + 3, low], in_half.at[w, 1], ss.at[w, 1], rs.at[w, 1], next_y
-                ),
-                "x": remote(mine.at[base + 1], in_x.at[w], ss.at[w, 2], rs.at[w, 2], next_x),
-                "y": remote(mine.at[base + 2], in_y.at[w], ss.at[w, 3], rs.at[w, 3], next_y),
-            }
+        functools.partial(ffn_forward_kernel, len(blocks)),
+        out_shape=[
+            jax.ShapeDtypeStruct((rows, width), F32),
+            jax.ShapeDtypeStruct((8, rows, width), BF16),
+            jax.ShapeDtypeStruct((8, rows, hidden), F32),
+            jax.ShapeDtypeStruct((8, rows, hidden), F32),
+        ],
+        in_specs=[anywhere] * (1 + len(blocks)),
+        out_specs=[pl.BlockSpec(memory_space=pltpu.VMEM)] + [anywhere] * 3,
+        scratch_shapes=[
+            pltpu.VMEM((3, hidden, width), BF16),
+            pltpu.VMEM((2, rows, hidden), F32),
+            pltpu.VMEM((2, rows, hidden), F32),
+            pltpu.VMEM((rows, hidden), BF16),
+            dma((3, len(blocks))),
+            dma((2, 2)),
+            dma,
+        ]
+        + cube_scratch(rows, width),
+        compiler_params=pltpu.CompilerParams(
+            collective_id=2, has_side_effects=True, vmem_limit_bytes=58 * 2**20
+        ),
+        cost_estimate=pl.CostEstimate(
+            flops=48 * rows * width * hidden, bytes_accessed=300 * 2**20, transcendentals=0
+        ),
+        name="ffn_forward",
+    )(own, *blocks)
+
+
+def ffn_backward_kernel(n_blocks, own, normed, gate_in, up_in, *refs):
+    blocks = refs[:n_blocks]
+    out, mine, theirs, weights, gate_st, up_st, grads, stage = refs[n_blocks : n_blocks + 8]
+    load_sem, read_sem, write_sem, normed_sem = refs[n_blocks + 8 : n_blocks + 12]
+    held, part, in_half, in_x, in_y, in_z, gs, gr, ss, sr, own_sem = refs[n_blocks + 12 :]
+    cube = TokenCube(own, held, part, in_half, in_x, in_y, in_z, gs, gr, ss, sr)
+    greet(cube.partners)
+    cube.start("zt", "zl", "x", "y")
+    keep = pltpu.make_async_copy(own, held.at[0], own_sem)
+    keep.start()
+    hidden, width = weights.shape[1], weights.shape[2]
+    rows = own.shape[0]
+    reads = []
+    for step, j in enumerate(ORDER):
+        slot = step % 2
+        reads.append(
+            [
+                pltpu.make_async_copy(gate_in.at[j], gate_st.at[slot], read_sem.at[0, slot]),
+                pltpu.make_async_copy(up_in.at[j], up_st.at[slot], read_sem.at[1, slot]),
+            ]
         )
-    across = remote(mine.at[4], in_z, ss.at[0, 4], rs.at[0, 4], next_z)
-    for w, base in enumerate((4, 0)):
-        loads[base + 3].wait()
-        waves[w]["a"].start()
-        waves[w]["b"].start()
-    for w, base in enumerate((4, 0)):
-        loads[base + 2].wait()
-        waves[w]["a"].wait_recv()
-        add_into(mine.at[base + 2, top], in_half.at[w, 0])
-        waves[w]["y"].start()
-        loads[base + 1].wait()
-        waves[w]["b"].wait_recv()
-        add_into(mine.at[base + 1, low], in_half.at[w, 1])
-        waves[w]["x"].start()
-        loads[base].wait()
-        if w == 0:
-            continue
-        waves[0]["x"].wait_recv()
-        waves[0]["y"].wait_recv()
-        add_into(mine.at[4], in_x.at[0], in_y.at[0])
-        across.start()
-    waves[1]["x"].wait_recv()
-    waves[1]["y"].wait_recv()
-    across.wait_recv()
-
-    @pl.loop(0, out.shape[0] // 16)
-    def _(i):
-        at = pl.ds(pl.multiple_of(i * 16, 16), 16)
-        out[at] = (
-            mine[0, at].astype(F32)
-            + in_x[1, at].astype(F32)
-            + in_y[1, at].astype(F32)
-            + in_z[at].astype(F32)
-        )
-
-    for wave in waves:
-        for copy in wave.values():
-            copy.wait_send()
-    across.wait_send()
-
-
-def scatter_tokens(part, collective_id):
-    rows, width = part.shape[0] // 8, part.shape[1]
+    for read in reads[0]:
+        read.start()
+    loads = load_weights(blocks, weights, load_sem)
+
+    def compute(step):
+        j, slot = ORDER[step], step % 2
+        if step < 7:
+            for read in reads[step + 1]:
+                read.start()
+        for read in reads[step]:
+            read.wait()
+
+        @pl.loop(0, hidden // HIDDEN_TILE)
+        def _(n):
+            at = pl.ds(pl.multiple_of(n * HIDDEN_TILE, HIDDEN_TILE), HIDDEN_TILE)
+            grad_act = dot_nt(held[j], weights[2, at]).astype(BF16).astype(F32)
+            gate, up = gate_st[slot, :, at], up_st[slot, :, at]
+            inner = tanh_inner(gate)
+            gelu = 0.5 * gate * (1.0 + inner)
+            slope = 0.5 * (1.0 + inner) + 0.5 * gate * (1.0 - inner * inner) * GELU_A * (
+                1.0 + 3.0 * GELU_B * gate * gate
+            )
+            token = pl.ds(j * rows, rows)
+            grads[2, token, at] = (gelu * up).astype(BF16)
+            grads[0, token, at] = (grad_act * up * slope).astype(BF16)
+            grads[1, token, at] = (grad_act * gelu).astype(BF16)
+
+        if step == 0:
+            for load in loads[0] + loads[1]:
+                load.wait()
+        token = pl.ds(j * rows, rows)
+
+        @pl.loop(0, width // WIDTH_TILE)
+        def _(n):
+            at = pl.ds(pl.multiple_of(n * WIDTH_TILE, WIDTH_TILE), WIDTH_TILE)
+            part[j, :, at] = (
+                jnp.dot(grads[0, token], weights[0, :, at], preferred_element_type=F32)
+                + jnp.dot(grads[1, token], weights[1, :, at], preferred_element_type=F32)
+            ).astype(BF16)
+
+    keep.wait()
+    for load in loads[2]:
+        load.wait()
+    compute(0)
+    cube.arrive("x", "y", "zt")
+    cube.start("xt", "yt")
+    compute(1)
+    compute(2)
+    cube.arrive("zl")
+    cube.start("xl", "yl")
+    cube.arrive("xt")
+    cube.start("et")
+    compute(3)
+    cube.arrive("xl", "yt", "yl")
+    cube.start("el", "dt", "dl")
+    compute(4)
+    compute(5)
+    cube.arrive("et", "el")
+    compute(6)
+    cube.corners(0)
+    cube.arrive("dt", "dl")
+    compute(7)
+    cube.corners(1)
+    tokens = 8 * rows
+    refill = pltpu.make_async_copy(
+        normed, weights.at[pl.ds(0, tokens // hidden)], normed_sem
+    )
+    refill.start()
+    tile = stage.shape[1]
+    half = hidden // 2
+    jobs = [(m, i) for m in (2, 0, 1) for i in range(hidden // tile)]
+    writes = []
+
+    def weight_grad(count):
+        for _ in range(count):
+            index = len(writes)
+            m, i = jobs[index]
+            slot = index % 2
+            if index >= 2:
+                writes[index - 2].wait()
+            if m == 0 and i == 0:
+                refill.wait()
+            first = (i * tile + half) % hidden
+
+            @pl.loop(0, width // WIDTH_TILE)
+            def _(n):
+                at = pl.ds(pl.multiple_of(n * WIDTH_TILE, WIDTH_TILE), WIDTH_TILE)
+                if m == 2:
+                    right = held[:, :, at].reshape(tokens, WIDTH_TILE)
+                else:
+                    right = weights[: tokens // hidden, :, at].reshape(tokens, WIDTH_TILE)
+                stage[slot, :, at] = dot_tn(
+                    grads[m, :, pl.ds(first, tile)], right
+                ).astype(BF16)
+
+            target = theirs if first >= half else mine
+            write = pltpu.make_async_copy(
+                stage.at[slot], target.at[m, pl.ds(first % half, tile)], write_sem.at[slot]
+            )
+            write.start()
+            writes.append(write)
+
+    weight_grad(1)
+    cube.sideways(0)
+    weight_grad(1)
+    cube.sideways(1)
+    weight_grad(4)
+    cube.across()
+    weight_grad(len(jobs) - 6)
+    cube.finish(out)
+    writes[-2].wait()
+    writes[-1].wait()
+
+
+def ffn_backward(own, normed, gate, up, blocks):
+    rows, width = own.shape
+    hidden = blocks[0].shape[1] * len(blocks)
     dma = pltpu.SemaphoreType.DMA
+    anywhere = pl.BlockSpec(memory_space=pl.ANY)
+    grad = jax.ShapeDtypeStruct((3, hidden // 2, width), BF16)
     return pl.pallas_call(
-        token_scatter_kernel,
-        out_shape=jax.ShapeDtypeStruct((rows, width), F32),
-        in_specs=[pl.BlockSpec(memory_space=pl.ANY)],
-        out_specs=pl.BlockSpec(memory_space=pltpu.VMEM),
+        functools.partial(ffn_backward_kernel, len(blocks)),
+        out_shape=[jax.ShapeDtypeStruct((rows, width), F32), grad, grad],
+        in_specs=[anywhere] * (4 + len(blocks)),
+        out_specs=[pl.BlockSpec(memory_space=pltpu.VMEM), anywhere, anywhere],
         scratch_shapes=[
-            pltpu.VMEM((8, rows, width), BF16),
-            pltpu.VMEM((2, 2, rows // 2, width), BF16),
-            pltpu.VMEM((2, rows, width), BF16),
-            pltpu.VMEM((2, rows, width), BF16),
-            pltpu.VMEM((rows, width), BF16),
-            dma((8,)),
-            dma((2, 5)),
-            dma((2, 5)),
-        ],
+            pltpu.VMEM((3, hidden, width), BF16),
+            pltpu.VMEM((2, rows, hidden), F32),
+            pltpu.VMEM((2, rows, hidden), F32),
+            pltpu.VMEM((3, 8 * rows, hidden), BF16),
+            pltpu.VMEM((2, 256, width), BF16),
+            dma((3, len(blocks))),
+            dma((2, 2)),
+            dma((2,)),
+            dma,
+        ]
+        + cube_scratch(rows, width),
         compiler_params=pltpu.CompilerParams(
-            collective_id=collective_id, has_side_effects=True, vmem_limit_bytes=40 * 2**20
+            collective_id=3, has_side_effects=True, vmem_limit_bytes=62 * 2**20
         ),
-        name="scatter_tokens",
-    )(part.reshape(8, rows, width))
+        cost_estimate=pl.CostEstimate(
+            flops=96 * rows * width * hidden, bytes_accessed=400 * 2**20, transcendentals=0
+        ),
+        name="ffn_backward",
+    )(own, normed.reshape(8 * rows // hidden, hidden, width), gate, up, *blocks)
 
 
 def passed_along(block, axis, distance):
@@ -578,16 +877,16 @@
     kv_width = KVH * HD
     count = lax.axis_size("fsdp")
     bits = weight_bits(count)
-    held = ffn_weights.transpose(1, 0, 2)
-    for bit in bits:
-        held = jnp.concatenate([held, swapped(held, bit)], axis=1)
-    gate_w, up_w, down_w = held[0], held[1], held[2]
     weight_rows = qkv_weight.shape[0]
     gain_block = jnp.pad(norm_gains, (0, weight_rows * LANES - norm_gains.shape[0]))
     qkv_gathered, out_gathered = gather_weights(
         jnp.concatenate([qkv_weight, gain_block.reshape(weight_rows, LANES)], axis=1),
         jnp.concatenate([out_weight, side_weights], axis=1),
     )
+    ffn_own, qkv_gathered = lax.optimization_barrier((ffn_weights, qkv_gathered))
+    ffn_blocks = [ffn_own.transpose(1, 0, 2)]
+    for bit in bits:
+        ffn_blocks += [swapped(block, bit) for block in ffn_blocks]
     qkv_all = qkv_gathered[:, : qkv_weight.shape[1]]
     out_all, side_all = out_gathered[:, :D], out_gathered[:, D:]
     gain_all = (
@@ -624,13 +923,7 @@
     first_sum = tokens_f + jnp.dot(mixed_b, out_all, preferred_element_type=jnp.float32)
     rms_two = inv_rms(first_sum)
     normed_two = (first_sum * rms_two * ffn_gain).astype(jnp.bfloat16)
-    normed_all = gather_tokens(normed_two, 2)
-    gate_out = contract_cols(normed_all, gate_w)
-    up_out = contract_cols(normed_all, up_w)
-    gelu_gate, pull_gate = jax.vjp(gelu_tanh, gate_out)
-    act_b = (gelu_gate * up_out).astype(jnp.bfloat16)
-    ffn_part = jnp.dot(act_b, down_w, preferred_element_type=jnp.float32).astype(jnp.bfloat16)
-    ffn_out = scatter_tokens(ffn_part, 3)
+    ffn_out, normed_all, gate_kept, up_kept = ffn_forward(normed_two, ffn_blocks)
     second_sum = first_sum + ffn_out
     second_b = second_sum.astype(jnp.bfloat16)
     side_in = jnp.dot(second_b, side_all[:, :split_at], preferred_element_type=jnp.float32)
@@ -651,27 +944,16 @@
     side_grad_full = jnp.concatenate([side_in_grad, side_out_grad], axis=1)
     grad_two = grad_y + contract_cols(grad_side, back_side[:, :split_at])
     grad_two_b = grad_two.astype(jnp.bfloat16)
-    grad_two_all = gather_tokens(grad_two_b, 4)
-    grad_act_b = contract_cols(grad_two_all, down_w).astype(jnp.bfloat16)
-    grad_gate_b = pull_gate(grad_act_b * up_out)[0].astype(jnp.bfloat16)
-    grad_up_b = (grad_act_b * gelu_gate).astype(jnp.bfloat16)
-    grad_h2 = jnp.dot(grad_gate_b, gate_w, preferred_element_type=jnp.float32)
-    grad_h2 = grad_h2 + jnp.dot(grad_up_b, up_w, preferred_element_type=jnp.float32)
-    grad_h2 = scatter_tokens(grad_h2.astype(BF16), 5)
-    ffn_parts = []
-    for left, right in (
-        (grad_gate_b, normed_all),
-        (grad_up_b, normed_all),
-        (act_b, grad_two_all),
-    ):
-        part = contract_rows(left, right).astype(BF16)
-        for bit in reversed(bits):
-            half = part.shape[0] // 2
-            part = (part[:half].astype(F32) + swapped(part[half:], bit).astype(F32)).astype(
-                F32 if bit == bits[0] else BF16
-            )
-        ffn_parts.append(part)
-    ffn_grad = jnp.stack(ffn_parts, axis=1)
+    grad_h2, ffn_part, ffn_sent = ffn_backward(
+        grad_two_b, normed_all, gate_kept, up_kept, ffn_blocks
+    )
+    for bit in reversed(bits):
+        ffn_part = ffn_part.astype(F32) + swapped(ffn_sent, bit).astype(F32)
+        if bit != bits[0]:
+            half = ffn_part.shape[1] // 2
+            ffn_sent = ffn_part[:, half:].astype(BF16)
+            ffn_part = ffn_part[:, :half]
+    ffn_grad = ffn_part.transpose(1, 0, 2)
     ffn_gain_grad = jnp.sum(grad_h2 * first_sum * rms_two, axis=0)
     grad_one = grad_two + norm_back(grad_h2, first_sum, rms_two, ffn_gain)
     grad_one_b = grad_one.astype(jnp.bfloat16)

time: 1120 us -> 850 us (0.76)
  matrix products: 218 us -> 85.2 us
  Pallas kernels: 635 us -> 562 us
  waiting for transfers between devices: 71.6 us -> 7.45 us
    pallas_call x1, Pallas kernels: 171 us -> 115 us  [gather_weights(): pl.pallas_call(functools.partial(gather_kernel, chain), out_shape=outs, i...]
    ppermute x8 -> x5, waiting for transfers between devices: 62.1 us -> 7.43 us  [swapped(): return lax.ppermute(block, 'fsdp', route)]
    dot_general x7 -> x4, matrix products: 71.3 us -> 20.5 us  [contract_cols(): lax.dot_general(left_op, right_op, (((1,), (1,)), ((), ())), preferred_el...]
    dot_general x7 -> x4, matrix products: 61.8 us -> 15.9 us  [contract_rows(): lax.dot_general(left_op, right_op, (((0,), (0,)), ((), ())), preferred_el...]
    dot_general x3 -> x0, matrix products: 42.6 us -> none  [the longest x1 17.6 us: local(): jnp.dot(grad_up_b, up_w, preferred_element_type=jnp.float32)]
    pallas_call x4 -> x2, Pallas kernels: 349 us -> 334 us  [the longest x1 176 us: ffn_forward(): pl.pallas_call(functools.partial(ffn_forward_kernel, len(blocks)), out_sh...]
    concatenate x2 -> x0, other arithmetic: 12.4 us -> none  [local(): held = jnp.concatenate([held, swapped(held, bit)], axis=1)]
    add x0 -> x1, other arithmetic: none -> 12.3 us  [local(): ffn_part = ffn_part.astype(F32) + swapped(ffn_sent, bit).astype(F32)]
  transfers between devices with their start and end apart: 16 -> 13, of which waited for: 4 -> 1; matrix products, arithmetic and copies ran while one was open for 17% -> 22% of each run, Pallas kernels for 34% -> 13%
where the time goes in v3:
time: 850 us; the launch traced here: 844 us
  Pallas kernels  562 us (66%)
  matrix products  85.2 us (10%)
  other arithmetic  83.3 us (10%)
  local copies, waits for them, and re-layouts  77.1 us (9%)
  starting transfers between devices  27.1 us (3%)
    pallas_call x1, Pallas kernels, ffn_forward(): pl.pallas_call(functools.partial(ffn_forward_kernel, len(blocks)), out_sh...  176 us
    pallas_call x1, Pallas kernels, ffn_backward(): pl.pallas_call(functools.partial(ffn_backward_kernel, len(blocks)), out_s...  158 us
    pallas_call x1, Pallas kernels, gather_weights(): pl.pallas_call(functools.partial(gather_kernel, chain), out_shape=outs, i...  115 us
    pallas_call x1, Pallas kernels, scatter_weights(): pl.pallas_call(functools.partial(scatter_kernel, chain), out_shape=outs,...  114 us
    unnamed x176, local copies, waits for them, and re-layouts  20.7 us
    dot_general x4, matrix products, contract_cols(): lax.dot_general(left_op, right_op, (((1,), (1,)), ((), ())), preferred_el...  20.5 us
    ppermute x8, starting transfers between devices, passed_along(): return lax.ppermute(block, axis, route)  18.6 us
  transfers between devices with their start and end apart: 13, of which 1 were waited for; matrix products, arithmetic and copies ran while one was open for 22% of the time, Pallas kernels for 13%

profile of v3, /device:TPU:0, one launch (start us, length us, event | category | flops | bytes accessed | tf_op | source)
XLA Modules:
  0.0 844.3 jit_solution(10892366674223080569)
XLA Ops:
  1.3 1.9 pad_maximum_fusion.6.own_a
  3.2 1.7 pad_maximum_fusion.7.own_b
  4.9 114.8 %gather_weights.1 = (bf16[4,2,2,2,64,3200]{5,4,3,2,1,0:T(8,128)(2,1)}, bf16[4,2,2,2,64,2688]{5,4,3,2,1,0:T(8,128)(2,1)}) custom-call(bf16[64,3200]{1,0:T(8,128)(2,1)} %pad_maximum_fusion.6.own_a, bf16[64,2688]{1,0:T(8,128)(2,1)} %pad_maximum_fusion.7.own_b), custom_call_target="tpu_custom_call" | custom-call | bytes 385875968 | tf_op jit(solution)/shard_map/gather_weights/pallas_call | solution.py:161
  122.6 6.5 fusion.3
  129.1 1.7 copy-done.24
  136.0 4.6 collective-permute-start.2
  140.6 2.7 collective-permute-start.3
  145.2 2.9 collective-permute-start
  148.1 1.7 slice.173
  154.6 2.9 copy.232
  158.3 1.8 copy.196
  160.4 1.5 slice_negate_fusion.1
  161.9 1.7 copy.194
  163.5 2.5 copy.195
  168.7 3.4 fusion.53
  175.1 2.2 copy.245
  177.8 2.2 copy.249
  180.2 2.2 copy.246
  183.0 7.4 collective-permute-done.4.refs_1_
  190.8 2.8 collective-permute-start.1
  193.6 5.9 fusion.114
  199.6 4.0 fusion.41
  203.6 6.2 multiply_reduce_fusion.4
  211.3 175.6 %ffn_forward.1 = (f32[256,2048]{1,0:T(8,128)}, bf16[8,256,2048]{2,1,0:T(8,128)(2,1)}, f32[8,256,1024]{2,1,0:T(8,128)}, f32[8,256,1024]{2,1,0:T(8,128)}) custom-call(bf16[256,2048]{1,0:T(8,128)(2,1)} %multiply_convert_fusion.own, bf16[3,256,2048]{2,1,0:T(8,128)(2,1)} %bitcast.13.refs_0_, bf16[3,256,2048]{2,1,0:T(8,128)(2,1)} %collective-permute-done.4.refs_1_, ...), custom_call_target="tpu_custom_call" | custom-call | flops 25769803776 | bytes 314572800 | tf_op jit(solution)/shard_map/ffn_forward/pallas_call | solution.py:569
  386.9 1.9 add.152
  388.8 2.9 fusion.51
  392.6 3.8 fusion.115
  396.4 1.7 convolution_convert_fusion.2
  398.1 158.1 %ffn_backward.1 = (f32[256,2048]{1,0:T(8,128)}, bf16[3,512,2048]{2,1,0:T(8,128)(2,1)}, bf16[3,512,2048]{2,1,0:T(8,128)(2,1)}) custom-call(bf16[256,2048]{1,0:T(8,128)(2,1)} %get-tuple-element.128.own, bf16[2,1024,2048]{2,1,0:T(8,128)(2,1)} %bitcast.198, f32[8,256,1024]{2,1,0:T(8,128)} %get-tuple-element.27.gate_in, f32[8,256,1024]{2,1,0:T(8,128)} %get-tuple-element.28.up_in, ...), custom_call_target="tpu_custom_call" | custom-call | flops 51539607552 | bytes 419430400 | tf_op jit(solution)/shard_map/ffn_backward/pallas_call | solution.py:740
  556.2 2.9 multiply_reduce_fusion.1
  559.7 2.3 subtract_add_fusion
  562.0 5.6 convolution_convert_fusion.1
  567.7 3.3 fusion.20
  571.0 1.7 copy.241
  572.8 1.6 fusion.23
  574.4 7.7 fusion.10
  582.1 4.2 fusion.12
  586.3 13.8 %pad_maximum_fusion.1 = bf16[2048,2688]{0,1:T(8,128)(2,1)} fusion(bf16[2048,320]{0,1:T(8,128)(2,1)} %fusion.23, bf16[2048,320]{0,1:T(8,128)(2,1)} %convolution_convert_fusion.2, bf16[2048,2048]{0,1:T(8,128)(2,1)S(1)} %bitcast.152), kind=kLoop, calls=%fused_computation.8 | loop fusion | flops 33030144 | bytes 22020096 | tf_op jit(solution)/shard_map/concatenate | solution.py:1026
  600.1 14.1 %copy.219 = bf16[2048,2688]{1,0:T(8,128)(2,1)} copy(bf16[2048,2688]{0,1:T(8,128)(2,1)} %pad_maximum_fusion.1) | data formatting | bytes 22020096 | tf_op jit(solution)/shard_map/concatenate | solution.py:1026
  614.2 3.5 convolution_multiply_fusion
  617.7 2.2 copy.205
  620.4 1.4 copy-done.1
  621.8 2.6 pad_maximum_fusion.2
  625.8 2.2 copy.250
  628.0 2.2 copy.247
  630.3 3.1 copy.237
  633.3 3.5 fusion.117
  640.4 5.2 fusion.116
  646.4 1.5 collective-permute-start.10
  647.9 1.5 collective-permute-start.9
  649.5 2.8 multiply_reduce_fusion
  653.2 3.6 fusion.19
  661.1 12.3 %convert_add_fusion = f32[3,512,2048]{2,1,0:T(8,128)} fusion(bf16[3,512,2048]{2,1,0:T(8,128)(2,1)} %collective-permute-done.11, bf16[3,512,2048]{2,1,0:T(8,128)(2,1)} %get-tuple-element.32), kind=kLoop, calls=%fused_computation.2 | loop fusion | flops 9437184 | bytes 25165824 | tf_op jit(solution)/shard_map/add | solution.py:951
  673.4 5.1 slice.260
  678.5 8.3 collective-permute-start.12
  686.8 9.7 %fusion.33 = (bf16[2048]{0:T(1024)(128)(2,1)S(1)}, f32[256]{0:T(256)S(1)}, f32[256,2048]{1,0:T(8,128)}) fusion(bf16[256,2048]{1,0:T(8,128)(2,1)S(1)} %copy-done.14, f32[256]{0:T(256)S(1)} %copy-done.61, f32[2048]{0:T(1024)S(1)} %copy-done.49, bf16[2048,3200]{1,0:T(8,128)(2,1)} %bitcast.197, bf16[256,512]{1,0:T(8,128)(2,1)S(1)} %copy.239, ...), kind=kOutput, calls=%fused_computation.51 | convolution fusion | flops 3229611776 | bytes 17315840 | tf_op jit(solution)/shard_map/dot_general | solution.py:828
  696.8 7.1 convolution_convert_fusion
  703.9 9.9 %pad_maximum_fusion.part_a = bf16[4,2,2,2,64,3200]{5,4,3,2,1,0:T(8,128)(2,1)} fusion(bf16[4,2,2,2,64,128]{5,4,3,2,1,0:T(8,128)(2,1)S(1)} %bitcast.178, bf16[4,2,2,2,64,3072]{5,4,3,2,1,0:T(8,128)(2,1)} %bitcast.150), kind=kLoop, calls=%fused_computation.1 | loop fusion | flops 26214400 | bytes 26214400 | tf_op jit(solution)/shard_map/concatenate | solution.py:1025
  713.8 113.6 %scatter_weights.1 = (f32[64,3200]{1,0:T(8,128)}, f32[64,2688]{1,0:T(8,128)}) custom-call(bf16[4,2,2,2,64,3200]{5,4,3,2,1,0:T(8,128)(2,1)} %pad_maximum_fusion.part_a, bf16[4,2,2,2,64,2688]{5,4,3,2,1,0:T(8,128)(2,1)} %bitcast.153), custom_call_target="tpu_custom_call" | custom-call | tf_op jit(solution)/shard_map/scatter_weights/pallas_call | solution.py:319
  827.4 2.0 slice.160
  829.5 1.6 slice.163
  831.1 2.1 slice.159
  834.5 1.6 fusion.30
  836.1 8.0 fusion.9
  (264 shorter events, 39.1 us)
Async XLA Ops:
  1.3 120.5 %copy-start.13 = (bf16[256,2048]{1,0:T(8,128)(2,1)S(1)}, bf16[256,2048]{1,0:T(8,128)(2,1)}, u32[]{:S(2)}) copy-start(bf16[256,2048]{1,0:T(8,128)(2,1)} %param.10) | copy-start | bytes 3145732
  119.7 70.8 %collective-permute-start.4 = (bf16[3,256,2048]{2,1,0:T(8,128)(2,1)}, bf16[3,256,2048]{2,1,0:T(8,128)(2,1)}, u32[]{:S(2)}, u32[]{:S(2)}) collective-permute-start(bf16[3,256,2048]{2,1,0:T(8,128)(2,1)} %bitcast.13.refs_0_), channel_id=1, source_target_pairs={{0,8},{1,9},{2,10},{3,11},{4,12},{5,13},{6,14},{7,15},{8,0},{9,1},... | collective-permute-start | bytes 9437192 | tf_op jit(solution)/shard_map/ppermute | solution.py:37
  121.2 7.9 copy-start.48
  121.8 13.4 %copy-start.58 = (f32[256]{0:T(256)}, f32[256]{0:T(256)S(1)}, u32[]{:S(2)}) copy-start(f32[256]{0:T(256)S(1)} %get-tuple-element.114) | copy-start | bytes 3076
  122.6 6.5 copy-start.60
  130.9 4.2 copy-start.9
  132.3 3.7 copy-start.50
  132.3 3.7 copy-start.63
  134.9 9.5 %copy-start.26 = (f32[256,256]{1,0:T(8,128)}, f32[256,256]{1,0:T(8,128)S(1)}, u32[]{:S(2)}) copy-start(f32[256,256]{1,0:T(8,128)S(1)} %get-tuple-element.111) | copy-start | bytes 786436
  136.0 54.8 %collective-permute-start.2 = (bf16[256,2,256]{2,0,1:T(8,128)(2,1)}, bf16[256,2,256]{2,0,1:T(8,128)(2,1)}, u32[]{:S(2)}, u32[]{:S(2)}) collective-permute-start(bf16[256,2,256]{2,0,1:T(8,128)(2,1)} %fusion.69), channel_id=1, source_target_pairs={{0,2},{1,3},{2,4},{3,5},{4,6},{5,7},{6,8},{7,9},{8,10},{9,11},{10,... | collective-permute-start | bytes 786440 | tf_op jit(solution)/shard_map/ppermute | solution.py:770
  140.6 53.0 %collective-permute-start.3 = (bf16[256,2,256]{2,0,1:T(8,128)(2,1)}, bf16[256,2,256]{2,0,1:T(8,128)(2,1)}, u32[]{:S(2)}, u32[]{:S(2)}) collective-permute-start(bf16[256,2,256]{2,0,1:T(8,128)(2,1)} %fusion.69), channel_id=1, source_target_pairs={{0,1},{1,2},{2,3},{3,4},{4,5},{5,6},{6,7},{7,8},{8,9},{9,10},{10,1... | collective-permute-start | bytes 786440 | tf_op jit(solution)/shard_map/ppermute | solution.py:770
  143.3 68.0 %collective-permute-start.5 = (bf16[3,256,2048]{2,1,0:T(8,128)(2,1)}, bf16[3,256,2048]{2,1,0:T(8,128)(2,1)}, u32[]{:S(2)}, u32[]{:S(2)}) collective-permute-start(bf16[3,256,2048]{2,1,0:T(8,128)(2,1)} %bitcast.13.refs_0_), channel_id=1, source_target_pairs={{0,1},{1,0},{2,3},{3,2},{4,5},{5,4},{6,7},{7,6},{8,9},{9,8},{10,11... | collective-permute-start | bytes 9437192 | tf_op jit(solution)/shard_map/ppermute | solution.py:37
  145.2 54.3 %collective-permute-start = (bf16[256,2,256]{0,2,1:T(8,128)(2,1)}, bf16[256,2,256]{0,2,1:T(8,128)(2,1)}, u32[]{:S(2)}, u32[]{:S(2)}) collective-permute-start(bf16[256,2,256]{0,2,1:T(8,128)(2,1)} %bitcast.36), channel_id=1, source_target_pairs={{0,2},{1,3},{2,4},{3,5},{4,6},{5,7},{6,8},{7,9},{8,10},{9,11},{10,... | collective-permute-start | bytes 786440 | tf_op jit(solution)/shard_map/ppermute | solution.py:770
  151.2 8.9 %copy-start = (f32[32,8,8,256]{3,2,1,0:T(8,128)}, f32[32,8,8,256]{3,2,1,0:T(8,128)S(1)}, u32[]{:S(2)}) copy-start(f32[32,8,8,256]{3,2,1,0:T(8,128)S(1)} %copy.244) | copy-start | bytes 6291460
  154.6 5.5 copy-start.56
  161.9 6.8 copy-start.33
  172.6 21.0 %copy-start.30 = (bf16[256,2,4,256]{0,3,2,1:T(8,128)(2,1)}, bf16[256,2,4,256]{0,3,2,1:T(8,128)(2,1)S(1)}, u32[]{:S(2)}) copy-start(bf16[256,2,4,256]{0,3,2,1:T(8,128)(2,1)S(1)} %fusion.35) | copy-start | bytes 3145732
  180.2 10.3 %copy-start.62 = (s32[768]{0:T(1024)S(1)}, s32[768]{0:T(1024)}, u32[]{:S(2)}) copy-start(s32[768]{0:T(1024)} %broadcast_add_fusion) | copy-start | bytes 9220
  180.2 10.3 %copy-start.64 = (s32[256]{0:T(256)S(1)}, s32[256]{0:T(256)}, u32[]{:S(2)}) copy-start(s32[256]{0:T(256)} %copy-done.63) | copy-start | bytes 3076
  190.4 20.9 %collective-permute-start.6 = (bf16[3,256,2048]{2,1,0:T(8,128)(2,1)}, bf16[3,256,2048]{2,1,0:T(8,128)(2,1)}, u32[]{:S(2)}, u32[]{:S(2)}) collective-permute-start(bf16[3,256,2048]{2,1,0:T(8,128)(2,1)} %collective-permute-done.4.refs_1_), channel_id=1, source_target_pairs={{0,1},{1,0},{2,3},{3,2},{4,5},{5,4},{6,7},{7,6},{8,9},{9,8},{10,11... | collective-permute-start | bytes 9437192 | tf_op jit(solution)/shard_map/ppermute | solution.py:37
  190.8 8.8 %collective-permute-start.1 = (bf16[256,2,256]{0,2,1:T(8,128)(2,1)}, bf16[256,2,256]{0,2,1:T(8,128)(2,1)S(1)}, u32[]{:S(2)}, u32[]{:S(2)}) collective-permute-start(bf16[256,2,256]{0,2,1:T(8,128)(2,1)} %bitcast.36), channel_id=1, source_target_pairs={{0,1},{1,2},{2,3},{3,4},{4,5},{5,6},{6,7},{7,8},{8,9},{9,10},{10,1... | collective-permute-start | bytes 786440 | tf_op jit(solution)/shard_map/ppermute | solution.py:770
  199.5 4.1 copy-start.65
  199.6 4.1 copy-start.71
  203.6 6.2 copy-start.36
  209.9 177.0 %copy-start.4 = (f32[256,2048]{1,0:T(8,128)}, f32[256,2048]{1,0:T(8,128)S(1)}, u32[]{:S(2)}) copy-start(f32[256,2048]{1,0:T(8,128)S(1)} %get-tuple-element.127) | copy-start | bytes 6291460
  388.7 7.7 copy-start.2
  388.8 3.8 copy-start.34
  398.1 174.7 %copy-start.45 = (bf16[256,64]{0,1:T(8,128)(2,1)}, bf16[256,64]{0,1:T(8,128)(2,1)S(1)}, u32[]{:S(2)}) copy-start(bf16[256,64]{0,1:T(8,128)(2,1)S(1)} %slice.263) | copy-start | bytes 98308
  556.2 5.8 copy-start.37
  559.7 7.9 slice-start.4
  559.7 7.9 slice-start.5
  562.0 5.6 copy-start.6
  562.0 5.6 slice-start.6
  571.0 90.1 %collective-permute-start.11 = (bf16[3,512,2048]{2,1,0:T(8,128)(2,1)}, bf16[3,512,2048]{2,1,0:T(8,128)(2,1)}, u32[]{:S(2)}, u32[]{:S(2)}) collective-permute-start(bf16[3,512,2048]{2,1,0:T(8,128)(2,1)} %get-tuple-element.33), channel_id=1, source_target_pairs={{0,1},{1,0},{2,3},{3,2},{4,5},{5,4},{6,7},{7,6},{8,9},{9,8},{10,11... | collective-permute-start | bytes 18874376 | tf_op jit(solution)/shard_map/ppermute | solution.py:37
  572.7 9.3 %copy-start.42 = (bf16[256,2048]{0,1:T(8,128)(2,1)}, bf16[256,2048]{0,1:T(8,128)(2,1)S(1)}, u32[]{:S(2)}) copy-start(bf16[256,2048]{0,1:T(8,128)(2,1)S(1)} %copy.241) | copy-start | bytes 3145732
  572.7 13.5 %slice-start = ((s8[8388608]{0:T(1024)(128)(4,1)}), s8[4194304]{0:T(1024)(128)(4,1)S(1)}, s32[]{:S(2)}) async-start(s8[8388608]{0:T(1024)(128)(4,1)} %bitcast.151), calls=%async_computation | async-start | bytes 8388608
  574.3 7.7 slice-start.2
  574.3 7.7 slice-start.3
  574.4 11.9 %slice-start.1 = ((s8[8388608]{0:T(1024)(128)(4,1)}), s8[4194304]{0:T(1024)(128)(4,1)S(1)}, s32[]{:S(2)}) async-start(s8[8388608]{0:T(1024)(128)(4,1)} %bitcast.151), calls=%async_computation.1 | async-start | bytes 8388608
  586.3 27.9 %copy-start.11 = (bf16[2,4,256,768]{2,3,1,0:T(8,128)(2,1)}, bf16[2,4,256,768]{2,3,1,0:T(8,128)(2,1)S(1)}, u32[]{:S(2)}) copy-start(bf16[2,4,256,768]{2,3,1,0:T(8,128)(2,1)S(1)} %fusion.12) | copy-start | bytes 9437188
  633.3 7.0 copy-start.43
  637.7 19.1 %collective-permute-start.7 = (bf16[256,2,256]{2,0,1:T(8,128)(2,1)}, bf16[256,2,256]{2,0,1:T(8,128)(2,1)S(1)}, u32[]{:S(2)}, u32[]{:S(2)}) collective-permute-start(bf16[256,2,256]{2,0,1:T(8,128)(2,1)} %get-tuple-element.99), channel_id=1, source_target_pairs={{1,0},{2,1},{3,2},{4,3},{5,4},{6,5},{7,6},{8,7},{9,8},{10,9},{11,1... | collective-permute-start | bytes 786440 | tf_op jit(solution)/shard_map/ppermute | solution.py:770
  639.0 10.4 %copy-start.52 = (f32[1,2,8,128]{3,1,2,0:T(2,128)S(1)}, f32[1,2,8,128]{3,1,2,0:T(2,128)}, u32[]{:S(2)}) copy-start(f32[1,2,8,128]{3,1,2,0:T(2,128)} %copy.248) | copy-start | bytes 24580
  639.0 17.9 %collective-permute-start.8 = (bf16[256,2,256]{2,0,1:T(8,128)(2,1)}, bf16[256,2,256]{2,0,1:T(8,128)(2,1)S(1)}, u32[]{:S(2)}, u32[]{:S(2)}) collective-permute-start(bf16[256,2,256]{2,0,1:T(8,128)(2,1)} %get-tuple-element.100), channel_id=1, source_target_pairs={{2,0},{3,1},{4,2},{5,3},{6,4},{7,5},{8,6},{9,7},{10,8},{11,9},{12,... | collective-permute-start | bytes 786440 | tf_op jit(solution)/shard_map/ppermute | solution.py:770
  640.3 9.1 %copy-start.15 = (f32[32,8,8,256]{3,1,2,0:T(8,128)S(1)}, f32[32,8,8,256]{3,1,2,0:T(8,128)}, u32[]{:S(2)}) copy-start(f32[32,8,8,256]{3,1,2,0:T(8,128)} %copy.245) | copy-start | bytes 6291460
  640.3 9.1 %copy-start.16 = (f32[32,8,8,256]{3,1,2,0:T(8,128)S(1)}, f32[32,8,8,256]{3,1,2,0:T(8,128)}, u32[]{:S(2)}) copy-start(f32[32,8,8,256]{3,1,2,0:T(8,128)} %copy.249) | copy-start | bytes 6291460
  640.3 9.1 %copy-start.17 = (f32[32,8,8,256]{3,1,2,0:T(8,128)S(1)}, f32[32,8,8,256]{3,1,2,0:T(8,128)}, u32[]{:S(2)}) copy-start(f32[32,8,8,256]{3,1,2,0:T(8,128)} %copy.246) | copy-start | bytes 6291460
  640.3 9.1 %copy-start.18 = (f32[32,8,8,256]{3,1,2,0:T(8,128)S(1)}, f32[32,8,8,256]{3,1,2,0:T(8,128)}, u32[]{:S(2)}) copy-start(f32[32,8,8,256]{3,1,2,0:T(8,128)} %copy.250) | copy-start | bytes 6291460
  640.3 9.1 %copy-start.19 = (f32[32,8,8,256]{3,1,2,0:T(8,128)S(1)}, f32[32,8,8,256]{3,1,2,0:T(8,128)}, u32[]{:S(2)}) copy-start(f32[32,8,8,256]{3,1,2,0:T(8,128)} %copy.247) | copy-start | bytes 6291460
  640.4 9.1 %copy-start.20 = (f32[256,2048]{1,0:T(8,128)S(1)}, f32[256,2048]{1,0:T(8,128)}, u32[]{:S(2)}) copy-start(f32[256,2048]{1,0:T(8,128)} %copy.237) | copy-start | bytes 6291460
  640.4 9.1 %copy-start.25 = (f32[256,3072]{1,0:T(8,128)S(1)}, f32[256,3072]{1,0:T(8,128)}, u32[]{:S(2)}) copy-start(f32[256,3072]{1,0:T(8,128)} %copy-done.24) | copy-start | bytes 9437188
  646.4 13.3 %collective-permute-start.10 = (bf16[256,2,256]{0,2,1:T(8,128)(2,1)}, bf16[256,2,256]{0,2,1:T(8,128)(2,1)}, u32[]{:S(2)}, u32[]{:S(2)}) collective-permute-start(bf16[256,2,256]{0,2,1:T(8,128)(2,1)} %get-tuple-element.102), channel_id=1, source_target_pairs={{2,0},{3,1},{4,2},{5,3},{6,4},{7,5},{8,6},{9,7},{10,8},{11,9},{12,... | collective-permute-start | bytes 786440 | tf_op jit(solution)/shard_map/ppermute | solution.py:770
  647.9 11.8 %collective-permute-start.9 = (bf16[256,2,256]{0,2,1:T(8,128)(2,1)}, bf16[256,2,256]{0,2,1:T(8,128)(2,1)}, u32[]{:S(2)}, u32[]{:S(2)}) collective-permute-start(bf16[256,2,256]{0,2,1:T(8,128)(2,1)} %get-tuple-element.101), channel_id=1, source_target_pairs={{1,0},{2,1},{3,2},{4,3},{5,4},{6,5},{7,6},{8,7},{9,8},{10,9},{11,1... | collective-permute-start | bytes 786440 | tf_op jit(solution)/shard_map/ppermute | solution.py:770
  649.5 3.6 copy-start.3
  653.2 4.4 copy-start.28
  653.2 4.4 copy-start.29
  673.4 13.4 %copy-start.14 = (bf16[256,2048]{1,0:T(8,128)(2,1)S(1)}, bf16[256,2048]{1,0:T(8,128)(2,1)}, u32[]{:S(2)}) copy-start(bf16[256,2048]{1,0:T(8,128)(2,1)} %param.10) | copy-start | bytes 3145732
  673.4 13.4 %copy-start.31 = (bf16[256,2048]{1,0:T(8,128)(2,1)S(1)}, bf16[256,2048]{1,0:T(8,128)(2,1)}, u32[]{:S(2)}) copy-start(bf16[256,2048]{1,0:T(8,128)(2,1)} %get-tuple-element.92) | copy-start | bytes 3145732
  673.4 13.4 %copy-start.49 = (f32[2048]{0:T(1024)S(1)}, f32[2048]{0:T(1024)}, u32[]{:S(2)}) copy-start(f32[2048]{0:T(1024)} %copy-done.48) | copy-start | bytes 24580
  673.4 13.4 %copy-start.61 = (f32[256]{0:T(256)S(1)}, f32[256]{0:T(256)}, u32[]{:S(2)}) copy-start(f32[256]{0:T(256)} %copy-done.60) | copy-start | bytes 3076
  678.5 157.6 %collective-permute-start.12 = (bf16[3,256,2048]{2,1,0:T(8,128)(2,1)}, bf16[3,256,2048]{2,1,0:T(8,128)(2,1)}, u32[]{:S(2)}, u32[]{:S(2)}) collective-permute-start(bf16[3,256,2048]{2,1,0:T(8,128)(2,1)} %slice.260), channel_id=1, source_target_pairs={{0,8},{1,9},{2,10},{3,11},{4,12},{5,13},{6,14},{7,15},{8,0},{9,1},... | collective-permute-start | bytes 9437192 | tf_op jit(solution)/shard_map/ppermute | solution.py:37
  713.8 120.7 %copy-start.35 = (f32[256,2048]{1,0:T(8,128)S(1)}, f32[256,2048]{1,0:T(8,128)}, u32[]{:S(2)}) copy-start(f32[256,2048]{1,0:T(8,128)} %get-tuple-element.136) | copy-start | bytes 6291460
  827.4 7.0 copy-start.7
  827.4 7.0 copy-start.68
  (31 other events, 70.6 us)

commit v4 on v3

--- a/solution.py
+++ b/solution.py
@@ -63,53 +63,84 @@
     return (width // LANES + 1) // 2 * LANES
 
 
-def gather_kernel(chain, own_a, own_b, out_a, out_b, *sems):
-    me = lax.axis_index("fsdp")
-    core, x_at, y_at = lax.rem(me, 2), lax.rem(lax.div(me, 2), 2), lax.rem(lax.div(me, 4), 2)
-    z_at = lax.div(me, PLANE)
-    next_x, next_y, next_c = flipped(me, 2), flipped(me, 4), flipped(me, 1)
-    z_peers = [me + (lax.rem(z_at + s, chain) - z_at) * PLANE for s in range(1, chain)]
-    greet([next_x, next_y, next_c] + z_peers)
-    waves = []
-    for own, out, (local, zs, zr, xs, xr, ys, yr, a_s, ar, bs, br, cs, cr) in (
-        (own_a, out_a, sems[:13]),
-        (own_b, out_b, sems[13:]),
-    ):
-        cut = half_split(own.shape[-1])
-        ops = {"own": pltpu.make_async_copy(own, out.at[z_at, y_at, x_at, core], local)}
-        ops["z"] = [
-            remote(own, out.at[z_at, y_at, x_at, core], zs.at[s], zr.at[s], z_peers[s - 1])
-            for s in range(1, chain)
-        ]
-        steps = []
-        for s in range(chain):
-            k = lax.rem(z_at + chain - s, chain)
-            here = out.at[k, y_at, x_at, core]
-            src = own if s == 0 else here
-            from_x = out.at[k, y_at, 1 - x_at, core]
-            from_y = out.at[k, 1 - y_at, x_at, core]
+def head_norm(field):
+    return lax.rsqrt(jnp.mean(field * field, axis=-1, keepdims=True) + EPSILON)
+
+
+def turn(field, cosine, sine):
+    half = field.shape[1] // 2
+    low, high = field[:, :half], field[:, half:]
+    return jnp.concatenate([low * cosine - high * sine, high * cosine + low * sine], axis=1)
+
+
+def gain_spans(count, total):
+    per = total // count
+    spans = []
+    for d in range(count):
+        first = per * d // LANES
+        last = (per * (d + 1) - 1) // LANES
+        spans.append((first, last - first + 1))
+    return spans
+
+
+def placed_gains(norm_gains, rows):
+    per = norm_gains.shape[0]
+    offset = lax.rem(per * lax.axis_index("fsdp"), LANES)
+    return lax.dynamic_update_slice(
+        jnp.zeros((rows * LANES,), norm_gains.dtype), norm_gains, (offset,)
+    ).reshape(rows, LANES)
+
+
+def soft_rows(query, keys, reach, gap):
+    scores = dot_nt(query, keys) * HD ** (-0.5)
+    scores = jnp.where((gap >= 0) & (gap <= reach), scores, NEGATIVE)
+    exponent = jnp.exp(scores - jnp.max(scores, axis=-1, keepdims=True))
+    return exponent / jnp.sum(exponent, axis=-1, keepdims=True)
+
+
+class WeightGather:
+    def __init__(self, chain, pairs):
+        me = lax.axis_index("fsdp")
+        core, x_at, y_at = lax.rem(me, 2), lax.rem(lax.div(me, 2), 2), lax.rem(lax.div(me, 4), 2)
+        z_at = lax.div(me, PLANE)
+        next_x, next_y, next_c = flipped(me, 2), flipped(me, 4), flipped(me, 1)
+        z_peers = [me + (lax.rem(z_at + s, chain) - z_at) * PLANE for s in range(1, chain)]
+        self.partners = [next_x, next_y, next_c] + z_peers
+        self.waves = []
+        for own, out, (local, zs, zr, xs, xr, ys, yr, a_s, ar, bs, br, cs, cr) in pairs:
+            cut = half_split(own.shape[-1])
             left, right = pl.ds(0, cut), pl.ds(cut, own.shape[-1] - cut)
-            steps.append(
-                {
-                    "x": remote(src, here, xs.at[s], xr.at[s], next_x),
-                    "y": remote(src, here, ys.at[s], yr.at[s], next_y),
-                    "a": remote(
-                        from_x.at[:, left], from_x.at[:, left], a_s.at[s], ar.at[s], next_y
-                    ),
-                    "b": remote(
-                        from_y.at[:, right], from_y.at[:, right], bs.at[s], br.at[s], next_x
-                    ),
-                    "c": remote(
-                        out.at[k, :, :, core], out.at[k, :, :, core], cs.at[s], cr.at[s], next_c
-                    ),
-                }
-            )
-        ops["steps"] = steps
-        waves.append(ops)
-    flat = [(w, s) for w in range(2) for s in range(chain)]
-
-    def spread(w, s):
-        ops = waves[w]
+            ops = {"own": pltpu.make_async_copy(own, out.at[z_at, y_at, x_at, core], local)}
+            ops["z"] = [
+                remote(own, out.at[z_at, y_at, x_at, core], zs.at[s], zr.at[s], z_peers[s - 1])
+                for s in range(1, chain)
+            ]
+            steps = []
+            for s in range(chain):
+                k = lax.rem(z_at + chain - s, chain)
+                here = out.at[k, y_at, x_at, core]
+                src = own if s == 0 else here
+                from_x = out.at[k, y_at, 1 - x_at, core]
+                from_y = out.at[k, 1 - y_at, x_at, core]
+                column = out.at[k, :, :, core]
+                steps.append(
+                    {
+                        "x": remote(src, here, xs.at[s], xr.at[s], next_x),
+                        "y": remote(src, here, ys.at[s], yr.at[s], next_y),
+                        "a": remote(
+                            from_x.at[:, left], from_x.at[:, left], a_s.at[s], ar.at[s], next_y
+                        ),
+                        "b": remote(
+                            from_y.at[:, right], from_y.at[:, right], bs.at[s], br.at[s], next_x
+                        ),
+                        "c": remote(column, column, cs.at[s], cr.at[s], next_c),
+                    }
+                )
+            ops["steps"] = steps
+            self.waves.append(ops)
+
+    def spread(self, w, s):
+        ops = self.waves[w]
         if s == 0:
             for copy in [ops["own"]] + ops["z"]:
                 copy.start()
@@ -118,57 +149,260 @@
         ops["steps"][s]["x"].start()
         ops["steps"][s]["y"].start()
 
-    def pass_on(w, s):
-        step = waves[w]["steps"][s]
+    def pass_on(self, w, s):
+        step = self.waves[w]["steps"][s]
         step["x"].wait_recv()
         step["a"].start()
         step["y"].wait_recv()
         step["b"].start()
 
-    def across(w, s):
-        step = waves[w]["steps"][s]
+    def across(self, w, s):
+        step = self.waves[w]["steps"][s]
         step["a"].wait_recv()
         step["b"].wait_recv()
         if s == 0:
-            waves[w]["own"].wait()
+            self.waves[w]["own"].wait()
         step["c"].start()
 
-    for i in range(len(flat) + 2):
-        if i < len(flat):
-            spread(*flat[i])
-        if 1 <= i <= len(flat):
-            pass_on(*flat[i - 1])
-        if i >= 2:
-            across(*flat[i - 2])
-    for ops in waves:
-        for copy in ops["z"]:
-            copy.wait_send()
-        for step in ops["steps"]:
-            for name in "xyab":
-                step[name].wait_send()
-            step["c"].wait()
-
-
-def gather_weights(own_a, own_b):
+    def complete(self, w):
+        for step in self.waves[w]["steps"]:
+            step["c"].wait_recv()
+
+    def drain(self):
+        for ops in self.waves:
+            for copy in ops["z"]:
+                copy.wait_send()
+            for step in ops["steps"]:
+                for name in "xyabc":
+                    step[name].wait_send()
+
+
+def attention_forward_kernel(
+    count,
+    own_a,
+    own_b,
+    own_ffn,
+    tokens,
+    cosine,
+    sine,
+    position,
+    full_a,
+    full_b,
+    full_ffn,
+    gains,
+    normed,
+    projected,
+    query,
+    key_rows,
+    value_rows,
+    mixed,
+    first_sum,
+    normed_two,
+    wa,
+    wb,
+    *sems,
+):
+    me = lax.axis_index("fsdp")
+    chain = count // PLANE
+    bits = weight_bits(count)
+    gather = WeightGather(chain, ((own_a, wa, sems[:13]), (own_b, wb, sems[13:26])))
+    ffn_local, ffn_s, ffn_r, halo_s, halo_r, save = sems[26:]
+    ahead = [lax.rem(me + d, count) for d in (1, 2)]
+    behind = [lax.rem(me + count - d, count) for d in (1, 2)]
+    greet(gather.partners + [flipped(me, bit) for bit in bits[:-1]] + ahead + behind)
+    ffn_own = pltpu.make_async_copy(own_ffn, full_ffn.at[0], ffn_local)
+    ffn_copies = []
+    for i, bit in enumerate(bits):
+        size = 1 << i
+        src = own_ffn if i == 0 else full_ffn.at[pl.ds(0, size)]
+        dst = full_ffn.at[1] if i == 0 else full_ffn.at[pl.ds(size, size)]
+        ffn_copies.append(remote(src, dst, ffn_s.at[i], ffn_r.at[i], flipped(me, bit)))
+    halo = []
+    for d in (1, 2):
+        for j, rows in enumerate((key_rows, value_rows)):
+            at = 2 * (d - 1) + j
+            halo.append(
+                remote(rows.at[2], rows.at[2 - d], halo_s.at[at], halo_r.at[at], ahead[d - 1])
+            )
+    for s in range(chain):
+        gather.spread(0, s)
+        if s >= 1:
+            gather.pass_on(0, s - 1)
+        if s >= 2:
+            gather.across(0, s - 2)
+    gather.spread(1, 0)
+    ffn_own.start()
+    gather.pass_on(0, chain - 1)
+    gather.across(0, chain - 2)
+    gather.across(0, chain - 1)
+    gather.complete(0)
+    keep_a = pltpu.make_async_copy(wa, full_a, save.at[0])
+    keep_a.start()
+
+    width_a, per = QKV_WIDTH, gains.shape[1] // count
+    spans = gain_spans(count, gains.shape[1])
+    pieces = {}
+    for d, (first, n_rows) in enumerate(spans):
+        block = wa[
+            d // PLANE, d // 4 % 2, d // 2 % 2, d % 2, 0:16, width_a : width_a + LANES
+        ].astype(F32)
+        for r in range(n_rows):
+            pieces.setdefault(first + r, []).append(block[r : r + 1])
+    for t, terms in pieces.items():
+        total = terms[0]
+        for term in terms[1:]:
+            total = total + term
+        gains[:, t * LANES : (t + 1) * LANES] = total
+
+    rows, depth = tokens.shape
+
+    @pl.loop(0, rows // 32)
+    def _(i):
+        at = pl.ds(pl.multiple_of(i * 32, 32), 32)
+        field = tokens[at].astype(F32)
+        normed[at] = (field * head_norm(field) * gains[:, :depth]).astype(BF16)
+
+    def project(n):
+        at = pl.ds(pl.multiple_of(n * 512, 512), 512)
+        weight = wa[:, :, :, :, :, at].reshape(depth, 512)
+        projected[:, at] = jnp.dot(normed[...], weight, preferred_element_type=F32)
+
+    query_width = HQ * HD
+    kv_width = KVH * HD
+
+    @pl.loop(query_width // 512, (query_width + 2 * kv_width) // 512)
+    def _(n):
+        project(n)
+
+    for g in range(KVH):
+        at = slice(query_width + g * HD, query_width + (g + 1) * HD)
+        field = projected[:, at]
+        key_gain = gains[:, 2 * depth + HD :]
+        key_rows[2, :, g * HD : (g + 1) * HD] = turn(
+            field * head_norm(field) * key_gain, cosine[...], sine[...]
+        ).astype(BF16)
+    value_rows[2] = projected[:, query_width + kv_width :].astype(BF16)
+    for copy in halo:
+        copy.start()
+    gather.pass_on(1, 0)
+    gather.spread(1, 1)
+    ffn_copies[0].start()
+
+    @pl.loop(0, query_width // 512)
+    def _(n):
+        project(n)
+
+    @pl.loop(0, HQ)
+    def _(h):
+        at = pl.ds(pl.multiple_of(h * HD, HD), HD)
+        field = projected[:, at]
+        query_gain = gains[:, 2 * depth : 2 * depth + HD]
+        query[:, at] = turn(
+            field * head_norm(field) * query_gain, cosine[...], sine[...]
+        ).astype(BF16)
+
+    gather.pass_on(1, 1)
+    gather.spread(1, 2)
+    gather.across(1, 0)
+    for copy in halo:
+        copy.wait_recv()
+    n_keys = 3 * rows
+    gap = (
+        lax.broadcasted_iota(jnp.int32, (rows, n_keys), 0)
+        - lax.broadcasted_iota(jnp.int32, (rows, n_keys), 1)
+        + 2 * rows
+    )
+    reach = jnp.minimum(position[...], WINDOW - 1)
+
+    def heads(first, last):
+        @pl.loop(first, last)
+        def _(h):
+            at = pl.ds(pl.multiple_of(h * HD, HD), HD)
+            group = pl.ds(pl.multiple_of(lax.div(h, HQ // KVH) * HD, HD), HD)
+            keys = key_rows[:, :, group].reshape(n_keys, HD)
+            values = value_rows[:, :, group].reshape(n_keys, HD)
+            probs = soft_rows(query[:, at], keys, reach, gap).astype(BF16)
+            mixed[:, at] = jnp.dot(probs, values, preferred_element_type=F32).astype(BF16)
+
+    heads(0, 2)
+    for s in range(3, chain):
+        gather.pass_on(1, s - 1)
+        gather.spread(1, s)
+        gather.across(1, s - 2)
+    heads(2, 5)
+    gather.pass_on(1, chain - 1)
+    gather.across(1, chain - 2)
+    heads(5, 8)
+    gather.across(1, chain - 1)
+    gather.complete(1)
+    keep_b = pltpu.make_async_copy(wb, full_b, save.at[1])
+    keep_b.start()
+
+    @pl.loop(0, depth // 512)
+    def _(n):
+        at = pl.ds(pl.multiple_of(n * 512, 512), 512)
+        weight = wb[:, :, :, :, :, at].reshape(depth, 512)
+        first_sum[:, at] = tokens[:, at].astype(F32) + jnp.dot(
+            mixed[...], weight, preferred_element_type=F32
+        )
+
+    @pl.loop(0, rows // 32)
+    def _(i):
+        at = pl.ds(pl.multiple_of(i * 32, 32), 32)
+        field = first_sum[at]
+        normed_two[at] = (field * head_norm(field) * gains[:, depth : 2 * depth]).astype(BF16)
+
+    ffn_own.wait()
+    for i, copy in enumerate(ffn_copies):
+        if i > 0:
+            copy.start()
+        copy.wait_recv()
+    for copy in ffn_copies + halo:
+        copy.wait_send()
+    gather.drain()
+    keep_a.wait()
+    keep_b.wait()
+
+
+QKV_WIDTH = (HQ + 2 * KVH) * HD
+
+
+def attention_forward(own_a, own_b, own_ffn, tokens, cosine, sine, position):
     count = lax.axis_size("fsdp")
     chain = count // PLANE
+    rows, depth = tokens.shape
+    n_blocks = 1 << len(weight_bits(count))
     dma = pltpu.SemaphoreType.DMA
-    sems = [dma] + [dma((chain,))] * 12
-    outs = [
-        jax.ShapeDtypeStruct((chain, 2, 2, 2) + own.shape, own.dtype) for own in (own_a, own_b)
-    ]
-    moved = sum(o.size * 2 for o in outs)
-    full_a, full_b = pl.pallas_call(
-        functools.partial(gather_kernel, chain),
-        out_shape=outs,
-        in_specs=[pl.BlockSpec(memory_space=pl.ANY)] * 2,
-        out_specs=[pl.BlockSpec(memory_space=pl.ANY)] * 2,
-        scratch_shapes=sems * 2,
-        compiler_params=pltpu.CompilerParams(collective_id=0, has_side_effects=True),
-        cost_estimate=pl.CostEstimate(flops=0, bytes_accessed=moved * 16, transcendentals=0),
-        name="gather_weights",
-    )(own_a, own_b)
-    return (full_a.reshape(-1, own_a.shape[1]), full_b.reshape(-1, own_b.shape[1]))
+    anywhere, vmem = pl.BlockSpec(memory_space=pl.ANY), pl.BlockSpec(memory_space=pltpu.VMEM)
+    shape_a, shape_b = ((chain, 2, 2, 2) + own.shape for own in (own_a, own_b))
+    full_a, full_b, *rest = pl.pallas_call(
+        functools.partial(attention_forward_kernel, count),
+        out_shape=[
+            jax.ShapeDtypeStruct(shape_a, BF16),
+            jax.ShapeDtypeStruct(shape_b, BF16),
+            jax.ShapeDtypeStruct((n_blocks,) + own_ffn.shape, BF16),
+            jax.ShapeDtypeStruct((1, 2 * depth + 2 * HD), F32),
+            jax.ShapeDtypeStruct((rows, depth), BF16),
+            jax.ShapeDtypeStruct((rows, QKV_WIDTH), F32),
+            jax.ShapeDtypeStruct((rows, HQ * HD), BF16),
+            jax.ShapeDtypeStruct((3, rows, KVH * HD), BF16),
+            jax.ShapeDtypeStruct((3, rows, KVH * HD), BF16),
+            jax.ShapeDtypeStruct((rows, HQ * HD), BF16),
+            jax.ShapeDtypeStruct((rows, depth), F32),
+            jax.ShapeDtypeStruct((rows, depth), BF16),
+        ],
+        in_specs=[anywhere] * 3 + [vmem] * 4,
+        out_specs=[anywhere] * 3 + [vmem] * 9,
+        scratch_shapes=[pltpu.VMEM(shape_a, BF16), pltpu.VMEM(shape_b, BF16)]
+        + ([dma] + [dma((chain,))] * 12) * 2
+        + [dma, dma((len(weight_bits(count)),)), dma((len(weight_bits(count)),))]
+        + [dma((4,)), dma((4,)), dma((2,))],
+        compiler_params=pltpu.CompilerParams(
+            collective_id=0, has_side_effects=True, vmem_limit_bytes=58 * 2**20
+        ),
+        name="attention_forward",
+    )(own_a, own_b, own_ffn, tokens, cosine, sine, position)
+    return (full_a.reshape(-1, own_a.shape[1]), full_b.reshape(-1, own_b.shape[1]), *rest)
 
 
 def add_into(target, *terms):
@@ -178,155 +412,495 @@
     @pl.loop(0, rows // tile)
     def _(i):
         at = pl.ds(pl.multiple_of(i * tile, tile), tile)
-        total = target[at].astype(F32)
-        for term in terms:
-            total = total + term[at].astype(F32)
-        target[at] = total.astype(target.dtype)
-
-
-def scatter_kernel(chain, part_a, part_b, out_a, out_b, *scratch):
-    me = lax.axis_index("fsdp")
-    core, x_at, y_at = lax.rem(me, 2), lax.rem(lax.div(me, 2), 2), lax.rem(lax.div(me, 4), 2)
-    z_at = lax.div(me, PLANE)
-    next_x, next_y, next_c = flipped(me, 2), flipped(me, 4), flipped(me, 1)
-    z_peers = [me + (lax.rem(z_at + s, chain) - z_at) * PLANE for s in range(1, chain)]
-    greet([next_x, next_y, next_c] + z_peers)
-    waves = []
-    half = len(scratch) // 2
-    for part, out, held in ((part_a, out_a, scratch[:half]), (part_b, out_b, scratch[half:])):
-        mine, sibling, in_a, in_b, in_x, in_y, in_z = held[:7]
-        local, cs, cr, a_s, ar, bs, br, xs, xr, ys, yr, zs, zr = held[7:]
-        width = out.shape[-1]
-        cut = half_split(width)
-        left, right = pl.ds(0, cut), pl.ds(cut, width - cut)
-        steps = []
+        if len(terms) == 1:
+            target[at] = target[at] + terms[0][at]
+        else:
+            total = target[at].astype(F32)
+            for term in terms:
+                total = total + term[at].astype(F32)
+            target[at] = total.astype(target.dtype)
+
+
+class WeightScatter:
+    def __init__(self, chain, part, out, sibling, in_a, in_b, in_x, in_y, in_z, *sems):
+        cs, cr, a_s, ar, bs, br, xs, xr, ys, yr, zs, zr = sems
+        me = lax.axis_index("fsdp")
+        core, x_at, y_at = lax.rem(me, 2), lax.rem(lax.div(me, 2), 2), lax.rem(lax.div(me, 4), 2)
+        z_at = lax.div(me, PLANE)
+        next_x, next_y, next_c = flipped(me, 2), flipped(me, 4), flipped(me, 1)
+        z_peers = [me + (lax.rem(z_at + s, chain) - z_at) * PLANE for s in range(1, chain)]
+        self.partners = [next_x, next_y, next_c] + z_peers
+        self.chain, self.out, self.in_z = chain, out, in_z
+        cut = half_split(out.shape[-1])
+        left, right = pl.ds(0, cut), pl.ds(cut, out.shape[-1] - cut)
+        self.left, self.right = left, right
+        self.order = list(range(1, chain)) + [0]
+        self.blocks = [lax.rem(z_at + s, chain) for s in range(chain)]
+        self.steps = []
         for s in range(chain):
-            k = lax.rem(z_at + s, chain)
+            mine = part.at[s, :, :, core]
             step = {
-                "left": left,
-                "right": right,
-                "mine": mine.at[s],
-                "sibling": sibling.at[s],
-                "in_a": in_a.at[s],
-                "in_b": in_b.at[s],
-                "in_x": in_x.at[s],
-                "in_y": in_y.at[s],
-                "here": mine.at[s, y_at, x_at],
-                "to_x": mine.at[s, y_at, 1 - x_at],
-                "to_y": mine.at[s, 1 - y_at, x_at],
-                "local": pltpu.make_async_copy(part.at[k, :, :, core], mine.at[s], local.at[s]),
+                "mine": [part.at[s, j // 2, j % 2, core] for j in range(4)],
+                "sibling": [sibling.at[s, j // 2, j % 2] for j in range(4)],
+                "in": (in_a.at[s], in_b.at[s], in_x.at[s], in_y.at[s]),
+                "here": part.at[s, y_at, x_at, core],
+                "to_x": part.at[s, y_at, 1 - x_at, core],
+                "to_y": part.at[s, 1 - y_at, x_at, core],
                 "c": remote(
-                    part.at[k, :, :, 1 - core], sibling.at[s], cs.at[s], cr.at[s], next_c
-                ),
-                "a": remote(
-                    mine.at[s, 1 - y_at, 1 - x_at, :, left],
-                    in_a.at[s],
-                    a_s.at[s],
-                    ar.at[s],
-                    next_x,
-                ),
-                "b": remote(
-                    mine.at[s, 1 - y_at, 1 - x_at, :, right],
-                    in_b.at[s],
-                    bs.at[s],
-                    br.at[s],
-                    next_y,
+                    part.at[s, :, :, 1 - core], sibling.at[s], cs.at[s], cr.at[s], next_c
                 ),
             }
-            step["x"] = remote(step["to_x"], step["in_x"], xs.at[s], xr.at[s], next_x)
-            step["y"] = remote(step["to_y"], step["in_y"], ys.at[s], yr.at[s], next_y)
+            corner = part.at[s, 1 - y_at, 1 - x_at, core]
+            step["a"] = remote(corner.at[:, left], in_a.at[s], a_s.at[s], ar.at[s], next_x)
+            step["b"] = remote(corner.at[:, right], in_b.at[s], bs.at[s], br.at[s], next_y)
+            step["x"] = remote(step["to_x"], in_x.at[s], xs.at[s], xr.at[s], next_x)
+            step["y"] = remote(step["to_y"], in_y.at[s], ys.at[s], yr.at[s], next_y)
             if s > 0:
                 step["z"] = remote(
                     step["here"], in_z.at[s - 1], zs.at[s - 1], zr.at[s - 1], z_peers[s - 1]
                 )
-            steps.append(step)
-        waves.append((steps, in_z, out))
-    order = [s for s in range(1, chain)] + [0]
-    flat = [waves[w][0][s] for w in range(2) for s in order]
-
-    def halve(step):
-        step["local"].wait()
+            self.steps.append(step)
+
+    def cross(self, i):
+        self.steps[self.order[i]]["c"].start()
+
+    def halve(self, i):
+        step = self.steps[self.order[i]]
         step["c"].wait_recv()
-        for j in range(4):
-            add_into(step["mine"].at[j // 2, j % 2], step["sibling"].at[j // 2, j % 2])
+        for mine, sibling in zip(step["mine"], step["sibling"]):
+            add_into(mine, sibling)
         step["a"].start()
         step["b"].start()
 
-    def sideways(step):
+    def sideways(self, i):
+        step = self.steps[self.order[i]]
+        in_a, in_b, _, _ = step["in"]
         step["a"].wait_recv()
-        add_into(step["to_y"].at[:, step["left"]], step["in_a"])
+        add_into(step["to_y"].at[:, self.left], in_a)
         step["y"].start()
         step["b"].wait_recv()
-        add_into(step["to_x"].at[:, step["right"]], step["in_b"])
+        add_into(step["to_x"].at[:, self.right], in_b)
         step["x"].start()
 
-    def finish(step):
+    def finish(self, i):
+        step = self.steps[self.order[i]]
         step["x"].wait_recv()
         step["y"].wait_recv()
-        add_into(step["here"], step["in_x"], step["in_y"])
+        add_into(step["here"], *step["in"][2:])
         if "z" in step:
             step["z"].start()
 
-    for step in flat:
-        step["local"].start()
-        step["c"].start()
-    for i in range(len(flat) + 2):
-        if i < len(flat):
-            halve(flat[i])
-        if 1 <= i <= len(flat):
-            sideways(flat[i - 1])
-        if i >= 2:
-            finish(flat[i - 2])
-    for steps, in_z, out in waves:
-        for step in steps[1:]:
+    def total(self):
+        for step in self.steps[1:]:
             step["z"].wait_recv()
-        rows = out.shape[0]
-
-        @pl.loop(0, rows // 16)
+
+        @pl.loop(0, self.out.shape[0] // 16)
         def _(i):
             at = pl.ds(pl.multiple_of(i * 16, 16), 16)
-            total = steps[0]["here"][at].astype(F32)
-            for s in range(chain - 1):
-                total = total + in_z[s, at].astype(F32)
-            out[at] = total
-
-    for step in flat:
-        for name in "cabxyz":
-            if name in step:
-                step[name].wait_send()
-
-
-def scatter_weights(part_a, part_b):
+            total = self.steps[0]["here"][at].astype(F32)
+            for s in range(self.chain - 1):
+                total = total + self.in_z[s, at].astype(F32)
+            self.out[at] = total
+
+        for step in self.steps:
+            for name in "cabxyz":
+                if name in step:
+                    step[name].wait_send()
+
+
+def scatter_scratch(chain, rows, width):
+    cut = half_split(width)
+    shapes = [
+        (chain, 2, 2, 2, rows, width),
+        (chain, 2, 2, rows, width),
+        (chain, rows, cut),
+        (chain, rows, width - cut),
+        (chain, rows, width),
+        (chain, rows, width),
+        (chain - 1, rows, width),
+    ]
+    return [pltpu.VMEM(shape, BF16) for shape in shapes] + [
+        pltpu.SemaphoreType.DMA((chain,))
+    ] * 12
+
+
+def turn_back(grad, cosine, sine):
+    half = grad.shape[1] // 2
+    low, high = grad[:, :half], grad[:, half:]
+    return jnp.concatenate([low * cosine + high * sine, high * cosine - low * sine], axis=1)
+
+
+def head_back(grad_rot, field, gain, cosine, sine):
+    grad = turn_back(grad_rot, cosine, sine)
+    scale = head_norm(field)
+    weighted = grad * gain
+    back = scale * weighted - field * (
+        scale * scale * scale * jnp.mean(weighted * field, axis=-1, keepdims=True)
+    )
+    return back, jnp.sum(grad * field * scale, axis=0, keepdims=True)
+
+
+def attention_backward_kernel(
+    count,
+    full_a,
+    full_b,
+    side_part,
+    grad_one_b,
+    grad_one,
+    tokens,
+    mixed,
+    query,
+    key_rows,
+    value_rows,
+    projected,
+    gains,
+    cosine,
+    sine,
+    position,
+    out_sum,
+    grad_projected,
+    input_grad,
+    attn_gain_grad,
+    head_gain_grad,
+    weight,
+    grad_mixed,
+    grad_normed,
+    grad_keys,
+    grad_values,
+    halo_out,
+    halo_in,
+    weight_sem,
+    side_sem,
+    halo_s,
+    halo_r,
+    part,
+    *scratch,
+):
+    me = lax.axis_index("fsdp")
+    chain = count // PLANE
+    scatter = WeightScatter(chain, part, out_sum, *scratch)
+    ahead = [lax.rem(me + d, count) for d in (1, 2)]
+    behind = [lax.rem(me + count - d, count) for d in (1, 2)]
+    greet(scatter.partners + ahead + behind)
+    rows, depth = tokens.shape
+    query_width, kv_width = HQ * HD, KVH * HD
+    out_width = depth
+    load_out = pltpu.make_async_copy(
+        full_b.at[:, :, :, :, :, pl.ds(0, out_width)],
+        weight.at[:, :, :, :, :, pl.ds(0, out_width)],
+        weight_sem,
+    )
+    load_out.start()
+    sides = []
+    for s in range(chain):
+        sides.append(
+            pltpu.make_async_copy(
+                side_part.at[scatter.blocks[s]],
+                part.at[s, :, :, :, :, pl.ds(out_width, part.shape[-1] - out_width)],
+                side_sem.at[s],
+            )
+        )
+        sides[-1].start()
+    tile = depth // chain
+    block_shape = part.shape[1:5]
+    for i, s in enumerate(scatter.order):
+        left = mixed[:, pl.ds(pl.multiple_of(scatter.blocks[s] * tile, tile), tile)]
+
+        @pl.loop(0, out_width // 512)
+        def _(n):
+            at = pl.ds(pl.multiple_of(n * 512, 512), 512)
+            part[s, :, :, :, :, at] = (
+                dot_tn(left, grad_one_b[:, at]).astype(BF16).reshape(block_shape + (512,))
+            )
+
+        sides[s].wait()
+        scatter.cross(i)
+    load_out.wait()
+
+    @pl.loop(0, chain)
+    def _(k):
+        at = pl.ds(pl.multiple_of(k * tile, tile), tile)
+        grad_mixed[:, at] = dot_nt(
+            grad_one_b[...], weight[k, :, :, :, :, 0:out_width].reshape(tile, out_width)
+        ).astype(BF16)
+
+    load_qkv = pltpu.make_async_copy(
+        full_a.at[:, :, :, :, :, pl.ds(0, QKV_WIDTH)], weight, weight_sem
+    )
+    load_qkv.start()
+    grad_keys[...] = jnp.zeros_like(grad_keys)
+    grad_values[...] = jnp.zeros_like(grad_values)
+    head_gain_grad[...] = jnp.zeros_like(head_gain_grad)
+    n_keys = 3 * rows
+    gap = (
+        lax.broadcasted_iota(jnp.int32, (rows, n_keys), 0)
+        - lax.broadcasted_iota(jnp.int32, (rows, n_keys), 1)
+        + 2 * rows
+    )
+    reach = jnp.minimum(position[...], WINDOW - 1)
+    query_gain = gains[:, 2 * depth : 2 * depth + HD]
+    key_gain = gains[:, 2 * depth + HD :]
+    scale = HD ** (-0.5)
+
+    def heads(first, last):
+        @pl.loop(first, last)
+        def _(h):
+            at = pl.ds(pl.multiple_of(h * HD, HD), HD)
+            group = pl.ds(pl.multiple_of(lax.div(h, HQ // KVH) * HD, HD), HD)
+            keys = key_rows[:, :, group].reshape(n_keys, HD)
+            values = value_rows[:, :, group].reshape(n_keys, HD)
+            probs = soft_rows(query[:, at], keys, reach, gap)
+            grad_probs = dot_nt(grad_mixed[:, at], values)
+            delta = jnp.sum(probs * grad_probs, axis=-1, keepdims=True)
+            grad_scores = (probs * (grad_probs - delta)).astype(BF16)
+            grad_rot = jnp.dot(grad_scores, keys, preferred_element_type=F32) * scale
+            grad_keys[:, :, group] += (dot_tn(grad_scores, query[:, at]) * scale).reshape(
+                3, rows, HD
+            )
+            grad_values[:, :, group] += dot_tn(probs.astype(BF16), grad_mixed[:, at]).reshape(
+                3, rows, HD
+            )
+            back, gain_grad = head_back(
+                grad_rot, projected[:, at], query_gain, cosine[...], sine[...]
+            )
+            grad_projected[:, at] = back.astype(BF16)
+            head_gain_grad[:, 0:HD] += gain_grad
+
+    last = chain - 1
+    for i in range(chain - 2):
+        scatter.halve(i)
+        if i >= 2:
+            scatter.sideways(i - 2)
+        if i >= 4:
+            scatter.finish(i - 4)
+    if chain > 5:
+        scatter.finish(last - 5)
+    heads(0, 1)
+    scatter.sideways(last - 3)
+    scatter.halve(last - 1)
+    heads(1, 2)
+    if chain > 4:
+        scatter.finish(last - 4)
+    scatter.sideways(last - 2)
+    scatter.halve(last)
+    heads(2, 3)
+    scatter.finish(last - 3)
+    scatter.sideways(last - 1)
+    heads(3, 5)
+    scatter.finish(last - 2)
+    scatter.sideways(last)
+    heads(5, 7)
+    scatter.finish(last - 1)
+    heads(7, 8)
+    halo = []
+    for d in (1, 2):
+        for j, grad in enumerate((grad_keys, grad_values)):
+            at = 2 * (d - 1) + j
+            halo_out[at] = grad[2 - d].astype(BF16)
+            halo.append(
+                remote(
+                    halo_out.at[at],
+                    halo_in.at[at],
+                    halo_s.at[at],
+                    halo_r.at[at],
+                    behind[d - 1],
+                )
+            )
+            halo[-1].start()
+    load_qkv.wait()
+
+    @pl.loop(0, chain)
+    def _(k):
+        at = pl.ds(pl.multiple_of(k * tile, tile), tile)
+        grad_normed[:, at] = dot_nt(
+            grad_projected[:, 0:query_width],
+            weight[k, :, :, :, :, 0:query_width].reshape(tile, query_width),
+        )
+
+    scatter.finish(last)
+    for copy in halo:
+        copy.wait_recv()
+    for g in range(KVH):
+        at = slice(g * HD, (g + 1) * HD)
+        place = slice(query_width + g * HD, query_width + (g + 1) * HD)
+        grad_rot = (
+            grad_keys[2, :, at] + halo_in[0, :, at].astype(F32) + halo_in[2, :, at].astype(F32)
+        )
+        back, gain_grad = head_back(
+            grad_rot, projected[:, place], key_gain, cosine[...], sine[...]
+        )
+        grad_projected[:, place] = back.astype(BF16)
+        head_gain_grad[:, HD : 2 * HD] += gain_grad
+    grad_projected[:, query_width + kv_width :] = (
+        grad_values[2] + halo_in[1].astype(F32) + halo_in[3].astype(F32)
+    ).astype(BF16)
+
+    @pl.loop(0, chain)
+    def _(k):
+        at = pl.ds(pl.multiple_of(k * tile, tile), tile)
+        grad_normed[:, at] += dot_nt(
+            grad_projected[:, query_width:],
+            weight[k, :, :, :, :, query_width:].reshape(tile, 2 * kv_width),
+        )
+
+    attn_gain_grad[...] = jnp.zeros_like(attn_gain_grad)
+    attn_gain = gains[:, :depth]
+
+    @pl.loop(0, rows // 16)
+    def _(i):
+        at = pl.ds(pl.multiple_of(i * 16, 16), 16)
+        field = tokens[at].astype(F32)
+        rms = head_norm(field)
+        grad = grad_normed[at]
+        weighted = grad * attn_gain
+        back = rms * weighted - field * (
+            rms * rms * rms * jnp.mean(weighted * field, axis=-1, keepdims=True)
+        )
+        input_grad[at] = (grad_one[at] + back).astype(BF16)
+        attn_gain_grad[...] += jnp.sum(grad * field * rms, axis=0, keepdims=True)
+
+    scatter.total()
+    for copy in halo:
+        copy.wait_send()
+
+
+def attention_backward(
+    full_a,
+    full_b,
+    side_part,
+    grad_one_b,
+    grad_one,
+    tokens,
+    mixed,
+    query,
+    key_rows,
+    value_rows,
+    projected,
+    gains,
+    cosine,
+    sine,
+    position,
+):
     count = lax.axis_size("fsdp")
     chain = count // PLANE
+    rows, depth = tokens.shape
+    weight_rows, out_width = full_b.shape[0] // count, full_b.shape[1]
     dma = pltpu.SemaphoreType.DMA
-    scratch, outs, parts = [], [], []
-    for part in (part_a, part_b):
-        rows, width = part.shape[0] // count, part.shape[1]
-        cut = half_split(width)
-        shapes = [
-            (chain, 2, 2, rows, width),
-            (chain, 2, 2, rows, width),
-            (chain, rows, cut),
-            (chain, rows, width - cut),
-            (chain, rows, width),
-            (chain, rows, width),
-            (chain - 1, rows, width),
+    anywhere, vmem = pl.BlockSpec(memory_space=pl.ANY), pl.BlockSpec(memory_space=pltpu.VMEM)
+    blocked = [
+        array.reshape(chain, 2, 2, 2, weight_rows, array.shape[1])
+        for array in (full_a, full_b, side_part)
+    ]
+    kv_width = KVH * HD
+    return pl.pallas_call(
+        functools.partial(attention_backward_kernel, count),
+        out_shape=[
+            jax.ShapeDtypeStruct((weight_rows, out_width), F32),
+            jax.ShapeDtypeStruct((rows, QKV_WIDTH), BF16),
+            jax.ShapeDtypeStruct((rows, depth), BF16),
+            jax.ShapeDtypeStruct((1, depth), F32),
+            jax.ShapeDtypeStruct((1, 2 * HD), F32),
+        ],
+        in_specs=[anywhere] * 3 + [vmem] * 12,
+        out_specs=[vmem] * 5,
+        scratch_shapes=[
+            pltpu.VMEM((chain, 2, 2, 2, weight_rows, QKV_WIDTH), BF16),
+            pltpu.VMEM((rows, HQ * HD), BF16),
+            pltpu.VMEM((rows, depth), F32),
+            pltpu.VMEM((3, rows, kv_width), F32),
+            pltpu.VMEM((3, rows, kv_width), F32),
+            pltpu.VMEM((4, rows, kv_width), BF16),
+            pltpu.VMEM((4, rows, kv_width), BF16),
+            dma,
+            dma((chain,)),
+            dma((4,)),
+            dma((4,)),
         ]
-        scratch += [pltpu.VMEM(shape, BF16) for shape in shapes] + [dma((chain,))] * 13
-        outs.append(jax.ShapeDtypeStruct((rows, width), F32))
-        parts.append(part.reshape(chain, 2, 2, 2, rows, width))
+        + scatter_scratch(chain, weight_rows, out_width),
+        compiler_params=pltpu.CompilerParams(
+            collective_id=1, has_side_effects=True, vmem_limit_bytes=62 * 2**20
+        ),
+        cost_estimate=pl.CostEstimate(
+            flops=40 * 10**9, bytes_accessed=180 * 2**20, transcendentals=0
+        ),
+        name="attention_backward",
+    )(
+        *blocked,
+        grad_one_b,
+        grad_one,
+        tokens,
+        mixed,
+        query,
+        key_rows,
+        value_rows,
+        projected,
+        gains,
+        cosine,
+        sine,
+        position,
+    )
+
+
+def qkv_scatter_kernel(count, gain_part, normed, grad_projected, out_sum, gain_sem, part, *scratch):
+    chain = count // PLANE
+    scatter = WeightScatter(chain, part, out_sum, *scratch)
+    greet(scatter.partners)
+    width = grad_projected.shape[1]
+    places = []
+    for s in range(chain):
+        places.append(
+            pltpu.make_async_copy(
+                gain_part.at[scatter.blocks[s]],
+                part.at[s, :, :, :, :, pl.ds(width, LANES)],
+                gain_sem.at[s],
+            )
+        )
+        places[-1].start()
+    tile = normed.shape[1] // chain
+    block_shape = part.shape[1:5]
+    for i in range(chain + 3):
+        if i < chain:
+            s = scatter.order[i]
+            left = normed[:, pl.ds(pl.multiple_of(scatter.blocks[s] * tile, tile), tile)]
+
+            @pl.loop(0, width // 512)
+            def _(n):
+                at = pl.ds(pl.multiple_of(n * 512, 512), 512)
+                part[s, :, :, :, :, at] = (
+                    dot_tn(left, grad_projected[:, at]).astype(BF16).reshape(block_shape + (512,))
+                )
+
+            places[s].wait()
+            scatter.cross(i)
+        if 1 <= i <= chain:
+            scatter.halve(i - 1)
+        if 2 <= i <= chain + 1:
+            scatter.sideways(i - 2)
+        if i >= 3:
+            scatter.finish(i - 3)
+    scatter.total()
+
+
+def qkv_scatter(gain_part, normed, grad_projected):
+    count = lax.axis_size("fsdp")
+    chain = count // PLANE
+    weight_rows, width = normed.shape[1] // count, grad_projected.shape[1] + LANES
+    vmem = pl.BlockSpec(memory_space=pltpu.VMEM)
     return pl.pallas_call(
-        functools.partial(scatter_kernel, chain),
-        out_shape=outs,
-        in_specs=[pl.BlockSpec(memory_space=pl.ANY)] * 2,
-        out_specs=[pl.BlockSpec(memory_space=pltpu.VMEM)] * 2,
-        scratch_shapes=scratch,
+        functools.partial(qkv_scatter_kernel, count),
+        out_shape=jax.ShapeDtypeStruct((weight_rows, width), F32),
+        in_specs=[pl.BlockSpec(memory_space=pl.ANY)] + [vmem] * 2,
+        out_specs=vmem,
+        scratch_shapes=[pltpu.SemaphoreType.DMA((chain,))]
+        + scatter_scratch(chain, weight_rows, width),
         compiler_params=pltpu.CompilerParams(
-            collective_id=1, has_side_effects=True, vmem_limit_bytes=56 * 2**20
+            collective_id=4, has_side_effects=True, vmem_limit_bytes=48 * 2**20
         ),
-        name="scatter_weights",
-    )(*parts)
+        cost_estimate=pl.CostEstimate(
+            flops=40 * 10**9, bytes_accessed=180 * 2**20, transcendentals=0
+        ),
+        name="qkv_scatter",
+    )(gain_part.reshape(chain, 2, 2, 2, weight_rows, LANES), normed, grad_projected)
 
 
 class TokenCube:
@@ -443,15 +1017,15 @@
 
 
 def load_weights(blocks, held, sems):
-    rows = blocks[0].shape[1]
+    rows = blocks.shape[2]
     loads = []
     for m in (2, 0, 1):
         loads.append(
             [
                 pltpu.make_async_copy(
-                    block.at[m], held.at[m, pl.ds(i * rows, rows)], sems.at[m, i]
+                    blocks.at[i, m], held.at[m, pl.ds(i * rows, rows)], sems.at[m, i]
                 )
-                for i, block in enumerate(blocks)
+                for i in range(blocks.shape[0])
             ]
         )
         for load in loads[-1]:
@@ -479,11 +1053,10 @@
 WIDTH_TILE = 1024
 
 
-def ffn_forward_kernel(n_blocks, own, *refs):
-    blocks = refs[:n_blocks]
-    out, held_out, gate_out, up_out, weights, gate_st, up_st, act = refs[n_blocks : n_blocks + 8]
-    load_sem, save_sem, keep_sem = refs[n_blocks + 8 : n_blocks + 11]
-    held, part, in_half, in_x, in_y, in_z, gs, gr, ss, sr, own_sem = refs[n_blocks + 11 :]
+def ffn_forward_kernel(own, blocks, *refs):
+    out, held_out, gate_out, up_out, weights, gate_st, up_st, act = refs[:8]
+    load_sem, save_sem, keep_sem = refs[8:11]
+    held, part, in_half, in_x, in_y, in_z, gs, gr, ss, sr, own_sem = refs[11:]
     cube = TokenCube(own, held, part, in_half, in_x, in_y, in_z, gs, gr, ss, sr)
     greet(cube.partners)
     cube.start("zt", "zl", "x", "y")
@@ -563,25 +1136,25 @@
 
 def ffn_forward(own, blocks):
     rows, width = own.shape
-    hidden = blocks[0].shape[1] * len(blocks)
+    hidden = blocks.shape[0] * blocks.shape[2]
     dma = pltpu.SemaphoreType.DMA
     anywhere = pl.BlockSpec(memory_space=pl.ANY)
     return pl.pallas_call(
-        functools.partial(ffn_forward_kernel, len(blocks)),
+        ffn_forward_kernel,
         out_shape=[
             jax.ShapeDtypeStruct((rows, width), F32),
             jax.ShapeDtypeStruct((8, rows, width), BF16),
             jax.ShapeDtypeStruct((8, rows, hidden), F32),
             jax.ShapeDtypeStruct((8, rows, hidden), F32),
         ],
-        in_specs=[anywhere] * (1 + len(blocks)),
+        in_specs=[anywhere] * 2,
         out_specs=[pl.BlockSpec(memory_space=pltpu.VMEM)] + [anywhere] * 3,
         scratch_shapes=[
             pltpu.VMEM((3, hidden, width), BF16),
             pltpu.VMEM((2, rows, hidden), F32),
             pltpu.VMEM((2, rows, hidden), F32),
             pltpu.VMEM((rows, hidden), BF16),
-            dma((3, len(blocks))),
+            dma((3, blocks.shape[0])),
             dma((2, 2)),
             dma,
         ]
@@ -593,14 +1166,13 @@
             flops=48 * rows * width * hidden, bytes_accessed=300 * 2**20, transcendentals=0
         ),
         name="ffn_forward",
-    )(own, *blocks)
-
-
-def ffn_backward_kernel(n_blocks, own, normed, gate_in, up_in, *refs):
-    blocks = refs[:n_blocks]
-    out, mine, theirs, weights, gate_st, up_st, grads, stage = refs[n_blocks : n_blocks + 8]
-    load_sem, read_sem, write_sem, normed_sem = refs[n_blocks + 8 : n_blocks + 12]
-    held, part, in_half, in_x, in_y, in_z, gs, gr, ss, sr, own_sem = refs[n_blocks + 12 :]
+    )(own, blocks)
+
+
+def ffn_backward_kernel(own, normed, gate_in, up_in, blocks, *refs):
+    out, mine, theirs, weights, gate_st, up_st, grads, stage = refs[:8]
+    load_sem, read_sem, write_sem, normed_sem = refs[8:12]
+    held, part, in_half, in_x, in_y, in_z, gs, gr, ss, sr, own_sem = refs[12:]
     cube = TokenCube(own, held, part, in_half, in_x, in_y, in_z, gs, gr, ss, sr)
     greet(cube.partners)
     cube.start("zt", "zl", "x", "y")
@@ -733,14 +1305,14 @@
 
 def ffn_backward(own, normed, gate, up, blocks):
     rows, width = own.shape
-    hidden = blocks[0].shape[1] * len(blocks)
+    hidden = blocks.shape[0] * blocks.shape[2]
     dma = pltpu.SemaphoreType.DMA
     anywhere = pl.BlockSpec(memory_space=pl.ANY)
     grad = jax.ShapeDtypeStruct((3, hidden // 2, width), BF16)
     return pl.pallas_call(
-        functools.partial(ffn_backward_kernel, len(blocks)),
+        ffn_backward_kernel,
         out_shape=[jax.ShapeDtypeStruct((rows, width), F32), grad, grad],
-        in_specs=[anywhere] * (4 + len(blocks)),
+        in_specs=[anywhere] * 5,
         out_specs=[pl.BlockSpec(memory_space=pltpu.VMEM), anywhere, anywhere],
         scratch_shapes=[
             pltpu.VMEM((3, hidden, width), BF16),
@@ -748,7 +1320,7 @@
             pltpu.VMEM((2, rows, hidden), F32),
             pltpu.VMEM((3, 8 * rows, hidden), BF16),
             pltpu.VMEM((2, 256, width), BF16),
-            dma((3, len(blocks))),
+            dma((3, blocks.shape[0])),
             dma((2, 2)),
             dma((2,)),
             dma,
@@ -761,7 +1333,7 @@
             flops=96 * rows * width * hidden, bytes_accessed=400 * 2**20, transcendentals=0
         ),
         name="ffn_backward",
-    )(own, normed.reshape(8 * rows // hidden, hidden, width), gate, up, *blocks)
+    )(own, normed.reshape(8 * rows // hidden, hidden, width), gate, up, blocks)
 
 
 def passed_along(block, axis, distance):
@@ -828,22 +1400,6 @@
     return lax.dot_general(
         left_op, right_op, (((1,), (1,)), ((), ())), preferred_element_type=jnp.float32
     )
-
-
-def split_gains(gain_all):
-    gain_f = gain_all.astype(jnp.float32)
-    return (gain_f[:D], gain_f[D : 2 * D], gain_f[2 * D : 2 * D + HD], gain_f[2 * D + HD :])
-
-
-def soft_weights(query_four, key_rows, allowed, score_scale):
-    scores = (
-        jnp.einsum("qkgd,nkd->kgqn", query_four, key_rows, preferred_element_type=jnp.float32)
-        * score_scale
-    )
-    scores = jnp.where(allowed[None, None], scores, NEGATIVE)
-    highest = jnp.max(scores, axis=-1, keepdims=True)
-    exponent = jnp.exp(scores - highest)
-    return exponent / jnp.sum(exponent, axis=-1, keepdims=True)
 
 
 def local(
@@ -864,6 +1420,7 @@
     segment, position = layout(seq_lengths, seq_order, token_index)
     cosine, sine = angles(position)
     reach = (WINDOW + tok_rows - 2) // tok_rows
+    assert reach == 2
     key_index = jnp.concatenate(
         [token_index - distance * tok_rows for distance in range(reach, 0, -1)] + [token_index]
     )
@@ -878,51 +1435,32 @@
     count = lax.axis_size("fsdp")
     bits = weight_bits(count)
     weight_rows = qkv_weight.shape[0]
-    gain_block = jnp.pad(norm_gains, (0, weight_rows * LANES - norm_gains.shape[0]))
-    qkv_gathered, out_gathered = gather_weights(
-        jnp.concatenate([qkv_weight, gain_block.reshape(weight_rows, LANES)], axis=1),
+    (
+        qkv_gathered,
+        out_gathered,
+        ffn_blocks,
+        gain_all,
+        normed_b,
+        projected,
+        query_b,
+        key_blocks,
+        value_blocks,
+        mixed_b,
+        first_sum,
+        normed_two,
+    ) = attention_forward(
+        jnp.concatenate([qkv_weight, placed_gains(norm_gains, weight_rows)], axis=1),
         jnp.concatenate([out_weight, side_weights], axis=1),
-    )
-    ffn_own, qkv_gathered = lax.optimization_barrier((ffn_weights, qkv_gathered))
-    ffn_blocks = [ffn_own.transpose(1, 0, 2)]
-    for bit in bits:
-        ffn_blocks += [swapped(block, bit) for block in ffn_blocks]
+        ffn_weights.transpose(1, 0, 2),
+        tokens,
+        cosine[:, 0, : HD // 2],
+        sine[:, 0, : HD // 2],
+        position[:, None],
+    )
     qkv_all = qkv_gathered[:, : qkv_weight.shape[1]]
     out_all, side_all = out_gathered[:, :D], out_gathered[:, D:]
-    gain_all = (
-        qkv_gathered[:, qkv_weight.shape[1] :]
-        .reshape(count, weight_rows * LANES)[:, : norm_gains.shape[0]]
-        .reshape(-1)
-    )
-    attn_gain, ffn_gain, query_gain, key_gain = split_gains(gain_all)
-    tokens_f = tokens.astype(jnp.float32)
-    rms_one = inv_rms(tokens_f)
-    normed_b = (tokens_f * rms_one * attn_gain).astype(jnp.bfloat16)
-    projected = jnp.dot(normed_b, qkv_all, preferred_element_type=jnp.float32)
-    query = projected[:, :query_width].reshape(tok_rows, HQ, HD)
-    key_raw = projected[:, query_width : query_width + kv_width].reshape(tok_rows, KVH, HD)
-    value_raw = projected[:, query_width + kv_width :].reshape(tok_rows, KVH, HD)
-    rms_query = inv_rms(query)
-    rms_key = inv_rms(key_raw)
-    query_b = rotate(query * rms_query * query_gain, cosine, sine).astype(jnp.bfloat16)
-    key_b = rotate(key_raw * rms_key * key_gain, cosine, sine).astype(jnp.bfloat16)
-    value_b = value_raw.astype(jnp.bfloat16)
-    key_parts = []
-    value_parts = []
-    for distance in range(reach, 0, -1):
-        moved_keys, moved_values = passed_along((key_b, value_b), "fsdp", distance)
-        key_parts.append(moved_keys)
-        value_parts.append(moved_values)
-    key_rows = jnp.concatenate(key_parts + [key_b], axis=0)
-    value_rows = jnp.concatenate(value_parts + [value_b], axis=0)
-    query_four = query_b.reshape(tok_rows, KVH, group_size, HD)
-    probs = soft_weights(query_four, key_rows, allowed, score_scale)
-    probs_b = probs.astype(jnp.bfloat16)
-    mixed = jnp.einsum("kgqn,nkd->qkgd", probs_b, value_rows, preferred_element_type=jnp.float32)
-    mixed_b = mixed.reshape(tok_rows, query_width).astype(jnp.bfloat16)
-    first_sum = tokens_f + jnp.dot(mixed_b, out_all, preferred_element_type=jnp.float32)
+    ffn_gain = gain_all[0, D : 2 * D]
     rms_two = inv_rms(first_sum)
-    normed_two = (first_sum * rms_two * ffn_gain).astype(jnp.bfloat16)
     ffn_out, normed_all, gate_kept, up_kept = ffn_forward(normed_two, ffn_blocks)
     second_sum = first_sum + ffn_out
     second_b = second_sum.astype(jnp.bfloat16)
@@ -941,7 +1479,7 @@
     grad_per = pull_per(grad_comb[:, :PL] * per_f)[0]
     grad_side = jnp.concatenate([grad_per, grad_comb[:, PL:]], axis=1).astype(jnp.bfloat16)
     side_in_grad = contract_rows(second_b, grad_side)
-    side_grad_full = jnp.concatenate([side_in_grad, side_out_grad], axis=1)
+    side_grad_full = jnp.concatenate([side_in_grad, side_out_grad], axis=1).astype(BF16)
     grad_two = grad_y + contract_cols(grad_side, back_side[:, :split_at])
     grad_two_b = grad_two.astype(jnp.bfloat16)
     grad_h2, ffn_part, ffn_sent = ffn_backward(
@@ -957,74 +1495,29 @@
     ffn_gain_grad = jnp.sum(grad_h2 * first_sum * rms_two, axis=0)
     grad_one = grad_two + norm_back(grad_h2, first_sum, rms_two, ffn_gain)
     grad_one_b = grad_one.astype(jnp.bfloat16)
-    out_grad_full = contract_rows(mixed_b, grad_one_b)
-    grad_mixed_b = contract_cols(grad_one_b, back_out).astype(jnp.bfloat16)
-    grad_mixed_four = grad_mixed_b.reshape(tok_rows, KVH, group_size, HD)
-    probs_again = soft_weights(query_four, key_rows, allowed, score_scale)
-    probs_again_b = probs_again.astype(jnp.bfloat16)
-    grad_probs = jnp.einsum(
-        "qkgd,nkd->kgqn", grad_mixed_four, value_rows, preferred_element_type=jnp.float32
-    )
-    row_delta = jnp.sum(probs_again * grad_probs, axis=-1, keepdims=True)
-    grad_scores_b = (probs_again * (grad_probs - row_delta)).astype(jnp.bfloat16)
-    grad_query_rot = (
-        jnp.einsum("kgqn,nkd->qkgd", grad_scores_b, key_rows, preferred_element_type=jnp.float32)
-        * score_scale
-    )
-    grad_keys = (
-        jnp.einsum("kgqn,qkgd->nkd", grad_scores_b, query_four, preferred_element_type=jnp.float32)
-        * score_scale
-    )
-    grad_values = jnp.einsum(
-        "kgqn,qkgd->nkd", probs_again_b, grad_mixed_four, preferred_element_type=jnp.float32
-    )
-    local_keys = grad_keys[reach * tok_rows :]
-    local_values = grad_values[reach * tok_rows :]
-    for distance in range(1, reach + 1):
-        first_row = (reach - distance) * tok_rows
-        back_keys, back_values = (
-            passed_along(
-                grad_keys[first_row : first_row + tok_rows].astype(jnp.bfloat16), "fsdp", -distance
-            ).astype(jnp.float32),
-            passed_along(
-                grad_values[first_row : first_row + tok_rows].astype(jnp.bfloat16),
-                "fsdp",
-                -distance,
-            ).astype(jnp.float32),
-        )
-        local_keys = local_keys + back_keys
-        local_values = local_values + back_values
-    grad_query_norm = rotate_back(grad_query_rot.reshape(tok_rows, HQ, HD), cosine, sine)
-    query_gain_grad = jnp.sum(grad_query_norm * query * rms_query, axis=(0, 1))
-    grad_query = norm_back(grad_query_norm, query, rms_query, query_gain)
-    grad_key_norm = rotate_back(local_keys, cosine, sine)
-    key_gain_grad = jnp.sum(grad_key_norm * key_raw * rms_key, axis=(0, 1))
-    grad_key = norm_back(grad_key_norm, key_raw, rms_key, key_gain)
-    grad_projected = jnp.concatenate(
-        [
-            grad_query.reshape(tok_rows, query_width),
-            grad_key.reshape(tok_rows, kv_width),
-            local_values.reshape(tok_rows, kv_width),
-        ],
-        axis=1,
-    ).astype(jnp.bfloat16)
-    qkv_grad_full = contract_rows(normed_b, grad_projected)
-    grad_normed = contract_cols(grad_projected, back_qkv)
-    attn_gain_grad = jnp.sum(grad_normed * tokens_f * rms_one, axis=0)
-    input_grad = (grad_one + norm_back(grad_normed, tokens_f, rms_one, attn_gain)).astype(
-        jnp.bfloat16
-    )
-    gains_grad_full = jnp.concatenate(
-        [attn_gain_grad, ffn_gain_grad, query_gain_grad, key_gain_grad]
-    )
+    out_sum, grad_projected, input_grad, attn_gain_grad, head_gain_grad = attention_backward(
+        qkv_gathered,
+        out_gathered,
+        side_grad_full,
+        grad_one_b,
+        grad_one,
+        tokens,
+        mixed_b,
+        query_b,
+        key_blocks,
+        value_blocks,
+        projected,
+        gain_all,
+        cosine[:, 0, : HD // 2],
+        sine[:, 0, : HD // 2],
+        position[:, None],
+    )
+    gains_grad_full = jnp.concatenate([attn_gain_grad[0], ffn_gain_grad, head_gain_grad[0]])
     gain_rows = jnp.pad(
         gains_grad_full.astype(BF16).reshape(count, -1),
         ((0, 0), (0, weight_rows * LANES - norm_gains.shape[0])),
     ).reshape(count * weight_rows, LANES)
-    qkv_sum, out_sum = scatter_weights(
-        jnp.concatenate([qkv_grad_full.astype(BF16), gain_rows], axis=1),
-        jnp.concatenate([out_grad_full.astype(BF16), side_grad_full.astype(BF16)], axis=1),
-    )
+    qkv_sum = qkv_scatter(gain_rows, normed_b, grad_projected)
     qkv_grad = qkv_sum[:, : qkv_weight.shape[1]]
     gains_grad = qkv_sum[:, qkv_weight.shape[1] :].reshape(-1)[: norm_gains.shape[0]]
     out_grad, side_grad = out_sum[:, :D], out_sum[:, D:]

time: 850 us -> 778 us (0.915)
  Pallas kernels: 562 us -> 691 us
  matrix products: 85.2 us -> 16.9 us
  local copies, waits for them, and re-layouts: 77.1 us -> 19 us
  other arithmetic: 83.3 us -> 36.6 us
  starting transfers between devices: 27.1 us -> 0.62 us
    pallas_call x4 -> x5, Pallas kernels: 562 us -> 691 us  [the longest x1 190 us: ffn_forward(): pl.pallas_call(ffn_forward_kernel, out_shape=[jax.ShapeDtypeStruct((rows,...]
    dot_general x7 -> x0, matrix products: 36.5 us -> none  [the longest x1 7.68 us: local(): jnp.einsum('qkgd,nkd->kgqn', grad_mixed_four, value_rows, preferred_eleme...]
    concatenate x6 -> x4, other arithmetic: 28.8 us -> 4.49 us  [the longest x1 2.6 us: local(): jnp.concatenate([side_in_grad, side_out_grad], axis=1).astype(BF16)]
    ppermute x8 -> x0, starting transfers between devices: 18.6 us -> none  [passed_along(): return lax.ppermute(block, axis, route)]
    concatenate x3 -> x0, local copies, waits for them, and re-layouts: 18.3 us -> none  [the longest x1 14.1 us: local(): jnp.concatenate([out_grad_full.astype(BF16), side_grad_full.astype(BF16)]...]
    unnamed x176 -> x29, local copies, waits for them, and re-layouts: 20.7 us -> 4.34 us
    dot_general x4 -> x2, matrix products: 20.5 us -> 7.33 us  [contract_cols(): lax.dot_general(left_op, right_op, (((1,), (1,)), ((), ())), preferred_el...]
    reshape x9 -> x0, local copies, waits for them, and re-layouts: 11.3 us -> none  [the longest x2 5.31 us: local(): grad_query_rot.reshape(tok_rows, HQ, HD)]
  transfers between devices with their start and end apart: 13 -> 2, of which waited for: 1 -> 0; matrix products, arithmetic and copies ran while one was open for 22% -> 3% of each run, Pallas kernels for 13% -> 23%
where the time goes in v4:
time: 778 us; the launch traced here: 766 us
  Pallas kernels  691 us (89%)
  other arithmetic  36.6 us (5%)
  local copies, waits for them, and re-layouts  19 us (2%)
  matrix products  16.9 us (2%)
    pallas_call x1, Pallas kernels, ffn_forward(): pl.pallas_call(ffn_forward_kernel, out_shape=[jax.ShapeDtypeStruct((rows,...  190 us
    pallas_call x1, Pallas kernels, attention_forward(): pl.pallas_call(functools.partial(attention_forward_kernel, count), out_sh...  163 us
    pallas_call x1, Pallas kernels, ffn_backward(): pl.pallas_call(ffn_backward_kernel, out_shape=[jax.ShapeDtypeStruct((rows...  160 us
    pallas_call x1, Pallas kernels, qkv_scatter(): pl.pallas_call(functools.partial(qkv_scatter_kernel, count), out_shape=ja...  92.7 us
    pallas_call x1, Pallas kernels, attention_backward(): pl.pallas_call(functools.partial(attention_backward_kernel, count), out_s...  85.3 us
  transfers between devices with their start and end apart: 2, of which 0 were waited for; matrix products, arithmetic and copies ran while one was open for 3% of the time, Pallas kernels for 23%

profile of v4, /device:TPU:0, one launch (start us, length us, event | category | flops | bytes accessed | tf_op | source)
XLA Modules:
  0.0 765.9 jit_solution(8095846300090755941)
XLA Ops:
  0.7 0.9 select_reduce_fusion.2
  1.5 0.1 select_reduce_fusion.1
  1.6 0.1 select_reduce_fusion
  1.7 0.1 multiply_bitcast_fusion
  1.9 1.2 fusion.26
  3.0 0.1 copy.27
  3.2 0.7 add_subtract_fusion.position
  3.8 0.8 dynamic_update_slice.3
  4.7 1.8 pad_maximum_fusion.1.own_a
  6.5 1.7 pad_maximum_fusion.2.own_b
  8.2 163.3 %attention_forward.1 = (bf16[4,2,2,2,64,3200]{5,4,3,2,1,0:T(8,128)(2,1)}, bf16[4,2,2,2,64,2688]{5,4,3,2,1,0:T(8,128)(2,1)}, bf16[4,3,256,2048]{3,2,1,0:T(8,128)(...) custom-call(bf16[64,3200]{1,0:T(8,128)(2,1)} %pad_maximum_fusion.1.o, ...), custom_call_target="tpu_custom_call" | custom-call | tf_op jit(solution)/shard_map/attention_forward/pallas_call | solution.py:378
  171.5 0.0 copy-start.4
  171.5 190.5 %ffn_forward.1 = (f32[256,2048]{1,0:T(8,128)}, bf16[8,256,2048]{2,1,0:T(8,128)(2,1)}, f32[8,256,1024]{2,1,0:T(8,128)}, f32[8,256,1024]{2,1,0:T(8,128)}) custom-call(bf16[256,2048]{1,0:T(8,128)(2,1)} %get-tuple-element.33.own, bf16[4,3,256,2048]{3,2,1,0:T(8,128)(2,1)} %get-tuple-element.34.blocks), custom_call_target="tpu_custom_call" | custom-call | flops 25769803776 | bytes 314572800 | tf_op jit(solution)/shard_map/ffn_forward/pallas_call | solution.py:1142
  362.0 0.0 copy-done.4
  362.0 1.9 multiply_reduce_fusion.2
  363.9 0.0 copy-start.8
  363.9 1.3 copy-done.2
  365.3 2.1 fusion.7
  367.4 0.0 copy-done.8
  367.4 0.0 copy-start.11
  367.4 2.5 fusion.9
  370.0 0.0 copy-done.11
  370.0 0.1 copy.28
  370.1 0.9 multiply_convert_fusion
  371.0 3.8 fusion.32
  374.8 159.6 %ffn_backward.1 = (f32[256,2048]{1,0:T(8,128)}, bf16[3,512,2048]{2,1,0:T(8,128)(2,1)}, bf16[3,512,2048]{2,1,0:T(8,128)(2,1)}) custom-call(bf16[256,2048]{1,0:T(8,128)(2,1)} %get-tuple-element.93.own, bf16[2,1024,2048]{2,1,0:T(8,128)(2,1)} %bitcast.40, f32[8,256,1024]{2,1,0:T(8,128)} %get-tuple-element.39.gate_in, f32[8,256,1024]{2,1,0:T(8,128)} %get-tuple-element.40.up_in, ...), custom_call_target="tpu_custom_call" | custom-call | flops 51539607552 | bytes 419430400 | tf_op jit(solution)/shard_map/ffn_backward/pallas_call | solution.py:1312
  534.4 0.1 collective-permute-start
  534.5 0.7 slice.67
  535.2 2.1 convolution_convert_fusion
  537.3 0.8 copy.29
  538.1 2.8 fusion.2
  540.9 2.0 copy.30
  543.0 0.0 copy-start.5
  543.0 0.0 copy-start.7
  543.0 2.6 pad_maximum_fusion.side_part
  545.6 0.0 copy-done.5
  545.6 0.0 copy-done.7
  545.6 0.0 copy-start.6
  545.6 0.6 multiply_reduce_fusion
  546.2 1.0 copy-done.6
  547.2 2.3 fusion.31
  549.5 85.3 %attention_backward.1 = (f32[64,2688]{1,0:T(8,128)}, bf16[256,3072]{1,0:T(8,128)(2,1)}, bf16[256,2048]{1,0:T(8,128)(2,1)}, f32[1,2048]{1,0:T(1,128)}, f32[1,512]{1,0:T(1,128)}) custom-call(bf16[4,2,2,2,64,3200]{5,4,3,2,1,0:T(8,128)(2,1)} %get-tuple-element.37.full_a, bf16[4,2,2,2,64,2688]{5,4,3,2,1,0:T(8,128)(2,1)} %get-tuple-element.36.full_b, ...), custom_call_target="tpu_custom_call" | custom-call | flops 40000000000 | bytes 188743680 | tf_op jit(solution)/shard_map/attention_backward/pallas_call | solution.py:795
  634.9 1.9 slice.69
  636.7 1.6 slice.72
  638.3 0.7 convert_reduce_fusion.1
  639.0 0.7 convert_reduce_fusion
  639.8 0.1 convert_element_type.61
  639.9 0.1 copy.32
  640.0 0.0 collective-permute-done
  640.0 12.2 %convert_add_fusion = f32[3,512,2048]{2,1,0:T(8,128)} fusion(bf16[3,512,2048]{2,1,0:T(8,128)(2,1)} %collective-permute-done, bf16[3,512,2048]{2,1,0:T(8,128)(2,1)} %get-tuple-element.54), kind=kLoop, calls=%fused_computation | loop fusion | flops 9437184 | bytes 25165824 | tf_op jit(solution)/shard_map/add | solution.py:1489
  652.3 5.1 slice.126
  657.4 0.6 collective-permute-start.1
  657.9 0.0 copy-done
  657.9 0.0 copy-done.1
  657.9 92.7 %qkv_scatter.1 = f32[64,3200]{1,0:T(8,128)S(1)} custom-call(bf16[4,2,2,2,64,128]{5,4,3,2,1,0:T(8,128)(2,1)S(1)} %bitcast.28, bf16[256,2048]{1,0:T(8,128)(2,1)S(1)} %copy-done, bf16[256,3072]{1,0:T(8,128)(2,1)S(1)} %copy-done.1), custom_call_target="tpu_custom_call" | custom-call | flops 40000000000 | bytes 188743680 | tf_op jit(solution)/shard_map/qkv_scatter/pallas_call | solution.py:889
  750.7 0.9 slice.68
  751.6 0.6 slice.85
  752.2 0.0 copy-done.10
  752.2 0.8 copy.31
  752.9 3.5 fusion.1
  756.4 0.0 collective-permute-done.1
  756.5 8.0 %fusion = f32[256,3,2048]{2,0,1:T(8,128)} fusion(f32[3,512,2048]{2,1,0:T(8,128)} %convert_add_fusion, bf16[3,256,2048]{2,1,0:T(8,128)(2,1)} %collective-permute-done.1), kind=kLoop, calls=%fused_computation.3 | loop fusion | flops 3145728 | bytes 15728640 | tf_op jit(solution)/shard_map/transpose | solution.py:1494
  764.5 0.0 copy-done.9
  764.5 1.0 copy.35
  (18 shorter events, 0.1 us)
Async XLA Ops:
  171.5 190.5 %copy-start.4 = (f32[256,2048]{1,0:T(8,128)S(1)}, f32[256,2048]{1,0:T(8,128)}, u32[]{:S(2)}) copy-start(f32[256,2048]{1,0:T(8,128)} %get-tuple-element.32) | copy-start | bytes 6291460
  363.9 1.3 copy-start.2
  363.9 3.5 copy-start.8
  367.4 2.6 copy-start.11
  534.4 105.6 %collective-permute-start = (bf16[3,512,2048]{2,1,0:T(8,128)(2,1)}, bf16[3,512,2048]{2,1,0:T(8,128)(2,1)}, u32[]{:S(2)}, u32[]{:S(2)}) collective-permute-start(bf16[3,512,2048]{2,1,0:T(8,128)(2,1)} %get-tuple-element.55), channel_id=1, source_target_pairs={{0,1},{1,0},{2,3},{3,2},{4,5},{5,4},{6,7},{7,6},{8,9},{9,8},{10,11... | collective-permute-start | bytes 18874376 | tf_op jit(solution)/shard_map/ppermute | solution.py:37
  543.0 2.6 copy-start.5
  543.0 2.6 copy-start.7
  545.6 1.6 copy-start.6
  652.3 5.6 copy-start
  652.3 5.6 copy-start.1
  657.4 99.1 %collective-permute-start.1 = (bf16[3,256,2048]{2,1,0:T(8,128)(2,1)}, bf16[3,256,2048]{2,1,0:T(8,128)(2,1)}, u32[]{:S(2)}, u32[]{:S(2)}) collective-permute-start(bf16[3,256,2048]{2,1,0:T(8,128)(2,1)} %slice.126), channel_id=1, source_target_pairs={{0,8},{1,9},{2,10},{3,11},{4,12},{5,13},{6,14},{7,15},{8,0},{9,1},... | collective-permute-start | bytes 9437192 | tf_op jit(solution)/shard_map/ppermute | solution.py:37
  657.9 94.3 %copy-start.10 = (bf16[256,256]{0,1:T(8,128)(2,1)S(1)}, bf16[256,256]{0,1:T(8,128)(2,1)}, u32[]{:S(2)}) copy-start(bf16[256,256]{0,1:T(8,128)(2,1)} %get-tuple-element.86) | copy-start | bytes 393220
  657.9 95.0 %copy-start.3 = (f32[256,2048]{1,0:T(8,128)S(1)}, f32[256,2048]{1,0:T(8,128)}, u32[]{:S(2)}) copy-start(f32[256,2048]{1,0:T(8,128)} %copy-done.2) | copy-start | bytes 6291460
  756.4 8.0 %copy-start.9 = (bf16[256,2048]{1,0:T(8,128)(2,1)S(1)}, bf16[256,2048]{1,0:T(8,128)(2,1)}, u32[]{:S(2)}) copy-start(bf16[256,2048]{1,0:T(8,128)(2,1)} %get-tuple-element.104) | copy-start | bytes 3145732

commit v5 on v4

--- a/solution.py
+++ b/solution.py
@@ -106,17 +106,18 @@
         next_x, next_y, next_c = flipped(me, 2), flipped(me, 4), flipped(me, 1)
         z_peers = [me + (lax.rem(z_at + s, chain) - z_at) * PLANE for s in range(1, chain)]
         self.partners = [next_x, next_y, next_c] + z_peers
+        self.order = sorted(range(chain), key=lambda s: (min(s, chain - s), s))
         self.waves = []
         for own, out, (local, zs, zr, xs, xr, ys, yr, a_s, ar, bs, br, cs, cr) in pairs:
             cut = half_split(own.shape[-1])
             left, right = pl.ds(0, cut), pl.ds(cut, own.shape[-1] - cut)
             ops = {"own": pltpu.make_async_copy(own, out.at[z_at, y_at, x_at, core], local)}
-            ops["z"] = [
+            ops["z"] = [None] + [
                 remote(own, out.at[z_at, y_at, x_at, core], zs.at[s], zr.at[s], z_peers[s - 1])
-                for s in range(1, chain)
+                for s in self.order[1:]
             ]
             steps = []
-            for s in range(chain):
+            for s in self.order:
                 k = lax.rem(z_at + chain - s, chain)
                 here = out.at[k, y_at, x_at, core]
                 src = own if s == 0 else here
@@ -142,10 +143,14 @@
     def spread(self, w, s):
         ops = self.waves[w]
         if s == 0:
-            for copy in [ops["own"]] + ops["z"]:
+            ops["own"].start()
+        else:
+            ops["z"][s].wait_recv()
+        if w == 0 and s + 1 < len(ops["z"]):
+            ops["z"][s + 1].start()
+        if w > 0 and s == 0:
+            for copy in ops["z"][1:]:
                 copy.start()
-        else:
-            ops["z"][s - 1].wait_recv()
         ops["steps"][s]["x"].start()
         ops["steps"][s]["y"].start()
 
@@ -170,7 +175,7 @@
 
     def drain(self):
         for ops in self.waves:
-            for copy in ops["z"]:
+            for copy in ops["z"][1:]:
                 copy.wait_send()
             for step in ops["steps"]:
                 for name in "xyabc":
@@ -206,17 +211,36 @@
     chain = count // PLANE
     bits = weight_bits(count)
     gather = WeightGather(chain, ((own_a, wa, sems[:13]), (own_b, wb, sems[13:26])))
-    ffn_local, ffn_s, ffn_r, halo_s, halo_r, save = sems[26:]
+    first_s, first_r, ffn_s, ffn_r, rest_s, rest_r, halo_s, halo_r, save = sems[26:]
     ahead = [lax.rem(me + d, count) for d in (1, 2)]
     behind = [lax.rem(me + count - d, count) for d in (1, 2)]
     greet(gather.partners + [flipped(me, bit) for bit in bits[:-1]] + ahead + behind)
-    ffn_own = pltpu.make_async_copy(own_ffn, full_ffn.at[0], ffn_local)
-    ffn_copies = []
-    for i, bit in enumerate(bits):
-        size = 1 << i
-        src = own_ffn if i == 0 else full_ffn.at[pl.ds(0, size)]
-        dst = full_ffn.at[1] if i == 0 else full_ffn.at[pl.ds(size, size)]
-        ffn_copies.append(remote(src, dst, ffn_s.at[i], ffn_r.at[i], flipped(me, bit)))
+    ffn_first, ffn_copies, ffn_rest = [], [], []
+    piece = own_ffn.shape[1] // FFN_PIECES
+    for j in range(2 * FFN_PIECES):
+        at = pl.ds(j % FFN_PIECES * piece, piece)
+        m = j // FFN_PIECES
+        ffn_first.append(
+            remote(
+                own_ffn.at[m, at],
+                full_ffn.at[1, m, at],
+                first_s.at[j],
+                first_r.at[j],
+                flipped(me, bits[0]),
+            )
+        )
+    for i, bit in enumerate(bits[1:]):
+        size, partner = 2 << i, flipped(me, bit)
+        ffn_copies.append(remote(own_ffn, full_ffn.at[size], ffn_s.at[i], ffn_r.at[i], partner))
+        ffn_rest.append(
+            remote(
+                full_ffn.at[pl.ds(1, size - 1)],
+                full_ffn.at[pl.ds(size + 1, size - 1)],
+                rest_s.at[i],
+                rest_r.at[i],
+                partner,
+            )
+        )
     halo = []
     for d in (1, 2):
         for j, rows in enumerate((key_rows, value_rows)):
@@ -231,11 +255,14 @@
         if s >= 2:
             gather.across(0, s - 2)
     gather.spread(1, 0)
-    ffn_own.start()
+    for copy in ffn_first + ffn_copies:
+        copy.start()
     gather.pass_on(0, chain - 1)
     gather.across(0, chain - 2)
     gather.across(0, chain - 1)
     gather.complete(0)
+    for s in range(1, chain):
+        gather.spread(1, s)
     keep_a = pltpu.make_async_copy(wa, full_a, save.at[0])
     keep_a.start()
 
@@ -284,13 +311,16 @@
     value_rows[2] = projected[:, query_width + kv_width :].astype(BF16)
     for copy in halo:
         copy.start()
-    gather.pass_on(1, 0)
-    gather.spread(1, 1)
-    ffn_copies[0].start()
+    for s in range(chain - 3):
+        gather.pass_on(1, s)
 
     @pl.loop(0, query_width // 512)
     def _(n):
         project(n)
+
+    gather.pass_on(1, chain - 3)
+    for s in range(chain - 3):
+        gather.across(1, s)
 
     @pl.loop(0, HQ)
     def _(h):
@@ -301,9 +331,8 @@
             field * head_norm(field) * query_gain, cosine[...], sine[...]
         ).astype(BF16)
 
-    gather.pass_on(1, 1)
-    gather.spread(1, 2)
-    gather.across(1, 0)
+    gather.pass_on(1, chain - 2)
+    gather.across(1, chain - 3)
     for copy in halo:
         copy.wait_recv()
     n_keys = 3 * rows
@@ -324,16 +353,13 @@
             probs = soft_rows(query[:, at], keys, reach, gap).astype(BF16)
             mixed[:, at] = jnp.dot(probs, values, preferred_element_type=F32).astype(BF16)
 
-    heads(0, 2)
-    for s in range(3, chain):
-        gather.pass_on(1, s - 1)
-        gather.spread(1, s)
-        gather.across(1, s - 2)
-    heads(2, 5)
+    heads(0, 1)
     gather.pass_on(1, chain - 1)
+    heads(1, 2)
     gather.across(1, chain - 2)
-    heads(5, 8)
+    heads(2, 4)
     gather.across(1, chain - 1)
+    heads(4, 8)
     gather.complete(1)
     keep_b = pltpu.make_async_copy(wb, full_b, save.at[1])
     keep_b.start()
@@ -352,18 +378,20 @@
         field = first_sum[at]
         normed_two[at] = (field * head_norm(field) * gains[:, depth : 2 * depth]).astype(BF16)
 
-    ffn_own.wait()
-    for i, copy in enumerate(ffn_copies):
-        if i > 0:
-            copy.start()
+    for copy in ffn_first:
         copy.wait_recv()
-    for copy in ffn_copies + halo:
+    for copy, rest in zip(ffn_copies, ffn_rest):
+        rest.start()
+        copy.wait_recv()
+        rest.wait_recv()
+    for copy in ffn_first + ffn_copies + ffn_rest + halo:
         copy.wait_send()
     gather.drain()
     keep_a.wait()
     keep_b.wait()
 
 
+FFN_PIECES = 2
 QKV_WIDTH = (HQ + 2 * KVH) * HD
 
 
@@ -395,7 +423,8 @@
         out_specs=[anywhere] * 3 + [vmem] * 9,
         scratch_shapes=[pltpu.VMEM(shape_a, BF16), pltpu.VMEM(shape_b, BF16)]
         + ([dma] + [dma((chain,))] * 12) * 2
-        + [dma, dma((len(weight_bits(count)),)), dma((len(weight_bits(count)),))]
+        + [dma((2 * FFN_PIECES,))] * 2
+        + [dma((len(weight_bits(count)) - 1,))] * 4
         + [dma((4,)), dma((4,)), dma((2,))],
         compiler_params=pltpu.CompilerParams(
             collective_id=0, has_side_effects=True, vmem_limit_bytes=58 * 2**20
@@ -544,15 +573,18 @@
     count,
     full_a,
     full_b,
-    side_part,
+    grad_one_in,
+    tokens_in,
+    query_in,
+    key_in,
+    value_in,
+    projected_in,
     grad_one_b,
-    grad_one,
-    tokens,
     mixed,
-    query,
-    key_rows,
-    value_rows,
-    projected,
+    second,
+    grad_side,
+    cotangent,
+    combined,
     gains,
     cosine,
     sine,
@@ -569,8 +601,14 @@
     grad_values,
     halo_out,
     halo_in,
+    grad_one,
+    tokens,
+    query,
+    key_rows,
+    value_rows,
+    projected,
     weight_sem,
-    side_sem,
+    fill_sem,
     halo_s,
     halo_r,
     part,
@@ -591,20 +629,26 @@
         weight_sem,
     )
     load_out.start()
-    sides = []
-    for s in range(chain):
-        sides.append(
-            pltpu.make_async_copy(
-                side_part.at[scatter.blocks[s]],
-                part.at[s, :, :, :, :, pl.ds(out_width, part.shape[-1] - out_width)],
-                side_sem.at[s],
+    fills = [
+        pltpu.make_async_copy(src, dst, fill_sem.at[i])
+        for i, (src, dst) in enumerate(
+            (
+                (query_in, query),
+                (key_in, key_rows),
+                (value_in, value_rows),
+                (projected_in, projected),
+                (tokens_in, tokens),
+                (grad_one_in, grad_one),
             )
         )
-        sides[-1].start()
+    ]
+    for fill in fills:
+        fill.start()
     tile = depth // chain
     block_shape = part.shape[1:5]
     for i, s in enumerate(scatter.order):
-        left = mixed[:, pl.ds(pl.multiple_of(scatter.blocks[s] * tile, tile), tile)]
+        columns = pl.ds(pl.multiple_of(scatter.blocks[s] * tile, tile), tile)
+        left = mixed[:, columns]
 
         @pl.loop(0, out_width // 512)
         def _(n):
@@ -613,8 +657,18 @@
                 dot_tn(left, grad_one_b[:, at]).astype(BF16).reshape(block_shape + (512,))
             )
 
-        sides[s].wait()
+        side = dot_tn(second[:, columns], grad_side[...])
+        side = side + dot_tn(cotangent[:, columns], combined[...])
+        part[s, :, :, :, :, out_width:] = side.astype(BF16).reshape(
+            block_shape + (part.shape[-1] - out_width,)
+        )
         scatter.cross(i)
+        if i >= 1:
+            scatter.halve(i - 1)
+        if i >= 3:
+            scatter.sideways(i - 3)
+        if i >= 5:
+            scatter.finish(i - 5)
     load_out.wait()
 
     @pl.loop(0, chain)
@@ -667,31 +721,21 @@
             head_gain_grad[:, 0:HD] += gain_grad
 
     last = chain - 1
-    for i in range(chain - 2):
-        scatter.halve(i)
-        if i >= 2:
-            scatter.sideways(i - 2)
-        if i >= 4:
-            scatter.finish(i - 4)
-    if chain > 5:
-        scatter.finish(last - 5)
-    heads(0, 1)
-    scatter.sideways(last - 3)
-    scatter.halve(last - 1)
-    heads(1, 2)
+    scatter.sideways(last - 2)
     if chain > 4:
         scatter.finish(last - 4)
-    scatter.sideways(last - 2)
     scatter.halve(last)
-    heads(2, 3)
+    for fill in fills:
+        fill.wait()
+    heads(0, 1)
+    scatter.sideways(last - 1)
     scatter.finish(last - 3)
-    scatter.sideways(last - 1)
-    heads(3, 5)
+    heads(1, 3)
+    scatter.sideways(last)
     scatter.finish(last - 2)
-    scatter.sideways(last)
-    heads(5, 7)
+    heads(3, 6)
     scatter.finish(last - 1)
-    heads(7, 8)
+    heads(6, 8)
     halo = []
     for d in (1, 2):
         for j, grad in enumerate((grad_keys, grad_values)):
@@ -717,7 +761,6 @@
             weight[k, :, :, :, :, 0:query_width].reshape(tile, query_width),
         )
 
-    scatter.finish(last)
     for copy in halo:
         copy.wait_recv()
     for g in range(KVH):
@@ -759,6 +802,7 @@
         input_grad[at] = (grad_one[at] + back).astype(BF16)
         attn_gain_grad[...] += jnp.sum(grad * field * rms, axis=0, keepdims=True)
 
+    scatter.finish(last)
     scatter.total()
     for copy in halo:
         copy.wait_send()
@@ -767,11 +811,14 @@
 def attention_backward(
     full_a,
     full_b,
-    side_part,
     grad_one_b,
     grad_one,
     tokens,
     mixed,
+    second,
+    grad_side,
+    cotangent,
+    combined,
     query,
     key_rows,
     value_rows,
@@ -789,9 +836,10 @@
     anywhere, vmem = pl.BlockSpec(memory_space=pl.ANY), pl.BlockSpec(memory_space=pltpu.VMEM)
     blocked = [
         array.reshape(chain, 2, 2, 2, weight_rows, array.shape[1])
-        for array in (full_a, full_b, side_part)
+        for array in (full_a, full_b)
     ]
     kv_width = KVH * HD
+    filled = (grad_one, tokens, query, key_rows, value_rows, projected)
     return pl.pallas_call(
         functools.partial(attention_backward_kernel, count),
         out_shape=[
@@ -801,7 +849,7 @@
             jax.ShapeDtypeStruct((1, depth), F32),
             jax.ShapeDtypeStruct((1, 2 * HD), F32),
         ],
-        in_specs=[anywhere] * 3 + [vmem] * 12,
+        in_specs=[anywhere] * 8 + [vmem] * 10,
         out_specs=[vmem] * 5,
         scratch_shapes=[
             pltpu.VMEM((chain, 2, 2, 2, weight_rows, QKV_WIDTH), BF16),
@@ -811,8 +859,12 @@
             pltpu.VMEM((3, rows, kv_width), F32),
             pltpu.VMEM((4, rows, kv_width), BF16),
             pltpu.VMEM((4, rows, kv_width), BF16),
+            *(
+                pltpu.VMEM(array.shape, array.dtype)
+                for array in filled
+            ),
             dma,
-            dma((chain,)),
+            dma((len(filled),)),
             dma((4,)),
             dma((4,)),
         ]
@@ -826,14 +878,18 @@
         name="attention_backward",
     )(
         *blocked,
-        grad_one_b,
         grad_one,
         tokens,
-        mixed,
         query,
         key_rows,
         value_rows,
         projected,
+        grad_one_b,
+        mixed,
+        second,
+        grad_side,
+        cotangent,
+        combined,
         gains,
         cosine,
         sine,
@@ -931,20 +987,21 @@
         }
         self.part, self.in_half, self.in_x, self.in_y, self.in_z = part, in_half, in_x, in_y, in_z
         self.waves = []
-        for w, base in enumerate((4, 0)):
-            self.waves.append(
-                {
-                    "a": remote(
-                        part.at[base + 3, top], in_half.at[w, 0], ss.at[w, 0], sr.at[w, 0], next_x
-                    ),
-                    "b": remote(
-                        part.at[base + 3, low], in_half.at[w, 1], ss.at[w, 1], sr.at[w, 1], next_y
-                    ),
-                    "x": remote(part.at[base + 1], in_x.at[w], ss.at[w, 2], sr.at[w, 2], next_x),
-                    "y": remote(part.at[base + 2], in_y.at[w], ss.at[w, 3], sr.at[w, 3], next_y),
-                }
-            )
-        self.waves[0]["z"] = remote(part.at[4], in_z, ss.at[0, 4], sr.at[0, 4], next_z)
+        side = own.shape[1] // 2
+        for w, (base, first) in enumerate(((4, 0), (4, side), (0, 0), (0, side))):
+            at = pl.ds(first, side)
+            corner = part.at[base + 3, :, at]
+            to_x, to_y = part.at[base + 1, :, at], part.at[base + 2, :, at]
+            here = part.at[base, :, at]
+            wave = {
+                "a": remote(corner.at[top], in_half.at[w, 0], ss.at[w, 0], sr.at[w, 0], next_x),
+                "b": remote(corner.at[low], in_half.at[w, 1], ss.at[w, 1], sr.at[w, 1], next_y),
+                "x": remote(to_x, in_x.at[w], ss.at[w, 2], sr.at[w, 2], next_x),
+                "y": remote(to_y, in_y.at[w], ss.at[w, 3], sr.at[w, 3], next_y),
+            }
+            if base:
+                wave["z"] = remote(here, in_z.at[w], ss.at[w, 4], sr.at[w, 4], next_z)
+            self.waves.append((wave, at, to_x, to_y, here))
 
     def start(self, *names):
         for name in names:
@@ -955,42 +1012,46 @@
             self.gather[name].wait_recv()
 
     def corners(self, w):
-        self.waves[w]["a"].start()
-        self.waves[w]["b"].start()
+        wave = self.waves[w][0]
+        wave["a"].start()
+        wave["b"].start()
 
     def sideways(self, w):
-        base, wave = 4 - 4 * w, self.waves[w]
+        wave, _, to_x, to_y, _ = self.waves[w]
         wave["a"].wait_recv()
-        add_into(self.part.at[base + 2, self.top], self.in_half.at[w, 0])
+        add_into(to_y.at[self.top], self.in_half.at[w, 0])
         wave["y"].start()
         wave["b"].wait_recv()
-        add_into(self.part.at[base + 1, self.low], self.in_half.at[w, 1])
+        add_into(to_x.at[self.low], self.in_half.at[w, 1])
         wave["x"].start()
 
-    def across(self):
-        self.waves[0]["x"].wait_recv()
-        self.waves[0]["y"].wait_recv()
-        add_into(self.part.at[4], self.in_x.at[0], self.in_y.at[0])
-        self.waves[0]["z"].start()
+    def across(self, w):
+        wave, _, _, _, here = self.waves[w]
+        wave["x"].wait_recv()
+        wave["y"].wait_recv()
+        add_into(here, self.in_x.at[w], self.in_y.at[w])
+        wave["z"].start()
 
     def finish(self, out):
-        self.waves[1]["x"].wait_recv()
-        self.waves[1]["y"].wait_recv()
-        self.waves[0]["z"].wait_recv()
-
-        @pl.loop(0, out.shape[0] // 16)
-        def _(i):
-            at = pl.ds(pl.multiple_of(i * 16, 16), 16)
-            out[at] = (
-                self.part[0, at].astype(F32)
-                + self.in_x[1, at].astype(F32)
-                + self.in_y[1, at].astype(F32)
-                + self.in_z[at].astype(F32)
-            )
+        for w in (2, 3):
+            wave, side = self.waves[w][:2]
+            wave["x"].wait_recv()
+            wave["y"].wait_recv()
+            self.waves[w - 2][0]["z"].wait_recv()
+
+            @pl.loop(0, out.shape[0] // 16)
+            def _(i):
+                at = pl.ds(pl.multiple_of(i * 16, 16), 16)
+                out[at, side] = (
+                    self.part[0, at, side].astype(F32)
+                    + self.in_x[w, at].astype(F32)
+                    + self.in_y[w, at].astype(F32)
+                    + self.in_z[w - 2, at].astype(F32)
+                )
 
         for copy in self.gather.values():
             copy.wait_send()
-        for wave in self.waves:
+        for wave, *_ in self.waves:
             for copy in wave.values():
                 copy.wait_send()
 
@@ -1004,33 +1065,32 @@
     return [
         pltpu.VMEM((8, rows, width), BF16),
         pltpu.VMEM((8, rows, width), BF16),
-        pltpu.VMEM((2, 2, rows // 2, width), BF16),
-        pltpu.VMEM((2, rows, width), BF16),
-        pltpu.VMEM((2, rows, width), BF16),
-        pltpu.VMEM((rows, width), BF16),
+        pltpu.VMEM((4, 2, rows // 2, width // 2), BF16),
+        pltpu.VMEM((4, rows, width // 2), BF16),
+        pltpu.VMEM((4, rows, width // 2), BF16),
+        pltpu.VMEM((2, rows, width // 2), BF16),
         dma((12,)),
         dma((12,)),
-        dma((2, 5)),
-        dma((2, 5)),
+        dma((4, 5)),
+        dma((4, 5)),
         dma,
     ]
 
 
-def load_weights(blocks, held, sems):
+def load_weights(own, blocks, held, sems):
     rows = blocks.shape[2]
     loads = []
-    for m in (2, 0, 1):
-        loads.append(
-            [
+    for m in range(2):
+        for i in range(blocks.shape[0]):
+            loads.append(
                 pltpu.make_async_copy(
-                    blocks.at[i, m], held.at[m, pl.ds(i * rows, rows)], sems.at[m, i]
+                    own.at[m] if i == 0 else blocks.at[i, m],
+                    held.at[m, pl.ds(i * rows, rows)],
+                    sems.at[m, i],
                 )
-                for i in range(blocks.shape[0])
-            ]
-        )
-        for load in loads[-1]:
-            load.start()
-    return loads[1:] + loads[:1]
+            )
+            loads[-1].start()
+    return loads
 
 
 GELU_A = 0.7978845608028654
@@ -1053,21 +1113,36 @@
 WIDTH_TILE = 1024
 
 
-def ffn_forward_kernel(own, blocks, *refs):
-    out, held_out, gate_out, up_out, weights, gate_st, up_st, act = refs[:8]
-    load_sem, save_sem, keep_sem = refs[8:11]
-    held, part, in_half, in_x, in_y, in_z, gs, gr, ss, sr, own_sem = refs[11:]
+def ffn_forward_kernel(count, own, own_down, own_ffn, blocks, *refs):
+    out, held_out, gate_out, up_out, down_out, weights, gate_st, up_st, act = refs[:9]
+    load_sem, save_sem, keep_sem, down_local, down_s, down_r = refs[9:15]
+    held, part, in_half, in_x, in_y, in_z, gs, gr, ss, sr, own_sem = refs[15:]
+    me = lax.axis_index("fsdp")
+    bits = weight_bits(count)
     cube = TokenCube(own, held, part, in_half, in_x, in_y, in_z, gs, gr, ss, sr)
-    greet(cube.partners)
+    greet(cube.partners + [flipped(me, bit) for bit in bits])
     cube.start("zt", "zl", "x", "y")
     keep = pltpu.make_async_copy(own, held.at[0], own_sem)
     keep.start()
-    loads = load_weights(blocks, weights, load_sem)
+    block = own_down.shape[0]
+    down_keep = pltpu.make_async_copy(own_down, weights.at[2, pl.ds(0, block)], down_local)
+    down_keep.start()
+    downs = []
+    for i, bit in enumerate(bits):
+        size = block << i
+        src = own_down if i == 0 else weights.at[2, pl.ds(0, size)]
+        downs.append(
+            remote(
+                src, weights.at[2, pl.ds(size, size)], down_s.at[i], down_r.at[i], flipped(me, bit)
+            )
+        )
+    downs[0].start()
+    loads = load_weights(own_ffn, blocks, weights, load_sem)
     hidden, width = weights.shape[1], weights.shape[2]
     saves = []
 
-    def compute(step):
-        j, slot = ORDER[step], step % 2
+    def enter(step):
+        j, slot, third = ORDER[step], step % 2, step % 3
         if step >= 2:
             for save in saves[step - 2]:
                 save.wait()
@@ -1079,7 +1154,7 @@
             up = dot_nt(held[j], weights[1, at])
             gate_st[slot, :, at] = gate
             up_st[slot, :, at] = up
-            act[:, at] = (0.5 * gate * (1.0 + tanh_inner(gate)) * up).astype(BF16)
+            act[third, :, at] = (0.5 * gate * (1.0 + tanh_inner(gate)) * up).astype(BF16)
 
         saves.append(
             [
@@ -1089,20 +1164,177 @@
         )
         for save in saves[step]:
             save.start()
-        if step == 0:
-            for load in loads[2]:
-                load.wait()
+
+    def leave(step):
+        j, third = ORDER[step], step % 3
 
         @pl.loop(0, width // WIDTH_TILE)
         def _(n):
             at = pl.ds(pl.multiple_of(n * WIDTH_TILE, WIDTH_TILE), WIDTH_TILE)
             part[j, :, at] = jnp.dot(
-                act[...], weights[2, :, at], preferred_element_type=F32
+                act[third], weights[2, :, at], preferred_element_type=F32
             ).astype(BF16)
 
     keep.wait()
-    for load in loads[0] + loads[1]:
+    for load in loads:
         load.wait()
+    enter(0)
+    cube.arrive("x", "y", "zt")
+    cube.start("xt", "yt")
+    enter(1)
+    down_keep.wait()
+    for i in range(1, len(downs)):
+        downs[i - 1].wait_recv()
+        downs[i].start()
+    enter(2)
+    cube.arrive("zl")
+    cube.start("xl", "yl")
+    cube.arrive("xt")
+    cube.start("et")
+    downs[-1].wait_recv()
+    leave(0)
+    leave(1)
+    leave(2)
+    save_down = pltpu.make_async_copy(weights.at[2], down_out, down_local)
+    save_down.start()
+    enter(3)
+    cube.arrive("xl", "yt", "yl")
+    cube.start("el", "dt", "dl")
+    leave(3)
+    for step in (4, 5):
+        enter(step)
+        leave(step)
+    cube.arrive("et", "el")
+    enter(6)
+    leave(6)
+    cube.corners(0)
+    cube.corners(1)
+    cube.arrive("dt", "dl")
+    whole = pltpu.make_async_copy(held, held_out, keep_sem)
+    whole.start()
+    enter(7)
+    leave(7)
+    cube.sideways(0)
+    cube.sideways(1)
+    cube.corners(2)
+    cube.corners(3)
+    cube.across(0)
+    cube.across(1)
+    cube.sideways(2)
+    cube.sideways(3)
+    cube.finish(out)
+    for save in saves[6] + saves[7] + [save_down, whole]:
+        save.wait()
+    for copy in downs:
+        copy.wait_send()
+
+
+def ffn_forward(own, own_down, own_ffn, blocks):
+    count = lax.axis_size("fsdp")
+    rows, width = own.shape
+    hidden = blocks.shape[0] * blocks.shape[2]
+    n_bits = len(weight_bits(count))
+    dma = pltpu.SemaphoreType.DMA
+    anywhere = pl.BlockSpec(memory_space=pl.ANY)
+    return pl.pallas_call(
+        functools.partial(ffn_forward_kernel, count),
+        out_shape=[
+            jax.ShapeDtypeStruct((rows, width), F32),
+            jax.ShapeDtypeStruct((8, rows, width), BF16),
+            jax.ShapeDtypeStruct((8, rows, hidden), F32),
+            jax.ShapeDtypeStruct((8, rows, hidden), F32),
+            jax.ShapeDtypeStruct((hidden, width), BF16),
+        ],
+        in_specs=[anywhere] * 4,
+        out_specs=[pl.BlockSpec(memory_space=pltpu.VMEM)] + [anywhere] * 4,
+        scratch_shapes=[
+            pltpu.VMEM((3, hidden, width), BF16),
+            pltpu.VMEM((2, rows, hidden), F32),
+            pltpu.VMEM((2, rows, hidden), F32),
+            pltpu.VMEM((3, rows, hidden), BF16),
+            dma((2, blocks.shape[0])),
+            dma((2, 2)),
+            dma,
+            dma,
+            dma((n_bits,)),
+            dma((n_bits,)),
+        ]
+        + cube_scratch(rows, width),
+        compiler_params=pltpu.CompilerParams(
+            collective_id=2, has_side_effects=True, vmem_limit_bytes=58 * 2**20
+        ),
+        cost_estimate=pl.CostEstimate(
+            flops=48 * rows * width * hidden, bytes_accessed=300 * 2**20, transcendentals=0
+        ),
+        name="ffn_forward",
+    )(own, own_down, own_ffn, blocks)
+
+
+def ffn_backward_kernel(own, normed, gate_in, up_in, down, own_ffn, blocks, *refs):
+    out, mine, further, landed, weights, gate_st, up_st, grads, stage, fetched = refs[:10]
+    load_sem, down_sem, read_sem, write_sem, normed_sem, pair_s, pair_r, fetch_sem = refs[10:18]
+    held, part, in_half, in_x, in_y, in_z, gs, gr, ss, sr, own_sem = refs[18:]
+    sibling = flipped(lax.axis_index("fsdp"), 1)
+    cube = TokenCube(own, held, part, in_half, in_x, in_y, in_z, gs, gr, ss, sr)
+    greet(cube.partners + [sibling])
+    cube.start("zt", "zl", "x", "y")
+    keep = pltpu.make_async_copy(own, held.at[0], own_sem)
+    keep.start()
+    hidden, width = weights.shape[1], weights.shape[2]
+    rows = own.shape[0]
+    reads = []
+    for step, j in enumerate(ORDER):
+        slot = step % 2
+        reads.append(
+            [
+                pltpu.make_async_copy(gate_in.at[j], gate_st.at[slot], read_sem.at[0, slot]),
+                pltpu.make_async_copy(up_in.at[j], up_st.at[slot], read_sem.at[1, slot]),
+            ]
+        )
+    for read in reads[0]:
+        read.start()
+    load_down = pltpu.make_async_copy(down, weights.at[2], down_sem)
+    load_down.start()
+    loads = load_weights(own_ffn, blocks, weights, load_sem)
+
+    def compute(step):
+        j, slot = ORDER[step], step % 2
+        if step < 7:
+            for read in reads[step + 1]:
+                read.start()
+        for read in reads[step]:
+            read.wait()
+
+        @pl.loop(0, hidden // HIDDEN_TILE)
+        def _(n):
+            at = pl.ds(pl.multiple_of(n * HIDDEN_TILE, HIDDEN_TILE), HIDDEN_TILE)
+            grad_act = dot_nt(held[j], weights[2, at]).astype(BF16).astype(F32)
+            gate, up = gate_st[slot, :, at], up_st[slot, :, at]
+            inner = tanh_inner(gate)
+            gelu = 0.5 * gate * (1.0 + inner)
+            slope = 0.5 * (1.0 + inner) + 0.5 * gate * (1.0 - inner * inner) * GELU_A * (
+                1.0 + 3.0 * GELU_B * gate * gate
+            )
+            token = pl.ds(j * rows, rows)
+            grads[2, token, at] = (gelu * up).astype(BF16)
+            grads[0, token, at] = (grad_act * up * slope).astype(BF16)
+            grads[1, token, at] = (grad_act * gelu).astype(BF16)
+
+        if step == 0:
+            for load in loads:
+                load.wait()
+        token = pl.ds(j * rows, rows)
+
+        @pl.loop(0, width // WIDTH_TILE)
+        def _(n):
+            at = pl.ds(pl.multiple_of(n * WIDTH_TILE, WIDTH_TILE), WIDTH_TILE)
+            part[j, :, at] = (
+                jnp.dot(grads[0, token], weights[0, :, at], preferred_element_type=F32)
+                + jnp.dot(grads[1, token], weights[1, :, at], preferred_element_type=F32)
+            ).astype(BF16)
+
+    keep.wait()
+    load_down.wait()
     compute(0)
     cube.arrive("x", "y", "zt")
     cube.start("xt", "yt")
@@ -1120,210 +1352,124 @@
     cube.arrive("et", "el")
     compute(6)
     cube.corners(0)
+    cube.corners(1)
     cube.arrive("dt", "dl")
-    whole = pltpu.make_async_copy(held, held_out, keep_sem)
-    whole.start()
     compute(7)
+    tokens = 8 * rows
+    refill = pltpu.make_async_copy(
+        normed, weights.at[pl.ds(0, tokens // hidden)], normed_sem
+    )
+    refill.start()
+    tile = stage.shape[1]
+    half, quarter = hidden // 2, hidden // 4
+    tiles = [(m, i * tile) for m in (2, 0, 1) for i in range(half // tile)]
+    pairs, busy = [], [None, None]
+    for n, (m, first) in enumerate(tiles):
+        pairs.append(
+            remote(
+                stage.at[n % 2],
+                landed.at[m, pl.ds(first, tile)],
+                pair_s.at[n],
+                pair_r.at[n],
+                sibling,
+            )
+        )
+    fetches = [
+        pltpu.make_async_copy(
+            landed.at[m, pl.ds(first, tile)], fetched.at[n % 2], fetch_sem.at[n % 2]
+        )
+        for n, (m, first) in enumerate(tiles)
+    ]
+    done = [0]
+
+    def weight_grad(times):
+        for _ in range(times):
+            job = done[0]
+            done[0] = job + 1
+            n, for_sibling = job % len(tiles), job < len(tiles)
+            m, first = tiles[n]
+            slot = job % 2
+            if job == len(tiles) // 3:
+                refill.wait()
+            if busy[slot] is not None:
+                busy[slot]()
+            if not for_sibling:
+                pairs[n].wait_recv()
+                fetches[n].start()
+                fetches[n].wait()
+            place = first + half if for_sibling else first
+
+            @pl.loop(0, width // WIDTH_TILE)
+            def _(k):
+                at = pl.ds(pl.multiple_of(k * WIDTH_TILE, WIDTH_TILE), WIDTH_TILE)
+                if m == 2:
+                    right = held[:, :, at].reshape(tokens, WIDTH_TILE)
+                else:
+                    right = weights[: tokens // hidden, :, at].reshape(tokens, WIDTH_TILE)
+                grad = dot_tn(grads[m, :, pl.ds(place, tile)], right)
+                if not for_sibling:
+                    grad = grad + fetched[n % 2, :, at].astype(F32)
+                stage[slot, :, at] = grad.astype(BF16)
+
+            if for_sibling:
+                pairs[n].start()
+                busy[slot] = pairs[n].wait_send
+            else:
+                target = mine if first < quarter else further
+                write = pltpu.make_async_copy(
+                    stage.at[slot],
+                    target.at[m, pl.ds(first % quarter, tile)],
+                    write_sem.at[slot],
+                )
+                write.start()
+                busy[slot] = write.wait
+
     cube.sideways(0)
-    cube.corners(1)
     cube.sideways(1)
-    cube.across()
+    cube.corners(2)
+    cube.corners(3)
+    weight_grad(3)
+    cube.across(0)
+    weight_grad(1)
+    cube.sideways(2)
+    cube.across(1)
+    weight_grad(1)
+    cube.sideways(3)
+    weight_grad(2 * len(tiles) - 5)
     cube.finish(out)
-    for save in saves[6] + saves[7]:
-        save.wait()
-    whole.wait()
-
-
-def ffn_forward(own, blocks):
+    for end in busy:
+        end()
+
+
+def ffn_backward(own, normed, gate, up, down, own_ffn, blocks):
     rows, width = own.shape
     hidden = blocks.shape[0] * blocks.shape[2]
     dma = pltpu.SemaphoreType.DMA
     anywhere = pl.BlockSpec(memory_space=pl.ANY)
+    tile = 256
+    n_tiles = 3 * (hidden // 2) // tile
+    grad = jax.ShapeDtypeStruct((3, hidden // 4, width), BF16)
+    landed = jax.ShapeDtypeStruct((3, hidden // 2, width), BF16)
     return pl.pallas_call(
-        ffn_forward_kernel,
-        out_shape=[
-            jax.ShapeDtypeStruct((rows, width), F32),
-            jax.ShapeDtypeStruct((8, rows, width), BF16),
-            jax.ShapeDtypeStruct((8, rows, hidden), F32),
-            jax.ShapeDtypeStruct((8, rows, hidden), F32),
-        ],
-        in_specs=[anywhere] * 2,
+        ffn_backward_kernel,
+        out_shape=[jax.ShapeDtypeStruct((rows, width), F32), grad, grad, landed],
+        in_specs=[anywhere] * 7,
         out_specs=[pl.BlockSpec(memory_space=pltpu.VMEM)] + [anywhere] * 3,
         scratch_shapes=[
             pltpu.VMEM((3, hidden, width), BF16),
             pltpu.VMEM((2, rows, hidden), F32),
             pltpu.VMEM((2, rows, hidden), F32),
-            pltpu.VMEM((rows, hidden), BF16),
-            dma((3, blocks.shape[0])),
-            dma((2, 2)),
+            pltpu.VMEM((3, 8 * rows, hidden), BF16),
+            pltpu.VMEM((2, tile, width), BF16),
+            pltpu.VMEM((2, tile, width), BF16),
+            dma((2, blocks.shape[0])),
             dma,
-        ]
-        + cube_scratch(rows, width),
-        compiler_params=pltpu.CompilerParams(
-            collective_id=2, has_side_effects=True, vmem_limit_bytes=58 * 2**20
-        ),
-        cost_estimate=pl.CostEstimate(
-            flops=48 * rows * width * hidden, bytes_accessed=300 * 2**20, transcendentals=0
-        ),
-        name="ffn_forward",
-    )(own, blocks)
-
-
-def ffn_backward_kernel(own, normed, gate_in, up_in, blocks, *refs):
-    out, mine, theirs, weights, gate_st, up_st, grads, stage = refs[:8]
-    load_sem, read_sem, write_sem, normed_sem = refs[8:12]
-    held, part, in_half, in_x, in_y, in_z, gs, gr, ss, sr, own_sem = refs[12:]
-    cube = TokenCube(own, held, part, in_half, in_x, in_y, in_z, gs, gr, ss, sr)
-    greet(cube.partners)
-    cube.start("zt", "zl", "x", "y")
-    keep = pltpu.make_async_copy(own, held.at[0], own_sem)
-    keep.start()
-    hidden, width = weights.shape[1], weights.shape[2]
-    rows = own.shape[0]
-    reads = []
-    for step, j in enumerate(ORDER):
-        slot = step % 2
-        reads.append(
-            [
-                pltpu.make_async_copy(gate_in.at[j], gate_st.at[slot], read_sem.at[0, slot]),
-                pltpu.make_async_copy(up_in.at[j], up_st.at[slot], read_sem.at[1, slot]),
-            ]
-        )
-    for read in reads[0]:
-        read.start()
-    loads = load_weights(blocks, weights, load_sem)
-
-    def compute(step):
-        j, slot = ORDER[step], step % 2
-        if step < 7:
-            for read in reads[step + 1]:
-                read.start()
-        for read in reads[step]:
-            read.wait()
-
-        @pl.loop(0, hidden // HIDDEN_TILE)
-        def _(n):
-            at = pl.ds(pl.multiple_of(n * HIDDEN_TILE, HIDDEN_TILE), HIDDEN_TILE)
-            grad_act = dot_nt(held[j], weights[2, at]).astype(BF16).astype(F32)
-            gate, up = gate_st[slot, :, at], up_st[slot, :, at]
-            inner = tanh_inner(gate)
-            gelu = 0.5 * gate * (1.0 + inner)
-            slope = 0.5 * (1.0 + inner) + 0.5 * gate * (1.0 - inner * inner) * GELU_A * (
-                1.0 + 3.0 * GELU_B * gate * gate
-            )
-            token = pl.ds(j * rows, rows)
-            grads[2, token, at] = (gelu * up).astype(BF16)
-            grads[0, token, at] = (grad_act * up * slope).astype(BF16)
-            grads[1, token, at] = (grad_act * gelu).astype(BF16)
-
-        if step == 0:
-            for load in loads[0] + loads[1]:
-                load.wait()
-        token = pl.ds(j * rows, rows)
-
-        @pl.loop(0, width // WIDTH_TILE)
-        def _(n):
-            at = pl.ds(pl.multiple_of(n * WIDTH_TILE, WIDTH_TILE), WIDTH_TILE)
-            part[j, :, at] = (
-                jnp.dot(grads[0, token], weights[0, :, at], preferred_element_type=F32)
-                + jnp.dot(grads[1, token], weights[1, :, at], preferred_element_type=F32)
-            ).astype(BF16)
-
-    keep.wait()
-    for load in loads[2]:
-        load.wait()
-    compute(0)
-    cube.arrive("x", "y", "zt")
-    cube.start("xt", "yt")
-    compute(1)
-    compute(2)
-    cube.arrive("zl")
-    cube.start("xl", "yl")
-    cube.arrive("xt")
-    cube.start("et")
-    compute(3)
-    cube.arrive("xl", "yt", "yl")
-    cube.start("el", "dt", "dl")
-    compute(4)
-    compute(5)
-    cube.arrive("et", "el")
-    compute(6)
-    cube.corners(0)
-    cube.arrive("dt", "dl")
-    compute(7)
-    cube.corners(1)
-    tokens = 8 * rows
-    refill = pltpu.make_async_copy(
-        normed, weights.at[pl.ds(0, tokens // hidden)], normed_sem
-    )
-    refill.start()
-    tile = stage.shape[1]
-    half = hidden // 2
-    jobs = [(m, i) for m in (2, 0, 1) for i in range(hidden // tile)]
-    writes = []
-
-    def weight_grad(count):
-        for _ in range(count):
-            index = len(writes)
-            m, i = jobs[index]
-            slot = index % 2
-            if index >= 2:
-                writes[index - 2].wait()
-            if m == 0 and i == 0:
-                refill.wait()
-            first = (i * tile + half) % hidden
-
-            @pl.loop(0, width // WIDTH_TILE)
-            def _(n):
-                at = pl.ds(pl.multiple_of(n * WIDTH_TILE, WIDTH_TILE), WIDTH_TILE)
-                if m == 2:
-                    right = held[:, :, at].reshape(tokens, WIDTH_TILE)
-                else:
-                    right = weights[: tokens // hidden, :, at].reshape(tokens, WIDTH_TILE)
-                stage[slot, :, at] = dot_tn(
-                    grads[m, :, pl.ds(first, tile)], right
-                ).astype(BF16)
-
-            target = theirs if first >= half else mine
-            write = pltpu.make_async_copy(
-                stage.at[slot], target.at[m, pl.ds(first % half, tile)], write_sem.at[slot]
-            )
-            write.start()
-            writes.append(write)
-
-    weight_grad(1)
-    cube.sideways(0)
-    weight_grad(1)
-    cube.sideways(1)
-    weight_grad(4)
-    cube.across()
-    weight_grad(len(jobs) - 6)
-    cube.finish(out)
-    writes[-2].wait()
-    writes[-1].wait()
-
-
-def ffn_backward(own, normed, gate, up, blocks):
-    rows, width = own.shape
-    hidden = blocks.shape[0] * blocks.shape[2]
-    dma = pltpu.SemaphoreType.DMA
-    anywhere = pl.BlockSpec(memory_space=pl.ANY)
-    grad = jax.ShapeDtypeStruct((3, hidden // 2, width), BF16)
-    return pl.pallas_call(
-        ffn_backward_kernel,
-        out_shape=[jax.ShapeDtypeStruct((rows, width), F32), grad, grad],
-        in_specs=[anywhere] * 5,
-        out_specs=[pl.BlockSpec(memory_space=pltpu.VMEM), anywhere, anywhere],
-        scratch_shapes=[
-            pltpu.VMEM((3, hidden, width), BF16),
-            pltpu.VMEM((2, rows, hidden), F32),
-            pltpu.VMEM((2, rows, hidden), F32),
-            pltpu.VMEM((3, 8 * rows, hidden), BF16),
-            pltpu.VMEM((2, 256, width), BF16),
-            dma((3, blocks.shape[0])),
             dma((2, 2)),
             dma((2,)),
             dma,
+            dma((n_tiles,)),
+            dma((n_tiles,)),
+            dma((2,)),
         ]
         + cube_scratch(rows, width),
         compiler_params=pltpu.CompilerParams(
@@ -1333,13 +1479,15 @@
             flops=96 * rows * width * hidden, bytes_accessed=400 * 2**20, transcendentals=0
         ),
         name="ffn_backward",
-    )(own, normed.reshape(8 * rows // hidden, hidden, width), gate, up, blocks)
-
-
-def passed_along(block, axis, distance):
-    devices = range(lax.axis_size(axis))
-    route = [(i - distance, i) for i in devices if i - distance in devices]
-    return lax.ppermute(block, axis, route)
+    )(
+        own,
+        normed.reshape(8 * rows // hidden, hidden, width),
+        gate,
+        up,
+        down,
+        own_ffn,
+        blocks,
+    )
 
 
 def inv_rms(field):
@@ -1367,20 +1515,6 @@
     phase = position.astype(jnp.float32)[:, None] * freq[None, :]
     phase = jnp.concatenate([phase, phase], axis=-1)
     return (jnp.cos(phase)[:, None, :], jnp.sin(phase)[:, None, :])
-
-
-def rotate(field, cosine, sine):
-    half_width = field.shape[-1] // 2
-    turned = jnp.concatenate([-field[..., half_width:], field[..., :half_width]], axis=-1)
-    return field * cosine + turned * sine
-
-
-def rotate_back(grad_in, cosine, sine):
-    half_width = grad_in.shape[-1] // 2
-    shifted = grad_in * sine
-    return grad_in * cosine + jnp.concatenate(
-        [shifted[..., half_width:], -shifted[..., :half_width]], axis=-1
-    )
 
 
 def norm_back(grad_out, field, scale_inv, gain):
@@ -1421,20 +1555,11 @@
     cosine, sine = angles(position)
     reach = (WINDOW + tok_rows - 2) // tok_rows
     assert reach == 2
-    key_index = jnp.concatenate(
-        [token_index - distance * tok_rows for distance in range(reach, 0, -1)] + [token_index]
-    )
-    key_segment, unused_pos = layout(seq_lengths, seq_order, key_index)
-    key_gap = token_index[:, None] - key_index[None, :]
-    allowed = (segment[:, None] == key_segment[None, :]) & (key_gap >= 0) & (key_gap < WINDOW)
-    score_scale = HD ** (-0.5)
     split_at = PL + RANK
-    group_size = HQ // KVH
-    query_width = HQ * HD
-    kv_width = KVH * HD
     count = lax.axis_size("fsdp")
     bits = weight_bits(count)
     weight_rows = qkv_weight.shape[0]
+    ffn_own = ffn_weights[:, :2].transpose(1, 0, 2)
     (
         qkv_gathered,
         out_gathered,
@@ -1451,17 +1576,18 @@
     ) = attention_forward(
         jnp.concatenate([qkv_weight, placed_gains(norm_gains, weight_rows)], axis=1),
         jnp.concatenate([out_weight, side_weights], axis=1),
-        ffn_weights.transpose(1, 0, 2),
+        ffn_own,
         tokens,
         cosine[:, 0, : HD // 2],
         sine[:, 0, : HD // 2],
         position[:, None],
     )
-    qkv_all = qkv_gathered[:, : qkv_weight.shape[1]]
-    out_all, side_all = out_gathered[:, :D], out_gathered[:, D:]
+    side_all = out_gathered[:, D:]
     ffn_gain = gain_all[0, D : 2 * D]
     rms_two = inv_rms(first_sum)
-    ffn_out, normed_all, gate_kept, up_kept = ffn_forward(normed_two, ffn_blocks)
+    ffn_out, normed_all, gate_kept, up_kept, down_all = ffn_forward(
+        normed_two, ffn_weights[:, 2], ffn_own, ffn_blocks
+    )
     second_sum = first_sum + ffn_out
     second_b = second_sum.astype(jnp.bfloat16)
     side_in = jnp.dot(second_b, side_all[:, :split_at], preferred_element_type=jnp.float32)
@@ -1471,21 +1597,18 @@
         [(gelu_per * per_f).astype(jnp.bfloat16), side_in[:, PL:].astype(jnp.bfloat16)], axis=1
     )
     output = (second_sum + contract_cols(combined, side_all[:, split_at:])).astype(jnp.bfloat16)
-    back_qkv, back_out, back_side = qkv_all, out_all, side_all
+    back_side = side_all
     grad_y = cotangent.astype(jnp.float32)
     grad_comb = jnp.dot(cotangent, back_side[:, split_at:], preferred_element_type=jnp.float32)
-    side_out_grad = contract_rows(cotangent, combined)
     per_layer_grad = (grad_comb[:, :PL] * gelu_per).astype(jnp.bfloat16)
     grad_per = pull_per(grad_comb[:, :PL] * per_f)[0]
     grad_side = jnp.concatenate([grad_per, grad_comb[:, PL:]], axis=1).astype(jnp.bfloat16)
-    side_in_grad = contract_rows(second_b, grad_side)
-    side_grad_full = jnp.concatenate([side_in_grad, side_out_grad], axis=1).astype(BF16)
     grad_two = grad_y + contract_cols(grad_side, back_side[:, :split_at])
     grad_two_b = grad_two.astype(jnp.bfloat16)
-    grad_h2, ffn_part, ffn_sent = ffn_backward(
-        grad_two_b, normed_all, gate_kept, up_kept, ffn_blocks
-    )
-    for bit in reversed(bits):
+    grad_h2, ffn_part, ffn_sent, _ = ffn_backward(
+        grad_two_b, normed_all, gate_kept, up_kept, down_all, ffn_own, ffn_blocks
+    )
+    for bit in reversed(bits[:-1]):
         ffn_part = ffn_part.astype(F32) + swapped(ffn_sent, bit).astype(F32)
         if bit != bits[0]:
             half = ffn_part.shape[1] // 2
@@ -1498,11 +1621,14 @@
     out_sum, grad_projected, input_grad, attn_gain_grad, head_gain_grad = attention_backward(
         qkv_gathered,
         out_gathered,
-        side_grad_full,
         grad_one_b,
         grad_one,
         tokens,
         mixed_b,
+        second_b,
+        jnp.pad(grad_side, ((0, 0), (0, split_at))),
+        cotangent,
+        jnp.pad(combined, ((0, 0), (split_at, 0))),
         query_b,
         key_blocks,
         value_blocks,

time: 778 us -> 707 us (0.909)
  Pallas kernels: 691 us -> 645 us
  other arithmetic: 36.6 us -> 22.3 us
    pallas_call x1, Pallas kernels: 190 us -> 157 us  [ffn_forward(): pl.pallas_call(functools.partial(ffn_forward_kernel, count), out_shape=[j...]
    pallas_call x1, Pallas kernels: 92.7 us -> 73.9 us  [qkv_scatter(): pl.pallas_call(functools.partial(qkv_scatter_kernel, count), out_shape=ja...]
    add x1 -> x0, other arithmetic: 12.2 us -> none  [local(): ffn_part = ffn_part.astype(F32) + swapped(ffn_sent, bit).astype(F32)]
    pallas_call x1, Pallas kernels: 85.3 us -> 96.4 us  [attention_backward(): pl.pallas_call(functools.partial(attention_backward_kernel, count), out_s...]
  transfers between devices with their start and end apart: 2 -> 1, of which waited for: 0 -> 0; matrix products, arithmetic and copies ran while one was open for 3% -> 3% of each run, Pallas kernels for 23% -> 24%
where the time goes in v5:
time: 707 us; the launch traced here: 695 us
  Pallas kernels  645 us (91%)
  other arithmetic  22.3 us (3%)
  local copies, waits for them, and re-layouts  14.9 us (2%)
  matrix products  12 us (2%)
    pallas_call x1, Pallas kernels, ffn_backward(): pl.pallas_call(ffn_backward_kernel, out_shape=[jax.ShapeDtypeStruct((rows...  161 us
    pallas_call x1, Pallas kernels, ffn_forward(): pl.pallas_call(functools.partial(ffn_forward_kernel, count), out_shape=[j...  157 us
    pallas_call x1, Pallas kernels, attention_forward(): pl.pallas_call(functools.partial(attention_forward_kernel, count), out_sh...  156 us
    pallas_call x1, Pallas kernels, attention_backward(): pl.pallas_call(functools.partial(attention_backward_kernel, count), out_s...  96.4 us
    pallas_call x1, Pallas kernels, qkv_scatter(): pl.pallas_call(functools.partial(qkv_scatter_kernel, count), out_shape=ja...  73.9 us
  transfers between devices with their start and end apart: 1, of which 0 were waited for; matrix products, arithmetic and copies ran while one was open for 3% of the time, Pallas kernels for 24%

profile of v5, /device:TPU:0, one launch (start us, length us, event | category | flops | bytes accessed | tf_op | source)
XLA Modules:
  0.0 695.4 jit_solution(8873596043246341498)
XLA Ops:
  0.7 3.2 slice_bitcast_fusion.own_ffn
  3.8 0.0 copy-start.11
  3.8 0.0 copy-start.13
  3.8 2.4 slice_bitcast_fusion.1.own_down
  6.2 0.0 copy-done.14
  6.2 0.0 copy-done.15
  6.2 0.2 select_reduce_fusion.2
  6.4 0.1 select_reduce_fusion.1
  6.5 0.1 select_reduce_fusion
  6.6 0.1 multiply_bitcast_fusion
  6.7 1.2 fusion.22
  7.9 0.1 copy.29
  8.1 0.7 add_subtract_fusion.position
  8.7 0.0 copy-done.16
  8.7 0.2 dynamic_update_slice.3
  9.0 0.0 copy-done.10
  9.0 0.8 pad_maximum_fusion.own_a
  9.7 0.0 copy-done.11
  9.7 0.0 copy-done.13
  9.7 0.8 pad_maximum_fusion.1.own_b
  10.5 156.2 %attention_forward.1 = (bf16[4,2,2,2,64,3200]{5,4,3,2,1,0:T(8,128)(2,1)}, bf16[4,2,2,2,64,2688]{5,4,3,2,1,0:T(8,128)(2,1)}, bf16[4,2,256,2048]{3,2,1,0:T(8,128)(...) custom-call(bf16[64,3200]{1,0:T(8,128)(2,1)} %pad_maximum_fusion.own, ...), custom_call_target="tpu_custom_call" | custom-call | tf_op jit(solution)/shard_map/attention_forward/pallas_call | solution.py:406
  166.7 0.0 copy-start.2
  166.8 156.7 %ffn_forward.1 = (f32[256,2048]{1,0:T(8,128)}, bf16[8,256,2048]{2,1,0:T(8,128)(2,1)}, f32[8,256,1024]{2,1,0:T(8,128)}, f32[8,256,1024]{2,1,0:T(8,128)}, bf16[1024,2048]{1,0:T(8,128)(2,1)}) custom-call(bf16[256,2048]{1,0:T(8,128)(2,1)} %get-tuple-element.34.own, bf16[256,2048]{1,0:T(8,128)(2,1)} %slice_bitcast_fusion.1.own_down, ...), custom_call_target="tpu_custom_call" | custom-call | flops 25769803776 | bytes 314572800 | tf_op jit(solution)/shard_map/ffn_forward/pallas_call | solution.py:1239
  323.5 0.0 copy-done.2
  323.5 3.2 fusion.24
  326.7 2.5 fusion.5
  329.3 0.0 copy-done.8
  329.3 0.0 copy-start.12
  329.3 2.3 fusion.7
  331.5 0.0 copy-done.9
  331.6 0.1 copy.34
  331.7 0.0 copy-done.12
  331.7 0.9 multiply_convert_fusion
  332.6 3.8 fusion.25
  336.5 161.5 %ffn_backward.1 = (f32[256,2048]{1,0:T(8,128)}, bf16[3,256,2048]{2,1,0:T(8,128)(2,1)}, bf16[3,256,2048]{2,1,0:T(8,128)(2,1)}, bf16[3,512,2048]{2,1,0:T(8,128)(2,1)}) custom-call(bf16[256,2048]{1,0:T(8,128)(2,1)} %get-tuple-element.72.own, bf16[2,1024,2048]{2,1,0:T(8,128)(2,1)} %bitcast.36, f32[8,256,1024]{2,1,0:T(8,128)} %get-tuple-element.40.gate_in, ...), custom_call_target="tpu_custom_call" | custom-call | flops 51539607552 | bytes 419430400 | tf_op jit(solution)/shard_map/ffn_backward/pallas_call | solution.py:1453
  497.9 0.1 collective-permute-start
  498.0 0.1 copy.35
  498.2 0.7 slice.68
  498.9 2.9 multiply_reduce_fusion
  501.9 0.8 pad.12.grad_side
  502.6 0.8 pad.13.combined
  503.5 0.0 copy-done.3
  503.5 0.0 copy-done.5
  503.5 3.9 fusion.23
  507.4 96.4 %attention_backward.1 = (f32[64,2688]{1,0:T(8,128)}, bf16[256,3072]{1,0:T(8,128)(2,1)}, bf16[256,2048]{1,0:T(8,128)(2,1)}, f32[1,2048]{1,0:T(1,128)}, f32[1,512]{1,0:T(1,128)}) custom-call(bf16[4,2,2,2,64,3200]{5,4,3,2,1,0:T(8,128)(2,1)} %get-tuple-element.38.full_a, bf16[4,2,2,2,64,2688]{5,4,3,2,1,0:T(8,128)(2,1)} %get-tuple-element.37.full_b, ...), custom_call_target="tpu_custom_call" | custom-call | flops 40000000000 | bytes 188743680 | tf_op jit(solution)/shard_map/attention_backward/pallas_call | solution.py:843
  603.8 0.0 copy-start
  603.8 0.0 copy-start.1
  603.8 2.0 slice.70
  605.9 1.6 slice.71
  607.4 0.7 convert_reduce_fusion.1
  608.1 0.7 convert_reduce_fusion
  608.9 0.1 convert_element_type.59
  609.0 0.1 copy.36
  609.1 0.0 copy-done
  609.1 0.0 copy-done.1
  609.2 0.0 copy-start.4
  609.2 73.9 %qkv_scatter.1 = f32[64,3200]{1,0:T(8,128)S(1)} custom-call(bf16[4,2,2,2,64,128]{5,4,3,2,1,0:T(8,128)(2,1)S(1)} %bitcast.27, bf16[256,2048]{1,0:T(8,128)(2,1)S(1)} %copy-done, bf16[256,3072]{1,0:T(8,128)(2,1)S(1)} %copy-done.1), custom_call_target="tpu_custom_call" | custom-call | flops 40000000000 | bytes 188743680 | tf_op jit(solution)/shard_map/qkv_scatter/pallas_call | solution.py:945
  683.1 0.9 slice.69
  684.0 0.6 slice.82
  684.6 0.0 copy-done.4
  684.6 3.4 fusion
  688.0 0.0 collective-permute-done
  688.0 6.0 add_bitcast_fusion
  694.0 1.0 copy.39
  (25 shorter events, 0.2 us)
Async XLA Ops:
  3.8 2.4 copy-start.14
  3.8 2.4 copy-start.15
  3.8 4.9 copy-start.16
  3.8 5.1 copy-start.10
  3.8 5.9 copy-start.11
  3.8 5.9 copy-start.13
  166.7 156.7 %copy-start.2 = (f32[256,2048]{1,0:T(8,128)S(1)}, f32[256,2048]{1,0:T(8,128)}, u32[]{:S(2)}) copy-start(f32[256,2048]{1,0:T(8,128)} %get-tuple-element.33) | copy-start | bytes 6291460
  326.7 4.8 copy-start.9
  326.7 2.6 copy-start.8
  329.3 2.5 copy-start.12
  497.9 190.0 %collective-permute-start = (bf16[3,256,2048]{2,1,0:T(8,128)(2,1)}, bf16[3,256,2048]{2,1,0:T(8,128)(2,1)}, u32[]{:S(2)}, u32[]{:S(2)}) collective-permute-start(bf16[3,256,2048]{2,1,0:T(8,128)(2,1)} %get-tuple-element.57), channel_id=1, source_target_pairs={{0,8},{1,9},{2,10},{3,11},{4,12},{5,13},{6,14},{7,15},{8,0},{9,1},... | collective-permute-start | bytes 9437192 | tf_op jit(solution)/shard_map/ppermute | solution.py:37
  498.9 4.6 copy-start.3
  498.9 4.6 copy-start.5
  603.8 5.3 copy-start
  603.8 5.3 copy-start.1
  609.2 75.4 %copy-start.4 = (f32[256,2048]{1,0:T(8,128)S(1)}, f32[256,2048]{1,0:T(8,128)}, u32[]{:S(2)}) copy-start(f32[256,2048]{1,0:T(8,128)} %get-tuple-element.63) | copy-start | bytes 6291460
  684.6 3.4 copy-start.6
  688.0 6.0 copy-start.7

commit v6 on v5

--- a/solution.py
+++ b/solution.py
@@ -194,24 +194,29 @@
     full_a,
     full_b,
     full_ffn,
+    normed_out,
+    projected_out,
+    query_out,
+    key_out,
+    value_out,
     gains,
+    mixed,
+    first_sum,
+    normed_two,
+    wa,
+    wb,
     normed,
     projected,
     query,
     key_rows,
     value_rows,
-    mixed,
-    first_sum,
-    normed_two,
-    wa,
-    wb,
     *sems,
 ):
     me = lax.axis_index("fsdp")
     chain = count // PLANE
     bits = weight_bits(count)
     gather = WeightGather(chain, ((own_a, wa, sems[:13]), (own_b, wb, sems[13:26])))
-    first_s, first_r, ffn_s, ffn_r, rest_s, rest_r, halo_s, halo_r, save = sems[26:]
+    first_s, first_r, ffn_s, ffn_r, rest_s, rest_r, halo_s, halo_r, save, early = sems[26:]
     ahead = [lax.rem(me + d, count) for d in (1, 2)]
     behind = [lax.rem(me + count - d, count) for d in (1, 2)]
     greet(gather.partners + [flipped(me, bit) for bit in bits[:-1]] + ahead + behind)
@@ -335,6 +340,20 @@
     gather.across(1, chain - 3)
     for copy in halo:
         copy.wait_recv()
+    early_saves = [
+        pltpu.make_async_copy(src, dst, early.at[i])
+        for i, (src, dst) in enumerate(
+            (
+                (normed, normed_out),
+                (projected, projected_out),
+                (query, query_out),
+                (key_rows, key_out),
+                (value_rows, value_out),
+            )
+        )
+    ]
+    for copy in early_saves:
+        copy.start()
     n_keys = 3 * rows
     gap = (
         lax.broadcasted_iota(jnp.int32, (rows, n_keys), 0)
@@ -387,8 +406,8 @@
     for copy in ffn_first + ffn_copies + ffn_rest + halo:
         copy.wait_send()
     gather.drain()
-    keep_a.wait()
-    keep_b.wait()
+    for copy in early_saves + [keep_a, keep_b]:
+        copy.wait()
 
 
 FFN_PIECES = 2
@@ -403,29 +422,33 @@
     dma = pltpu.SemaphoreType.DMA
     anywhere, vmem = pl.BlockSpec(memory_space=pl.ANY), pl.BlockSpec(memory_space=pltpu.VMEM)
     shape_a, shape_b = ((chain, 2, 2, 2) + own.shape for own in (own_a, own_b))
+    kept = [
+        jax.ShapeDtypeStruct((rows, depth), BF16),
+        jax.ShapeDtypeStruct((rows, QKV_WIDTH), F32),
+        jax.ShapeDtypeStruct((rows, HQ * HD), BF16),
+        jax.ShapeDtypeStruct((3, rows, KVH * HD), BF16),
+        jax.ShapeDtypeStruct((3, rows, KVH * HD), BF16),
+    ]
     full_a, full_b, *rest = pl.pallas_call(
         functools.partial(attention_forward_kernel, count),
         out_shape=[
             jax.ShapeDtypeStruct(shape_a, BF16),
             jax.ShapeDtypeStruct(shape_b, BF16),
             jax.ShapeDtypeStruct((n_blocks,) + own_ffn.shape, BF16),
+            *kept,
             jax.ShapeDtypeStruct((1, 2 * depth + 2 * HD), F32),
-            jax.ShapeDtypeStruct((rows, depth), BF16),
-            jax.ShapeDtypeStruct((rows, QKV_WIDTH), F32),
-            jax.ShapeDtypeStruct((rows, HQ * HD), BF16),
-            jax.ShapeDtypeStruct((3, rows, KVH * HD), BF16),
-            jax.ShapeDtypeStruct((3, rows, KVH * HD), BF16),
             jax.ShapeDtypeStruct((rows, HQ * HD), BF16),
             jax.ShapeDtypeStruct((rows, depth), F32),
             jax.ShapeDtypeStruct((rows, depth), BF16),
         ],
         in_specs=[anywhere] * 3 + [vmem] * 4,
-        out_specs=[anywhere] * 3 + [vmem] * 9,
+        out_specs=[anywhere] * 8 + [vmem] * 4,
         scratch_shapes=[pltpu.VMEM(shape_a, BF16), pltpu.VMEM(shape_b, BF16)]
+        + [pltpu.VMEM(array.shape, array.dtype) for array in kept]
         + ([dma] + [dma((chain,))] * 12) * 2
         + [dma((2 * FFN_PIECES,))] * 2
         + [dma((len(weight_bits(count)) - 1,))] * 4
-        + [dma((4,)), dma((4,)), dma((2,))],
+        + [dma((4,)), dma((4,)), dma((2,)), dma((len(kept),))],
         compiler_params=pltpu.CompilerParams(
             collective_id=0, has_side_effects=True, vmem_limit_bytes=58 * 2**20
         ),
@@ -720,6 +743,26 @@
             grad_projected[:, at] = back.astype(BF16)
             head_gain_grad[:, 0:HD] += gain_grad
 
+    halo = []
+
+    def send_back(g):
+        at = slice(g * HD, (g + 1) * HD)
+        lanes = pl.ds(g * HD, HD)
+        for d in (2, 1):
+            for j, grad in enumerate((grad_keys, grad_values)):
+                slot = 2 * (d - 1) + j
+                halo_out[slot, :, at] = grad[2 - d, :, at].astype(BF16)
+                halo.append(
+                    remote(
+                        halo_out.at[slot, :, lanes],
+                        halo_in.at[slot, :, lanes],
+                        halo_s.at[g, slot],
+                        halo_r.at[g, slot],
+                        behind[d - 1],
+                    )
+                )
+                halo[-1].start()
+
     last = chain - 1
     scatter.sideways(last - 2)
     if chain > 4:
@@ -733,24 +776,12 @@
     heads(1, 3)
     scatter.sideways(last)
     scatter.finish(last - 2)
-    heads(3, 6)
+    heads(3, 4)
+    send_back(0)
+    heads(4, 6)
     scatter.finish(last - 1)
     heads(6, 8)
-    halo = []
-    for d in (1, 2):
-        for j, grad in enumerate((grad_keys, grad_values)):
-            at = 2 * (d - 1) + j
-            halo_out[at] = grad[2 - d].astype(BF16)
-            halo.append(
-                remote(
-                    halo_out.at[at],
-                    halo_in.at[at],
-                    halo_s.at[at],
-                    halo_r.at[at],
-                    behind[d - 1],
-                )
-            )
-            halo[-1].start()
+    send_back(1)
     load_qkv.wait()
 
     @pl.loop(0, chain)
@@ -865,8 +896,8 @@
             ),
             dma,
             dma((len(filled),)),
-            dma((4,)),
-            dma((4,)),
+            dma((KVH, 4)),
+            dma((KVH, 4)),
         ]
         + scatter_scratch(chain, weight_rows, out_width),
         compiler_params=pltpu.CompilerParams(
@@ -1564,12 +1595,12 @@
         qkv_gathered,
         out_gathered,
         ffn_blocks,
-        gain_all,
         normed_b,
         projected,
         query_b,
         key_blocks,
         value_blocks,
+        gain_all,
         mixed_b,
         first_sum,
         normed_two,

time: 707 us -> 702 us (level)
  no operation moved by 1% of the time
where the time goes in v6:
time: 702 us; the launch traced here: 689 us
  Pallas kernels  638 us (91%)
  other arithmetic  22.3 us (3%)
  local copies, waits for them, and re-layouts  14.9 us (2%)
  matrix products  12 us (2%)
    pallas_call x1, Pallas kernels, ffn_backward(): pl.pallas_call(ffn_backward_kernel, out_shape=[jax.ShapeDtypeStruct((rows...  161 us
    pallas_call x1, Pallas kernels, ffn_forward(): pl.pallas_call(functools.partial(ffn_forward_kernel, count), out_shape=[j...  157 us
    pallas_call x1, Pallas kernels, attention_forward(): pl.pallas_call(functools.partial(attention_forward_kernel, count), out_sh...  154 us
    pallas_call x1, Pallas kernels, attention_backward(): pl.pallas_call(functools.partial(attention_backward_kernel, count), out_s...  96.6 us
    pallas_call x1, Pallas kernels, qkv_scatter(): pl.pallas_call(functools.partial(qkv_scatter_kernel, count), out_shape=ja...  69.3 us
  transfers between devices with their start and end apart: 1, of which 0 were waited for; matrix products, arithmetic and copies ran while one was open for 3% of the time, Pallas kernels for 24%

profile of v6, /device:TPU:0, one launch (start us, length us, event | category | flops | bytes accessed | tf_op | source)
XLA Modules:
  0.0 688.9 jit_solution(16197409125264516691)
XLA Ops:
  0.7 3.2 slice_bitcast_fusion.own_ffn
  3.8 0.0 copy-start.11
  3.8 0.0 copy-start.13
  3.8 2.4 slice_bitcast_fusion.1.own_down
  6.2 0.0 copy-done.14
  6.2 0.0 copy-done.15
  6.2 0.2 select_reduce_fusion.2
  6.4 0.1 select_reduce_fusion.1
  6.5 0.1 select_reduce_fusion
  6.6 0.1 multiply_bitcast_fusion
  6.7 1.2 fusion.22
  7.9 0.1 copy.29
  8.1 0.7 add_subtract_fusion.position
  8.7 0.0 copy-done.16
  8.7 0.2 dynamic_update_slice.3
  9.0 0.0 copy-done.10
  9.0 0.8 pad_maximum_fusion.own_a
  9.7 0.0 copy-done.11
  9.7 0.0 copy-done.13
  9.7 0.8 pad_maximum_fusion.1.own_b
  10.5 154.2 %attention_forward.1 = (bf16[4,2,2,2,64,3200]{5,4,3,2,1,0:T(8,128)(2,1)}, bf16[4,2,2,2,64,2688]{5,4,3,2,1,0:T(8,128)(2,1)}, bf16[4,2,256,2048]{3,2,1,0:T(8,128)(...) custom-call(bf16[64,3200]{1,0:T(8,128)(2,1)} %pad_maximum_fusion.own, ...), custom_call_target="tpu_custom_call" | custom-call | tf_op jit(solution)/shard_map/attention_forward/pallas_call | solution.py:432
  164.7 0.0 copy-start.2
  164.7 156.7 %ffn_forward.1 = (f32[256,2048]{1,0:T(8,128)}, bf16[8,256,2048]{2,1,0:T(8,128)(2,1)}, f32[8,256,1024]{2,1,0:T(8,128)}, f32[8,256,1024]{2,1,0:T(8,128)}, bf16[1024,2048]{1,0:T(8,128)(2,1)}) custom-call(bf16[256,2048]{1,0:T(8,128)(2,1)} %get-tuple-element.34.own, bf16[256,2048]{1,0:T(8,128)(2,1)} %slice_bitcast_fusion.1.own_down, ...), custom_call_target="tpu_custom_call" | custom-call | flops 25769803776 | bytes 314572800 | tf_op jit(solution)/shard_map/ffn_forward/pallas_call | solution.py:1270
  321.4 0.0 copy-done.2
  321.5 3.2 fusion.24
  324.7 2.5 fusion.5
  327.2 0.0 copy-done.8
  327.2 0.0 copy-start.12
  327.3 2.3 fusion.7
  329.5 0.0 copy-done.9
  329.6 0.1 copy.34
  329.7 0.0 copy-done.12
  329.7 0.9 multiply_convert_fusion
  330.6 3.8 fusion.25
  334.4 161.4 %ffn_backward.1 = (f32[256,2048]{1,0:T(8,128)}, bf16[3,256,2048]{2,1,0:T(8,128)(2,1)}, bf16[3,256,2048]{2,1,0:T(8,128)(2,1)}, bf16[3,512,2048]{2,1,0:T(8,128)(2,1)}) custom-call(bf16[256,2048]{1,0:T(8,128)(2,1)} %get-tuple-element.72.own, bf16[2,1024,2048]{2,1,0:T(8,128)(2,1)} %bitcast.36, f32[8,256,1024]{2,1,0:T(8,128)} %get-tuple-element.40.gate_in, ...), custom_call_target="tpu_custom_call" | custom-call | flops 51539607552 | bytes 419430400 | tf_op jit(solution)/shard_map/ffn_backward/pallas_call | solution.py:1484
  495.9 0.1 collective-permute-start
  496.0 0.1 copy.35
  496.1 0.7 slice.68
  496.8 2.9 multiply_reduce_fusion
  499.8 0.8 pad.12.grad_side
  500.6 0.8 pad.13.combined
  501.4 0.0 copy-done.3
  501.4 0.0 copy-done.5
  501.4 3.9 fusion.23
  505.3 96.6 %attention_backward.1 = (f32[64,2688]{1,0:T(8,128)}, bf16[256,3072]{1,0:T(8,128)(2,1)}, bf16[256,2048]{1,0:T(8,128)(2,1)}, f32[1,2048]{1,0:T(1,128)}, f32[1,512]{1,0:T(1,128)}) custom-call(bf16[4,2,2,2,64,3200]{5,4,3,2,1,0:T(8,128)(2,1)} %get-tuple-element.38.full_a, bf16[4,2,2,2,64,2688]{5,4,3,2,1,0:T(8,128)(2,1)} %get-tuple-element.37.full_b, ...), custom_call_target="tpu_custom_call" | custom-call | flops 40000000000 | bytes 188743680 | tf_op jit(solution)/shard_map/attention_backward/pallas_call | solution.py:874
  601.9 0.0 copy-start
  601.9 0.0 copy-start.1
  601.9 2.0 slice.70
  603.9 1.6 slice.71
  605.5 0.7 convert_reduce_fusion.1
  606.2 0.7 convert_reduce_fusion
  606.9 0.1 convert_element_type.59
  607.1 0.1 copy.36
  607.2 0.0 copy-done
  607.2 0.0 copy-done.1
  607.2 0.0 copy-start.4
  607.2 69.3 %qkv_scatter.1 = f32[64,3200]{1,0:T(8,128)S(1)} custom-call(bf16[4,2,2,2,64,128]{5,4,3,2,1,0:T(8,128)(2,1)S(1)} %bitcast.27, bf16[256,2048]{1,0:T(8,128)(2,1)S(1)} %copy-done, bf16[256,3072]{1,0:T(8,128)(2,1)S(1)} %copy-done.1), custom_call_target="tpu_custom_call" | custom-call | flops 40000000000 | bytes 188743680 | tf_op jit(solution)/shard_map/qkv_scatter/pallas_call | solution.py:976
  676.5 0.9 slice.69
  677.5 0.6 slice.82
  678.0 3.4 fusion
  681.4 0.0 collective-permute-done
  681.4 0.0 copy-done.6
  681.4 6.0 add_bitcast_fusion
  687.4 1.0 copy.39
  (25 shorter events, 0.2 us)
Async XLA Ops:
  3.8 2.4 copy-start.14
  3.8 2.4 copy-start.15
  3.8 4.9 copy-start.16
  3.8 5.1 copy-start.10
  3.8 5.9 copy-start.11
  3.8 5.9 copy-start.13
  164.7 156.7 %copy-start.2 = (f32[256,2048]{1,0:T(8,128)S(1)}, f32[256,2048]{1,0:T(8,128)}, u32[]{:S(2)}) copy-start(f32[256,2048]{1,0:T(8,128)} %get-tuple-element.33) | copy-start | bytes 6291460
  324.7 4.8 copy-start.9
  324.7 2.6 copy-start.8
  327.2 2.5 copy-start.12
  495.9 185.5 %collective-permute-start = (bf16[3,256,2048]{2,1,0:T(8,128)(2,1)}, bf16[3,256,2048]{2,1,0:T(8,128)(2,1)}, u32[]{:S(2)}, u32[]{:S(2)}) collective-permute-start(bf16[3,256,2048]{2,1,0:T(8,128)(2,1)} %get-tuple-element.57), channel_id=1, source_target_pairs={{0,8},{1,9},{2,10},{3,11},{4,12},{5,13},{6,14},{7,15},{8,0},{9,1},... | collective-permute-start | bytes 9437192 | tf_op jit(solution)/shard_map/ppermute | solution.py:37
  496.8 4.6 copy-start.3
  496.8 4.6 copy-start.5
  601.9 5.3 copy-start
  601.9 5.3 copy-start.1
  607.2 70.8 %copy-start.4 = (f32[256,2048]{1,0:T(8,128)S(1)}, f32[256,2048]{1,0:T(8,128)}, u32[]{:S(2)}) copy-start(f32[256,2048]{1,0:T(8,128)} %get-tuple-element.63) | copy-start | bytes 6291460
  678.0 3.4 copy-start.6
  681.4 6.0 copy-start.7

commit v7 on v6

--- a/solution.py
+++ b/solution.py
@@ -773,15 +773,13 @@
     heads(0, 1)
     scatter.sideways(last - 1)
     scatter.finish(last - 3)
-    heads(1, 3)
+    heads(1, 4)
+    send_back(0)
     scatter.sideways(last)
     scatter.finish(last - 2)
-    heads(3, 4)
-    send_back(0)
-    heads(4, 6)
+    heads(4, 8)
+    send_back(1)
     scatter.finish(last - 1)
-    heads(6, 8)
-    send_back(1)
     load_qkv.wait()
 
     @pl.loop(0, chain)

time: 702 us -> 700 us (level)
  no operation moved by 1% of the time
where the time goes in v7:
time: 700 us; the launch traced here: 687 us
  Pallas kernels  637 us (91%)
  other arithmetic  22.3 us (3%)
  local copies, waits for them, and re-layouts  14.9 us (2%)
  matrix products  12 us (2%)
    pallas_call x1, Pallas kernels, ffn_backward(): pl.pallas_call(ffn_backward_kernel, out_shape=[jax.ShapeDtypeStruct((rows...  161 us
    pallas_call x1, Pallas kernels, ffn_forward(): pl.pallas_call(functools.partial(ffn_forward_kernel, count), out_shape=[j...  157 us
    pallas_call x1, Pallas kernels, attention_forward(): pl.pallas_call(functools.partial(attention_forward_kernel, count), out_sh...  154 us
    pallas_call x1, Pallas kernels, attention_backward(): pl.pallas_call(functools.partial(attention_backward_kernel, count), out_s...  99.2 us
    pallas_call x1, Pallas kernels, qkv_scatter(): pl.pallas_call(functools.partial(qkv_scatter_kernel, count), out_shape=ja...  65.1 us
  transfers between devices with their start and end apart: 1, of which 0 were waited for; matrix products, arithmetic and copies ran while one was open for 3% of the time, Pallas kernels for 24%

profile of v7, /device:TPU:0, one launch (start us, length us, event | category | flops | bytes accessed | tf_op | source)
XLA Modules:
  0.0 687.4 jit_solution(10810389715059056533)
XLA Ops:
  0.7 3.2 slice_bitcast_fusion.own_ffn
  3.8 0.0 copy-start.11
  3.8 0.0 copy-start.13
  3.8 2.4 slice_bitcast_fusion.1.own_down
  6.2 0.0 copy-done.14
  6.2 0.0 copy-done.15
  6.2 0.2 select_reduce_fusion.2
  6.4 0.1 select_reduce_fusion.1
  6.5 0.1 select_reduce_fusion
  6.6 0.1 multiply_bitcast_fusion
  6.7 1.2 fusion.22
  7.9 0.1 copy.29
  8.1 0.7 add_subtract_fusion.position
  8.7 0.0 copy-done.16
  8.7 0.2 dynamic_update_slice.3
  9.0 0.0 copy-done.10
  9.0 0.8 pad_maximum_fusion.own_a
  9.7 0.0 copy-done.11
  9.7 0.0 copy-done.13
  9.7 0.8 pad_maximum_fusion.1.own_b
  10.5 154.2 %attention_forward.1 = (bf16[4,2,2,2,64,3200]{5,4,3,2,1,0:T(8,128)(2,1)}, bf16[4,2,2,2,64,2688]{5,4,3,2,1,0:T(8,128)(2,1)}, bf16[4,2,256,2048]{3,2,1,0:T(8,128)(...) custom-call(bf16[64,3200]{1,0:T(8,128)(2,1)} %pad_maximum_fusion.own, ...), custom_call_target="tpu_custom_call" | custom-call | tf_op jit(solution)/shard_map/attention_forward/pallas_call | solution.py:432
  164.7 0.0 copy-start.2
  164.7 156.7 %ffn_forward.1 = (f32[256,2048]{1,0:T(8,128)}, bf16[8,256,2048]{2,1,0:T(8,128)(2,1)}, f32[8,256,1024]{2,1,0:T(8,128)}, f32[8,256,1024]{2,1,0:T(8,128)}, bf16[1024,2048]{1,0:T(8,128)(2,1)}) custom-call(bf16[256,2048]{1,0:T(8,128)(2,1)} %get-tuple-element.34.own, bf16[256,2048]{1,0:T(8,128)(2,1)} %slice_bitcast_fusion.1.own_down, ...), custom_call_target="tpu_custom_call" | custom-call | flops 25769803776 | bytes 314572800 | tf_op jit(solution)/shard_map/ffn_forward/pallas_call | solution.py:1268
  321.4 0.0 copy-done.2
  321.5 3.2 fusion.24
  324.7 2.5 fusion.5
  327.2 0.0 copy-done.8
  327.2 0.0 copy-start.12
  327.3 2.3 fusion.7
  329.5 0.0 copy-done.9
  329.6 0.1 copy.34
  329.7 0.0 copy-done.12
  329.7 0.9 multiply_convert_fusion
  330.6 3.8 fusion.25
  334.4 161.4 %ffn_backward.1 = (f32[256,2048]{1,0:T(8,128)}, bf16[3,256,2048]{2,1,0:T(8,128)(2,1)}, bf16[3,256,2048]{2,1,0:T(8,128)(2,1)}, bf16[3,512,2048]{2,1,0:T(8,128)(2,1)}) custom-call(bf16[256,2048]{1,0:T(8,128)(2,1)} %get-tuple-element.72.own, bf16[2,1024,2048]{2,1,0:T(8,128)(2,1)} %bitcast.36, f32[8,256,1024]{2,1,0:T(8,128)} %get-tuple-element.40.gate_in, ...), custom_call_target="tpu_custom_call" | custom-call | flops 51539607552 | bytes 419430400 | tf_op jit(solution)/shard_map/ffn_backward/pallas_call | solution.py:1482
  495.9 0.1 collective-permute-start
  496.0 0.1 copy.35
  496.1 0.7 slice.68
  496.8 2.9 multiply_reduce_fusion
  499.8 0.8 pad.12.grad_side
  500.6 0.8 pad.13.combined
  501.4 0.0 copy-done.3
  501.4 0.0 copy-done.5
  501.4 3.9 fusion.23
  505.3 99.2 %attention_backward.1 = (f32[64,2688]{1,0:T(8,128)}, bf16[256,3072]{1,0:T(8,128)(2,1)}, bf16[256,2048]{1,0:T(8,128)(2,1)}, f32[1,2048]{1,0:T(1,128)}, f32[1,512]{1,0:T(1,128)}) custom-call(bf16[4,2,2,2,64,3200]{5,4,3,2,1,0:T(8,128)(2,1)} %get-tuple-element.38.full_a, bf16[4,2,2,2,64,2688]{5,4,3,2,1,0:T(8,128)(2,1)} %get-tuple-element.37.full_b, ...), custom_call_target="tpu_custom_call" | custom-call | flops 40000000000 | bytes 188743680 | tf_op jit(solution)/shard_map/attention_backward/pallas_call | solution.py:872
  604.5 0.0 copy-start
  604.6 0.0 copy-start.1
  604.6 2.0 slice.70
  606.6 1.6 slice.71
  608.2 0.7 convert_reduce_fusion.1
  608.9 0.7 convert_reduce_fusion
  609.6 0.1 convert_element_type.59
  609.8 0.1 copy.36
  609.9 0.0 copy-done
  609.9 0.0 copy-done.1
  609.9 0.0 copy-start.4
  609.9 65.1 %qkv_scatter.1 = f32[64,3200]{1,0:T(8,128)S(1)} custom-call(bf16[4,2,2,2,64,128]{5,4,3,2,1,0:T(8,128)(2,1)S(1)} %bitcast.27, bf16[256,2048]{1,0:T(8,128)(2,1)S(1)} %copy-done, bf16[256,3072]{1,0:T(8,128)(2,1)S(1)} %copy-done.1), custom_call_target="tpu_custom_call" | custom-call | flops 40000000000 | bytes 188743680 | tf_op jit(solution)/shard_map/qkv_scatter/pallas_call | solution.py:974
  675.0 0.9 slice.69
  676.0 0.6 slice.82
  676.5 3.4 fusion
  679.9 0.0 collective-permute-done
  679.9 6.0 add_bitcast_fusion
  686.0 0.0 copy-done.7
  686.0 1.0 copy.39
  (25 shorter events, 0.2 us)
Async XLA Ops:
  3.8 2.4 copy-start.14
  3.8 2.4 copy-start.15
  3.8 4.9 copy-start.16
  3.8 5.1 copy-start.10
  3.8 5.9 copy-start.11
  3.8 5.9 copy-start.13
  164.7 156.7 %copy-start.2 = (f32[256,2048]{1,0:T(8,128)S(1)}, f32[256,2048]{1,0:T(8,128)}, u32[]{:S(2)}) copy-start(f32[256,2048]{1,0:T(8,128)} %get-tuple-element.33) | copy-start | bytes 6291460
  324.7 4.8 copy-start.9
  324.7 2.6 copy-start.8
  327.2 2.5 copy-start.12
  495.9 184.0 %collective-permute-start = (bf16[3,256,2048]{2,1,0:T(8,128)(2,1)}, bf16[3,256,2048]{2,1,0:T(8,128)(2,1)}, u32[]{:S(2)}, u32[]{:S(2)}) collective-permute-start(bf16[3,256,2048]{2,1,0:T(8,128)(2,1)} %get-tuple-element.57), channel_id=1, source_target_pairs={{0,8},{1,9},{2,10},{3,11},{4,12},{5,13},{6,14},{7,15},{8,0},{9,1},... | collective-permute-start | bytes 9437192 | tf_op jit(solution)/shard_map/ppermute | solution.py:37
  496.8 4.6 copy-start.3
  496.8 4.6 copy-start.5
  604.5 5.3 copy-start
  604.6 5.3 copy-start.1
  609.9 66.7 %copy-start.4 = (f32[256,2048]{1,0:T(8,128)S(1)}, f32[256,2048]{1,0:T(8,128)}, u32[]{:S(2)}) copy-start(f32[256,2048]{1,0:T(8,128)} %get-tuple-element.63) | copy-start | bytes 6291460
  676.5 3.4 copy-start.6
  679.9 6.0 copy-start.7
